TPU v7x, 128 devices: a whole 4x4x4 slice. The times are simulated.
128 devices in a mesh: gz: 32 (over z, x_lo, y), gx: 4 (over x_hi, core).
Axes of the slice: x: 4 (x_hi: 2, x_lo: 2; x = x_hi * 2 + x_lo), y: 4, z: 4, core: 2. Of those that a mesh axis runs over, the one named last changes fastest.
Arguments:
- right_side: float32 [2, 3, 2, 128, 128, 128], P(None, None, None, 'gz', 'gx'), may hold values from -10 to 10
- conductance: float32 [128, 128, 128], P('gz', 'gx'), may hold values from 0.05 to 5
- owned_cells: int32 [128, 4, 32], P(('gz', 'gx')), may hold values from 0 to 4095, as said below
- spectra: float32 [512, 4], replicated, may hold values from -8 to 8
- scenario_tile: int32 [512], replicated, may hold values from 0 to 3
Outputs:
- solution_field: float32 [2, 3, 2, 128, 128, 128], P(None, None, None, 'gz', 'gx')
- hazard: float32 [16384, 512], P(('gz', 'gx'))
Inputs may be any that keep to these rules, and one draw needn't show every extreme that they name: For each tile j, owned_cells[:, j, :] holds each of the 4096 cell numbers of tile j exactly once.
All inputs are finite; a program needn't handle non-finite values.
Results may differ from a plain program's by a relative error of at most 0.0015.
Values sent between devices are 32-bit elements; how exact they have to be, the bound alone decides.
No kernel may reach another device: no remote copies, remote signals or barrier semaphores. Data moves between devices by JAX's collectives and lax.ppermute only.
A program may use at most 64 MiB of HBM per device.

v0:
```python
import jax
import jax.numpy as jnp
from jax import lax
from jax.sharding import PartitionSpec as P

ITERS = 3


def padded_2(value, sides, width):
    for axis, dim in sides:
        devices, length = (lax.axis_size(axis), value.shape[dim])
        up = [(i, (i + 1) % devices) for i in range(devices - 1)]
        down = [(j, i) for i, j in up]
        last = lax.slice_in_dim(value, length - width, length, axis=dim)
        leading = lax.slice_in_dim(value, 0, width, axis=dim)
        before = lax.ppermute(last, axis, up)
        after = lax.ppermute(leading, axis, down)
        value = jnp.concatenate([before, value, after], axis=dim)
    return value


def from_root(block, axis, holder):
    block = jnp.where(lax.axis_index(axis) == holder, block, jnp.zeros_like(block))
    return lax.psum(block, axis)


def shift_next(field, axis):
    size = field.shape[axis]
    rest = lax.slice_in_dim(field, 1, size, axis=axis)
    return jnp.concatenate(
        [rest, jnp.zeros_like(lax.slice_in_dim(field, 0, 1, axis=axis))], axis=axis
    )


def shift_prev(field, axis):
    size = field.shape[axis]
    rest = lax.slice_in_dim(field, 0, size - 1, axis=axis)
    return jnp.concatenate(
        [jnp.zeros_like(lax.slice_in_dim(field, 0, 1, axis=axis)), rest], axis=axis
    )


def forward(field, axis):
    return shift_next(field, axis) - field


def backward(field, axis):
    return field - shift_prev(field, axis)


def curl_curl(padded):
    ex_part = padded[:, 0]
    ey_part = padded[:, 1]
    ez_part = padded[:, 2]
    hx_part = forward(ez_part, 4) - forward(ey_part, 2)
    hy_part = forward(ex_part, 2) - forward(ez_part, 3)
    hz_part = forward(ey_part, 3) - forward(ex_part, 4)
    cx_part = backward(hz_part, 4) - backward(hy_part, 2)
    cy_part = backward(hx_part, 2) - backward(hz_part, 3)
    cz_part = backward(hy_part, 3) - backward(hx_part, 4)
    whole = jnp.stack([cx_part, cy_part, cz_part], axis=1)
    return whole[:, :, :, 1:-1, 1:-1, 1:-1]


def apply_operator(field, padded, conductance):
    curled = curl_curl(padded)
    real_part = curled[:, :, 0] - conductance * field[:, :, 1]
    imag_part = curled[:, :, 1] + conductance * field[:, :, 0]
    return jnp.stack([real_part, imag_part], axis=2)


def precondition(field, conductance):
    denom = 16.0 + conductance * conductance
    m_real = 4.0 / denom
    m_imag = -conductance / denom
    real_part = m_real * field[:, :, 0] - m_imag * field[:, :, 1]
    imag_part = m_real * field[:, :, 1] + m_imag * field[:, :, 0]
    return jnp.stack([real_part, imag_part], axis=2)


def inner(left, right):
    real_part = jnp.sum(
        left[:, :, 0] * right[:, :, 0] + left[:, :, 1] * right[:, :, 1], axis=(1, 2, 3, 4)
    )
    imag_part = jnp.sum(
        left[:, :, 0] * right[:, :, 1] - left[:, :, 1] * right[:, :, 0], axis=(1, 2, 3, 4)
    )
    return (real_part, imag_part)


def squares(field):
    return jnp.sum(field * field, axis=(1, 2, 3, 4, 5))


def cdiv(numer, denom, floor):
    size = jnp.maximum(denom[0] * denom[0] + denom[1] * denom[1], floor)
    return (
        (numer[0] * denom[0] + numer[1] * denom[1]) / size,
        (numer[1] * denom[0] - numer[0] * denom[1]) / size,
    )


def cmul(left, right):
    return (left[0] * right[0] - left[1] * right[1], left[0] * right[1] + left[1] * right[0])


def cscale(scalar, field):
    s_real = scalar[0][:, None, None, None, None]
    s_imag = scalar[1][:, None, None, None, None]
    real_part = s_real * field[:, :, 0] - s_imag * field[:, :, 1]
    imag_part = s_real * field[:, :, 1] + s_imag * field[:, :, 0]
    return jnp.stack([real_part, imag_part], axis=2)


def impedance(top, below):
    ones = jnp.ones_like(top[0, 0, 0])
    zeros = jnp.zeros_like(top[0, 0, 0])
    ex_pol = []
    ey_pol = []
    hx_pol = []
    hy_pol = []
    for pol in range(2):
        ex_pol.append((top[pol, 0, 0], top[pol, 0, 1]))
        ey_pol.append((top[pol, 1, 0], top[pol, 1, 1]))
        base_x = ones if pol == 0 else zeros
        base_y = ones if pol == 1 else zeros
        hx_pol.append(
            (
                base_x - 2.0 * (below[pol, 1, 0] - top[pol, 1, 0]),
                -2.0 * (below[pol, 1, 1] - top[pol, 1, 1]),
            )
        )
        hy_pol.append(
            (
                base_y + 2.0 * (below[pol, 0, 0] - top[pol, 0, 0]),
                2.0 * (below[pol, 0, 1] - top[pol, 0, 1]),
            )
        )

    def csub(left, right):
        return (left[0] - right[0], left[1] - right[1])

    det = csub(cmul(hx_pol[0], hy_pol[1]), cmul(hx_pol[1], hy_pol[0]))
    zxx = cdiv(csub(cmul(ex_pol[0], hy_pol[1]), cmul(ex_pol[1], hy_pol[0])), det, 0.25)
    zxy = cdiv(csub(cmul(ex_pol[1], hx_pol[0]), cmul(ex_pol[0], hx_pol[1])), det, 0.25)
    zyx = cdiv(csub(cmul(ey_pol[0], hy_pol[1]), cmul(ey_pol[1], hy_pol[0])), det, 0.25)
    zyy = cdiv(csub(cmul(ey_pol[1], hx_pol[0]), cmul(ey_pol[0], hx_pol[1])), det, 0.25)
    return jnp.stack([zxx[0], zxx[1], zxy[0], zxy[1], zyx[0], zyx[1], zyy[0], zyy[1]], axis=0)


def hazard_rows(chosen, spectra, scenario_tile, slots, tiles):
    bx_real = spectra[:, 0][None, :]
    bx_imag = spectra[:, 1][None, :]
    by_real = spectra[:, 2][None, :]
    by_imag = spectra[:, 3][None, :]
    zxx_r, zxx_i, zxy_r, zxy_i, zyx_r, zyx_i, zyy_r, zyy_i = [
        chosen[index][:, None] for index in range(8)
    ]
    gx_real = zxx_r * bx_real - zxx_i * bx_imag + zxy_r * by_real - zxy_i * by_imag
    gx_imag = zxx_r * bx_imag + zxx_i * bx_real + zxy_r * by_imag + zxy_i * by_real
    gy_real = zyx_r * bx_real - zyx_i * bx_imag + zyy_r * by_real - zyy_i * by_imag
    gy_imag = zyx_r * bx_imag + zyx_i * bx_real + zyy_r * by_imag + zyy_i * by_real
    rows = chosen.shape[1]
    tile_row = jnp.arange(rows, dtype=jnp.int32) // slots % tiles
    weight = jnp.where(tile_row[:, None] == scenario_tile[None, :], 1.0, 0.25).astype(spectra.dtype)
    return weight * (gx_real * gx_real + gx_imag * gx_imag + gy_real * gy_real + gy_imag * gy_imag)


def operate(field, conductance):
    padded = padded_2(field, (("gz", 3), ("gx", 4)), 1)
    padded = jnp.pad(padded, ((0, 0), (0, 0), (0, 0), (0, 0), (0, 0), (1, 1)))
    return apply_operator(field, padded, conductance)


def per_device(right_side, conductance, owned_cells, spectra, scenario_tile):
    solution = jnp.zeros_like(right_side)
    residual = right_side
    direction = right_side
    image = right_side
    rho_prev = None
    alpha = None
    omega = None
    floor = None
    rho = None
    for step in range(ITERS):
        part_real, part_imag = inner(right_side, residual)
        rho = lax.psum((part_real, part_imag), ("gz", "gx"))
        if step == 0:
            floor = 1e-06 * rho[0] * rho[0]
            direction = residual
        else:
            beta = cmul(cdiv(rho, rho_prev, floor), cdiv(alpha, omega, 0.0001))
            direction = residual + cscale(beta, direction - cscale(omega, image))
        search = precondition(direction, conductance)
        image = operate(search, conductance)
        den_real, den_imag = inner(right_side, image)
        alpha = cdiv(rho, lax.psum((den_real, den_imag), ("gz", "gx")), floor)
        middle = residual - cscale(alpha, image)
        smooth = precondition(middle, conductance)
        bent = operate(smooth, conductance)
        bm_real, bm_imag = inner(bent, middle)
        bent_local = squares(bent)
        bm_real, bm_imag, bent_norm = lax.psum((bm_real, bm_imag, bent_local), ("gz", "gx"))
        bent_norm = bent_norm + 1e-06
        omega = (bm_real / bent_norm, bm_imag / bent_norm)
        solution = solution + cscale(alpha, search) + cscale(omega, smooth)
        residual = middle - cscale(omega, bent)
        rho_prev = rho
    surface = impedance(solution[:, :, :, 0], solution[:, :, :, 1])
    tile_cells = surface.shape[1] * surface.shape[2]
    local_tile = surface.reshape(8, tile_cells)
    tile = from_root(local_tile, "gz", 0)
    tiles = lax.axis_size("gx")
    slots = owned_cells.shape[2]
    whole = lax.all_gather(tile, "gx", axis=1, tiled=True)
    offsets = (jnp.arange(tiles, dtype=jnp.int32) * tile_cells)[:, None]
    index = (owned_cells[0] + offsets).reshape(-1)
    chosen = jnp.take(whole, index, axis=1)
    hazard = hazard_rows(chosen, spectra, scenario_tile, slots, tiles)
    return (solution, hazard)


def solution(mesh):
    return jax.shard_map(
        per_device,
        mesh=mesh,
        in_specs=(
            P(None, None, None, "gz", "gx", None),
            P("gz", "gx", None),
            P(("gz", "gx"), None, None),
            P(),
            P(),
        ),
        out_specs=(P(None, None, None, "gz", "gx", None), P(("gz", "gx"), None)),
        check_vma=False,
    )
```

profile of v0, /device:TPU:1, one launch (start us, length us, event | category | flops | bytes accessed | tf_op | source)
XLA Modules:
  0.0 1039.2 jit_solution(18396750720864668991)
XLA Ops:
  9.5 4.0 collective-permute-start
  17.1 3.8 collective-permute-done.1
  21.0 6.4 collective-permute-start.2
  29.5 4.6 collective-permute-done.3
  40.3 67.3 %all-reduce.85 = (f32[2]{0:T(128)S(1)}, f32[2]{0:T(128)S(1)}, f32[2]{0:T(128)S(1)}, f32[2]{0:T(128)S(1)}) all-reduce(f32[2]{0:T(128)S(1)} %get-tuple-element.25, f32[2]{0:T(128)S(1)} %get-tuple-element.15, f32[2]{0:T(128)S(1)} %get-tuple-element.24, f32[2]{0:T(128)S(1)} %get-tuple-element.14), channel_id=1, replica_groups=mesh['gz'=32,'gx'=4] {'gz','gx'}, use_global_device_ids=true, to_apply=%region_1.0 | all-reduce | flops 8 | bytes 64 | tf_op jit(solution)/shard_map/psum | solution.py:187
  115.8 3.8 collective-permute-done.5
  119.6 5.6 collective-permute-start.6
  127.5 4.6 collective-permute-done.7
  137.7 67.0 %all-reduce.84 = (f32[2]{0:T(128)S(1)}, f32[2]{0:T(128)S(1)}, f32[2]{0:T(128)S(1)}) all-reduce(f32[2]{0:T(128)S(1)} %get-tuple-element.13, f32[2]{0:T(128)S(1)} %fusion.5, f32[2]{0:T(128)S(1)} %get-tuple-element.12), channel_id=1, replica_groups=mesh['gz'=32,'gx'=4] {'gz','gx'}, use_global_device_ids=true, to_apply=%region_13.14 | all-reduce | flops 6 | bytes 48 | tf_op jit(solution)/shard_map/psum | solution.py:203
  204.7 2.9 multiply_subtract_fusion.14
  208.2 62.5 %all-reduce.83 = (f32[2]{0:T(128)S(1)}, f32[2]{0:T(128)S(1)}) all-reduce(f32[2]{0:T(128)S(1)} %get-tuple-element.23, f32[2]{0:T(128)S(1)} %get-tuple-element.22), channel_id=1, replica_groups=mesh['gz'=32,'gx'=4] {'gz','gx'}, use_global_device_ids=true, to_apply=%region_15.16 | all-reduce | flops 4 | bytes 32 | tf_op jit(solution)/shard_map/psum | solution.py:187
  277.7 3.8 collective-permute-done.9
  281.6 5.6 collective-permute-start.10
  289.3 4.6 collective-permute-done.11
  300.8 67.0 %all-reduce.82 = (f32[2]{0:T(128)S(1)}, f32[2]{0:T(128)S(1)}) all-reduce(f32[2]{0:T(128)S(1)} %get-tuple-element.21, f32[2]{0:T(128)S(1)} %get-tuple-element.20), channel_id=1, replica_groups=mesh['gz'=32,'gx'=4] {'gz','gx'}, use_global_device_ids=true, to_apply=%region_21.22 | all-reduce | flops 4 | bytes 32 | tf_op jit(solution)/shard_map/psum | solution.py:197
  376.3 3.5 collective-permute-done.13
  379.9 5.0 collective-permute-start.14
  387.3 4.4 collective-permute-done.15
  398.0 67.2 %all-reduce.81 = (f32[2]{0:T(128)S(1)}, f32[2]{0:T(128)S(1)}, f32[2]{0:T(128)S(1)}) all-reduce(f32[2]{0:T(128)S(1)} %get-tuple-element.11, f32[2]{0:T(128)S(1)} %fusion.6, f32[2]{0:T(128)S(1)} %get-tuple-element.10), channel_id=1, replica_groups=mesh['gz'=32,'gx'=4] {'gz','gx'}, use_global_device_ids=true, to_apply=%region_27.28 | all-reduce | flops 6 | bytes 48 | tf_op jit(solution)/shard_map/psum | solution.py:203
  469.8 64.0 %all-reduce.80 = (f32[2]{0:T(128)S(1)}, f32[2]{0:T(128)S(1)}) all-reduce(f32[2]{0:T(128)S(1)} %get-tuple-element.19, f32[2]{0:T(128)S(1)} %get-tuple-element.18), channel_id=1, replica_groups=mesh['gz'=32,'gx'=4] {'gz','gx'}, use_global_device_ids=true, to_apply=%region_29.30 | all-reduce | flops 4 | bytes 32 | tf_op jit(solution)/shard_map/psum | solution.py:187
  540.2 4.1 collective-permute-done.17
  545.7 4.9 collective-permute-start.18
  557.7 3.0 select_maximum_fusion.2
  565.3 67.1 %all-reduce.79 = (f32[2]{0:T(128)S(1)}, f32[2]{0:T(128)S(1)}) all-reduce(f32[2]{0:T(128)S(1)} %get-tuple-element.17, f32[2]{0:T(128)S(1)} %get-tuple-element.16), channel_id=1, replica_groups=mesh['gz'=32,'gx'=4] {'gz','gx'}, use_global_device_ids=true, to_apply=%region_35.36 | all-reduce | flops 4 | bytes 32 | tf_op jit(solution)/shard_map/psum | solution.py:197
  641.3 3.8 collective-permute-done.21
  646.2 5.6 collective-permute-start.22
  653.9 4.6 collective-permute-done.23
  666.0 67.0 %all-reduce.78 = (f32[2]{0:T(128)S(1)}, f32[2]{0:T(128)S(1)}, f32[2]{0:T(128)S(1)}) all-reduce(f32[2]{0:T(128)S(1)} %get-tuple-element.9, f32[2]{0:T(128)S(1)} %fusion.7, f32[2]{0:T(128)S(1)} %get-tuple-element.8), channel_id=1, replica_groups=mesh['gz'=32,'gx'=4] {'gz','gx'}, use_global_device_ids=true, to_apply=%region_41.42 | all-reduce | flops 6 | bytes 48 | tf_op jit(solution)/shard_map/psum | solution.py:203
  738.0 260.2 %all-reduce.88.cloned.1.call-done = f32[8,4096]{1,0:T(8,128)} async-done(((f32[8,4096]{1,0:T(8,128)}), f32[8,4096]{1,0:T(8,128)}) %all-reduce.88.cloned.1.call-update) | async-done | bytes 131088 | tf_op jit(solution)/shard_map/psum | solution.py:24
  998.1 22.9 %all_gather.3 = f32[8,16384]{1,0:T(8,128)S(1)} all-gather(f32[8,4096]{1,0:T(8,128)} %all-reduce.88.cloned.1.call-done), channel_id=1, replica_groups=mesh['gz'=32,'gx'=4] {'gx'}, dimensions={1}, use_global_device_ids=true | all-gather | bytes 655360 | tf_op jit(solution)/shard_map/all_gather | solution.py:215
  1021.0 5.3 copy.348
  1026.3 4.0 gather_fusion
  (301 shorter events, 113.3 us)
Async XLA Ops:
  7.2 991.0 %all-reduce.88.cloned.1.call-start = ((), (), s32[]{:S(2)}) async-start(), calls=%async_computation | async-start | bytes 262144 | tf_op jit(solution)/shard_map/psum | solution.py:24
  9.5 7.6 collective-permute-start
  13.6 7.3 collective-permute-start.1
  21.0 8.6 collective-permute-start.2
  27.4 6.8 collective-permute-start.3
  109.9 5.8 collective-permute-start.4
  112.7 6.9 collective-permute-start.5
  119.6 7.8 collective-permute-start.6
  125.3 6.8 collective-permute-start.7
  271.9 5.7 collective-permute-start.8
  274.5 7.0 collective-permute-start.9
  281.6 7.7 collective-permute-start.10
  287.1 6.8 collective-permute-start.11
  371.3 5.0 collective-permute-start.12
  372.6 7.2 collective-permute-start.13
  379.9 7.4 collective-permute-start.14
  384.9 6.8 collective-permute-start.15
  535.5 4.7 collective-permute-start.16
  536.8 7.5 collective-permute-start.17
  545.7 10.4 %collective-permute-start.18 = (f32[2,3,2,6,1,128]{5,4,1,0,3,2:T(1,128)}, f32[2,3,2,6,1,128]{5,4,1,0,3,2:T(1,128)}, u32[]{:S(2)}, u32[]{:S(2)}) collective-permute-start(f32[2,3,2,6,1,128]{5,4,1,0,3,2:T(1,128)} %get-tuple-element.147), channel_id=1, source_target_pairs={{0,1},{1,2},{2,3},{4,5},{5,6},{6,7},{8,9},{9,10},{10,11},{12,13},{... | collective-permute-start | bytes 110600 | tf_op jit(solution)/shard_map/ppermute | solution.py:16
  550.6 7.1 collective-permute-start.19
  564.5 67.9 %copy-start.39 = (f32[2]{0:T(128)S(1)}, f32[2]{0:T(128)}, u32[]{:S(2)}) copy-start(f32[2]{0:T(128)} %copy-done.38) | copy-start | bytes 28
  565.3 69.4 %copy-start.5 = (f32[2,3,1,4,32,128]{5,4,0,3,2,1:T(8,128)S(1)}, f32[2,3,1,4,32,128]{5,4,0,3,2,1:T(8,128)}, u32[]{:S(2)}) copy-start(f32[2,3,1,4,32,128]{5,4,0,3,2,1:T(8,128)} %copy-done.4) | copy-start | bytes 1179652
  565.3 69.4 %copy-start.7 = (f32[2,3,1,4,32,128]{5,4,0,3,2,1:T(8,128)S(1)}, f32[2,3,1,4,32,128]{5,4,0,3,2,1:T(8,128)}, u32[]{:S(2)}) copy-start(f32[2,3,1,4,32,128]{5,4,0,3,2,1:T(8,128)} %copy-done.6) | copy-start | bytes 1179652
  635.5 5.7 collective-permute-start.20
  638.1 7.0 collective-permute-start.21
  646.2 7.7 collective-permute-start.22
  651.8 6.8 collective-permute-start.23
  664.8 68.4 %copy-start.29 = (f32[2,3,1,4,32,128]{5,4,1,0,3,2:T(8,128)S(1)}, f32[2,3,1,4,32,128]{5,4,1,0,3,2:T(8,128)}, u32[]{:S(2)}) copy-start(f32[2,3,1,4,32,128]{5,4,1,0,3,2:T(8,128)} %get-tuple-element.198) | copy-start | bytes 1179652
  664.8 68.4 %copy-start.30 = (f32[2,3,1,4,32,128]{5,4,1,0,3,2:T(8,128)S(1)}, f32[2,3,1,4,32,128]{5,4,1,0,3,2:T(8,128)}, u32[]{:S(2)}) copy-start(f32[2,3,1,4,32,128]{5,4,1,0,3,2:T(8,128)} %get-tuple-element.199) | copy-start | bytes 1179652
  664.8 68.4 %copy-start.31 = (f32[2,3,1,4,32,128]{5,4,1,0,3,2:T(8,128)S(1)}, f32[2,3,1,4,32,128]{5,4,1,0,3,2:T(8,128)}, u32[]{:S(2)}) copy-start(f32[2,3,1,4,32,128]{5,4,1,0,3,2:T(8,128)} %get-tuple-element.194) | copy-start | bytes 1179652
  664.8 68.4 %copy-start.32 = (f32[2,3,1,4,32,128]{5,4,1,0,3,2:T(8,128)S(1)}, f32[2,3,1,4,32,128]{5,4,1,0,3,2:T(8,128)}, u32[]{:S(2)}) copy-start(f32[2,3,1,4,32,128]{5,4,1,0,3,2:T(8,128)} %get-tuple-element.195) | copy-start | bytes 1179652
  (38 other events, 444.1 us)
Sparse Core Ops, SparseCore 0:
  737.1 260.9 all-reduce.87
where the time goes:
time: 1050 us; the launch traced here: 1040 us
  blocking collectives  552 us (53%)
  waiting for transfers between devices  319 us (30%)
  starting transfers between devices  68.3 us (7%)
  other arithmetic  55.8 us (5%)
  local copies, waits for them, and re-layouts  28.6 us (3%)
  between operations  15.8 us (2%)
    psum x1, waiting for transfers between devices, from_root(): return lax.psum(block, axis)  260 us
    psum x3, blocking collectives, per_device(): lax.psum((bm_real, bm_imag, bent_local), ('gz', 'gx'))  201 us
    psum x3, blocking collectives, per_device(): rho = lax.psum((part_real, part_imag), ('gz', 'gx'))  194 us
    psum x2, blocking collectives, per_device(): alpha = cdiv(rho, lax.psum((den_real, den_imag), ('gz', 'gx')), floor)  134 us
    ppermute x12, starting transfers between devices, padded_2(): before = lax.ppermute(last, axis, up)  47.6 us
    ppermute x12, waiting for transfers between devices, padded_2(): after = lax.ppermute(leading, axis, down)  47.3 us
    all_gather x1, blocking collectives, per_device(): whole = lax.all_gather(tile, 'gx', axis=1, tiled=True)  22.9 us
  transfers between devices with their start and end apart: 25, of which 19 were waited for; matrix products, arithmetic and copies ran while one was open for 1% of the time, Pallas kernels for 0%

commit v1 on v0

v1 whole, which is shorter than its diff:
```python
import jax
import jax.numpy as jnp
from jax import lax
from jax.experimental import pallas as pl
from jax.experimental.pallas import tpu as pltpu
from jax.sharding import PartitionSpec as P

SHIFTS = (1.8, 0.6, 1.8, 0.6, 1.8, 0.6)
SCALE = 1.0
ITERS = 3
REACH = 3
SIDE = 2 * REACH
NF = 12
CX, NZL, NY = 32, 4, 128
WX = 48
EZ = NZL + 2 * REACH
BACK = 40
f32 = jnp.float32
VM = pl.BlockSpec(memory_space=pltpu.VMEM)
LIMIT = 48 * 1024 * 1024


def call(body, outs, scratch=(), n_in=1, flops=0, moved=0):
    return pl.pallas_call(
        body,
        out_shape=[jax.ShapeDtypeStruct(s, d) for s, d in outs],
        in_specs=[VM] * n_in,
        out_specs=[VM] * len(outs),
        scratch_shapes=list(scratch),
        compiler_params=pltpu.CompilerParams(vmem_limit_bytes=LIMIT),
        cost_estimate=pl.CostEstimate(flops=flops, bytes_accessed=moved, transcendentals=0),
    )


def pack_x(r, k, up, down):
    for f in range(NF + 1):
        for z in range(NZL):
            row = (f * NZL + z) * SIDE
            src = k.at[z] if f == NF else r.at[f, z]
            up[row : row + SIDE, :] = src[CX - SIDE : CX, :]
            down[row : row + SIDE, :] = src[0:SIDE, :]


def pack_z(r, k, left, right, up, down):
    width = CX + 2 * SIDE
    for f in range(NF + 1):
        for z in range(NZL):
            near = (f * NZL + z) * SIDE
            src = k.at[z] if f == NF else r.at[f, z]
            for out, first in ((up, NZL - REACH), (down, 0)):
                if first <= z < first + REACH:
                    row = (f * REACH + z - first) * width
                    out[row : row + SIDE, :] = left[near : near + SIDE, :]
                    out[row + SIDE : row + SIDE + CX, :] = src[:, :]
                    out[row + SIDE + CX : row + width, :] = right[near : near + SIDE, :]


def lanes():
    lane = lax.broadcasted_iota(jnp.int32, (WX, NY), 1)
    return lane == 0, lane == NY - 1


def next_y(a, last):
    return jnp.where(last, 0.0, pltpu.roll(a, NY - 1, 1))


def next_x(a):
    return pltpu.roll(a, WX - 1, 0)


def prev_x(a):
    return pltpu.roll(a, 1, 0)


def h_flat(y, base, z, last):
    ex, ey, ez = y[base, z], y[base + 2, z], y[base + 4, z]
    hx = next_y(ez, last) - ez - (y[base + 2, z + 1] - ey)
    hy = y[base, z + 1] - ex - (next_x(ez) - ez)
    return hx, hy


def smooth(b, y, m, base, z):
    mr, mi = m[0, z], m[1, z]
    for c in range(3):
        re, im = b[base + 2 * c, z], b[base + 2 * c + 1, z]
        y[base + 2 * c, z] = mr * re - mi * im
        y[base + 2 * c + 1, z] = mr * im + mi * re


def apply_k(b, y, bn, yn, m, lo, hi, shift, want_y):
    first, last = lanes()
    own = (1.0 - shift) / SCALE
    inv = 1.0 / SCALE

    def pol(p, _):
        base = p * 6

        def layer(z, prev):
            out = []
            for q in range(2):
                e = base + q
                hxp, hyp = prev[q]
                ex, ey, ez = y[e, z], y[e + 2, z], y[e + 4, z]
                hx, hy = h_flat(y, e, z, last)
                hz = next_x(ey) - ey - (next_y(ex, last) - ex)
                cx = hz - jnp.where(first, -ex, pltpu.roll(hz, 1, 1)) - (hy - hyp)
                cy = hx - hxp - (hz - prev_x(hz))
                cz = hy - prev_x(hy) - (hx - jnp.where(first, ez, pltpu.roll(hx, 1, 1)))
                for c, (cur, old) in enumerate(((cx, ex), (cy, ey), (cz, ez))):
                    new = cur - 4.0 * old
                    if inv != 1.0:
                        new = new * inv
                    bn[e + 2 * c, z] = new + own * b[e + 2 * c, z]
                out.append((hx, hy))
            if want_y:
                smooth(bn, yn, m, base, z)
            return tuple(out)

        start = tuple(h_flat(y, base + q, lo - 1, last) for q in range(2))
        lax.fori_loop(lo, hi, layer, start)
        return 0

    lax.fori_loop(0, 2, pol, 0)


def all_smooth(b, y, m):
    def pol(p, _):
        def layer(z, _):
            smooth(b, y, m, p * 6, z)
            return 0

        return lax.fori_loop(0, EZ, layer, 0)

    lax.fori_loop(0, 2, pol, 0)


def first_half(r, k, left, right, below, above, b1, b2, b3w, m, up, down, ba, bb, ya, yb, kx):
    width = CX + 2 * SIDE
    x0 = 8 - SIDE
    for f in range(NF + 1):
        dst = kx if f == NF else ba.at[f]
        src = k if f == NF else r.at[f]
        zero = jnp.zeros((EZ, 8, NY), f32)
        dst[:, 0:8, :] = zero
        dst[:, WX - 8 : WX, :] = zero
        for z in range(NZL):
            near = (f * NZL + z) * SIDE
            dst[REACH + z, x0:8, :] = left[near : near + SIDE, :]
            dst[REACH + z, 8 : 8 + CX, :] = src[z]
            dst[REACH + z, 8 + CX : 8 + CX + SIDE, :] = right[near : near + SIDE, :]
        for z in range(REACH):
            row = (f * REACH + z) * width
            dst[z, x0 : x0 + width, :] = below[row : row + width, :]
            dst[REACH + NZL + z, x0 : x0 + width, :] = above[row : row + width, :]

    def weights(z, _):
        kz = kx[z]
        inv = jnp.where(kz > 0.0, 1.0, 0.0) / (16.0 + kz * kz)
        m[0, z] = 4.0 * inv
        m[1, z] = -kz * inv
        return 0

    lax.fori_loop(0, EZ, weights, 0)
    all_smooth(ba, ya, m)

    def keep(src, out):
        def field(f, _):
            out[f] = src[f, REACH : REACH + NZL, 8 : 8 + CX, :]
            return 0

        lax.fori_loop(0, NF, field, 0)

    apply_k(ba, ya, bb, yb, m, 1, EZ - 1, SHIFTS[0], True)
    keep(bb, b1)
    apply_k(bb, yb, ba, ya, m, 2, EZ - 2, SHIFTS[1], True)
    keep(ba, b2)
    apply_k(ba, ya, bb, yb, m, 3, EZ - 3, SHIFTS[2], False)
    cut = (WX - BACK) // 2

    def field(f, _):
        b3w[f] = bb[f, REACH : REACH + NZL]
        up[f] = bb[f, NZL : REACH + NZL, cut : cut + BACK, :]
        down[f] = bb[f, REACH : 2 * REACH, cut : cut + BACK, :]
        return 0

    lax.fori_loop(0, NF, field, 0)


PAIRS = [(i, j) for i in range(7) for j in range(i, 7)]
LOW = [pair for pair in PAIRS if pair[1] <= REACH]
HIGH = [pair for pair in PAIRS if pair[1] > REACH]
SLOT = {}
for _pair in LOW + HIGH:
    SLOT[_pair] = sum(1 if a == b else 2 for a, b in SLOT)


def gram(read, pairs, out):
    used = sorted({i for pair in pairs for i in pair})
    count = sum(1 if i == j else 2 for i, j in pairs)

    def pol(p, _):
        def block(step, acc):
            c, z = step // NZL, step % NZL
            acc = list(acc)
            for xb in range(CX // 8):
                vec = {}
                for i in used:
                    vec[i] = (read(i, p * 6 + 2 * c, z, xb), read(i, p * 6 + 2 * c + 1, z, xb))
                at = 0
                for i, j in pairs:
                    (ar, ai), (br, bi) = vec[i], vec[j]
                    acc[at] = acc[at] + (ar * br + ai * bi)
                    at += 1
                    if i != j:
                        acc[at] = acc[at] + (ar * bi - ai * br)
                        at += 1
            return tuple(acc)

        acc = lax.fori_loop(0, 3 * NZL, block, (jnp.zeros((8, NY), f32),) * count)
        at = 0
        for i, j in pairs:
            for part in range(1 if i == j else 2):
                out[pl.ds(p * 64 + SLOT[i, j] + part, 1), :] = jnp.sum(acc[at], axis=0, keepdims=True)
                at += 1
        return 0

    lax.fori_loop(0, 2, pol, 0)


def reader(refs, wide):
    def read(i, f, z, xb):
        off = 8 if i in wide else 0
        return refs[i][f, z, pl.ds(off + 8 * xb, 8), :]

    return read


def low_gram(b0, b1, b2, b3w, part):
    part[...] = jnp.zeros((NY, NY), f32)
    gram(reader([b0, b1, b2, b3w], (3,)), LOW, part)


def second_half(b0, b1, b2, b3w, m, below, above, part, owned, b4, b5, send, ba, bb, ya, yb, bc, total):
    cut = (WX - BACK) // 2

    def field(f, _):
        zero = jnp.zeros((REACH, 8, NY), f32)
        for first, halo in ((0, below), (REACH + NZL, above)):
            ba[f, first : first + REACH, 0:8, :] = zero
            ba[f, first : first + REACH, WX - 8 : WX, :] = zero
            ba[f, first : first + REACH, cut : cut + BACK, :] = halo[f]
        ba[f, REACH : REACH + NZL] = b3w[f]
        return 0

    lax.fori_loop(0, NF, field, 0)
    all_smooth(ba, ya, m)

    def keep(src, out):
        def field(f, _):
            out[f] = src[f, REACH : REACH + NZL, 8 : 8 + CX, :]
            return 0

        lax.fori_loop(0, NF, field, 0)

    apply_k(ba, ya, bb, yb, m, 1, EZ - 1, SHIFTS[3], True)
    keep(bb, b4)
    apply_k(bb, yb, ba, ya, m, 2, EZ - 2, SHIFTS[4], True)
    keep(ba, b5)
    apply_k(ba, ya, bc, yb, m, 3, EZ - 3, SHIFTS[5], False)
    total[...] = part[...]
    low = reader([b0, b1, b2, b3w, b4, b5], (3,))

    def read(i, f, z, xb):
        if i == 6:
            return bc[f, REACH + z, pl.ds(8 + 8 * xb, 8), :]
        return low(i, f, z, xb)

    gram(read, HIGH, total)
    sums = jnp.sum(jnp.transpose(total[...]), axis=0, keepdims=True)
    cells = jnp.concatenate([owned[j : j + 1, :] for j in range(4)], axis=1).astype(f32)
    send[...] = jnp.broadcast_to(jnp.concatenate([sums, cells], axis=1), (128, 2 * NY))


def cadd(a, b):
    return (a[0] + b[0], a[1] + b[1])


def csub(a, b):
    return (a[0] - b[0], a[1] - b[1])


def cmul(a, b):
    return (a[0] * b[0] - a[1] * b[1], a[0] * b[1] + a[1] * b[0])


def cconj_mul(a, b):
    return (a[0] * b[0] + a[1] * b[1], a[0] * b[1] - a[1] * b[0])


def cdiv(numer, denom, floor):
    size = jnp.maximum(denom[0] * denom[0] + denom[1] * denom[1], floor)
    return (
        (numer[0] * denom[0] + numer[1] * denom[1]) / size,
        (numer[1] * denom[0] - numer[0] * denom[1]) / size,
    )


def tree(terms):
    terms = list(terms)
    while len(terms) > 1:
        terms = [cadd(*terms[i : i + 2]) if i + 1 < len(terms) else terms[i] for i in range(0, len(terms), 2)]
    return terms[0]


def combine(a, scale, b):
    out = []
    for i in range(max(len(a), len(b))):
        if i >= len(b):
            out.append(a[i])
        elif i >= len(a):
            out.append(cmul(scale, b[i]))
        else:
            out.append(cadd(a[i], cmul(scale, b[i])))
    return out


def times_k(a):
    zero = (jnp.zeros_like(a[0][0]),) * 2
    out = [(SHIFTS[i] * v[0], SHIFTS[i] * v[1]) for i, v in enumerate(a)] + [zero]
    return [
        cadd(out[i], (SCALE * a[i - 1][0], SCALE * a[i - 1][1])) if i > 0 else out[i]
        for i in range(len(out))
    ]


def coefficients(entry):
    def g(i, j):
        if i > j:
            re, im = g(j, i)
            return (re, -im)
        if i == j:
            return (entry(SLOT[i, j]), 0.0)
        return (entry(SLOT[i, j]), entry(SLOT[i, j] + 1))

    def times_g(b, rows):
        return [tree([cmul(g(i, j), b[j]) for j in range(len(b))]) for i in range(rows)]

    def dot(a, gb):
        return tree([cconj_mul(a[i], gb[i]) for i in range(len(a))])

    def shadow(b):
        return tree([cmul(g(0, j), b[j]) for j in range(len(b))])

    one = jnp.ones_like(entry(0))
    residual = [(one, jnp.zeros_like(one))]
    direction = residual
    solution = []
    for step in range(ITERS):
        rho = shadow(residual)
        if step == 0:
            floor = 1e-06 * rho[0] * rho[0]
        else:
            beta = cmul(cdiv(rho, rho_prev, floor), cdiv(alpha, omega, 0.0001))
            minus = (-omega[0], -omega[1])
            direction = combine(residual, beta, combine(direction, minus, image))
        image = times_k(direction)
        alpha = cdiv(rho, shadow(image), floor)
        middle = combine(residual, (-alpha[0], -alpha[1]), image)
        bent = times_k(middle)
        seen = times_g(bent, len(bent))
        norm = dot(bent, seen)[0] + 1e-06
        against = dot(middle, seen)
        omega = (against[0] / norm, -against[1] / norm)
        solution = combine(combine(solution, alpha, direction), omega, middle)
        residual = combine(middle, (-omega[0], -omega[1]), bent)
        rho_prev = rho
    return solution


def impedance(x, z0, rows):
    def e(p, c, z):
        f = p * 6 + 2 * c
        return (x[f, z, rows, :], x[f + 1, z, rows, :])

    ex, ey, hx, hy = [], [], [], []
    for p in range(2):
        ex0, ey0 = e(p, 0, z0), e(p, 1, z0)
        ex1, ey1 = e(p, 0, z0 + 1), e(p, 1, z0 + 1)
        ex.append(ex0)
        ey.append(ey0)
        one_x, one_y = (1.0, 0.0) if p == 0 else (0.0, 1.0)
        hx.append((one_x - 2.0 * (ey1[0] - ey0[0]), -2.0 * (ey1[1] - ey0[1])))
        hy.append((one_y + 2.0 * (ex1[0] - ex0[0]), 2.0 * (ex1[1] - ex0[1])))
    det = csub(cmul(hx[0], hy[1]), cmul(hx[1], hy[0]))
    zxx = cdiv(csub(cmul(ex[0], hy[1]), cmul(ex[1], hy[0])), det, 0.25)
    zxy = cdiv(csub(cmul(ex[1], hx[0]), cmul(ex[0], hx[1])), det, 0.25)
    zyx = cdiv(csub(cmul(ey[0], hy[1]), cmul(ey[1], hy[0])), det, 0.25)
    zyy = cdiv(csub(cmul(ey[1], hx[0]), cmul(ey[0], hx[1])), det, 0.25)
    return [*zxx, *zxy, *zyx, *zyy]


def finish(tile, got, b0, b1, b2, b3w, b4, b5, m, x, send, surface, picked):
    sub = lax.broadcasted_iota(jnp.int32, (8, NY), 0)
    row = jnp.broadcast_to(jnp.sum(got[:, 0:NY], axis=0, keepdims=True), (8, NY))
    table = jnp.where(sub == 0, row, pltpu.roll(row, 64, 1))
    cache = {}

    def entry(slot):
        if slot not in cache:
            cache[slot] = jnp.broadcast_to(table[:, slot : slot + 1], (8, NY))
        return cache[slot]

    coefs = coefficients(entry)
    refs = [b0, b1, b2, b3w, b4, b5]
    read = reader(refs, (3,))
    for p in range(2):
        scal = [tuple(jnp.broadcast_to(part[p : p + 1, :], (8, NY)) for part in c) for c in coefs]

        def block(step, _):
            c, z = step // NZL, step % NZL
            f = p * 6 + 2 * c
            for xb in range(CX // 8):
                terms = [cmul(scal[i], (read(i, f, z, xb), read(i, f + 1, z, xb))) for i in range(2 * ITERS)]
                total = tree(terms)
                cols = pl.ds(8 + 8 * xb, 8)
                y = cmul((m[0, REACH + z, cols, :], m[1, REACH + z, cols, :]), total)
                rows = pl.ds(8 * xb, 8)
                x[f, z, rows, :] = y[0]
                x[f + 1, z, rows, :] = y[1]
            return 0

        lax.fori_loop(0, 3 * NZL, block, 0)

    for xb in range(CX // 8):
        rows = pl.ds(8 * xb, 8)
        for v, value in enumerate(impedance(x, 0, rows)):
            surface[v * CX + 8 * xb : v * CX + 8 * xb + 8, :] = value
    mine = pltpu.roll(got[:, NY : 2 * NY], lax.rem(NY - 32 * tile[0], NY), 1).astype(jnp.int32)
    group = lax.broadcasted_iota(jnp.int32, (32, NY), 1) // 32
    cells = mine[0:32, :]
    for e in range(1, 4):
        cells = jnp.where(group == e, pltpu.roll(mine[32 * e : 32 * e + 32, :], 32 * e, 1), cells)
    col = cells % NY
    line = cells // NY
    cols = [col[8 * i : 8 * i + 8, :] for i in range(4)]
    lines = [line[8 * i : 8 * i + 8, :] for i in range(4)]

    def value(v, _):
        acc = [jnp.zeros((8, NY), f32)] * 4
        for r in range(CX):
            src = jnp.broadcast_to(surface[pl.ds(v * CX + r, 1), :], (8, NY))
            for i in range(4):
                hit = jnp.take_along_axis(src, cols[i], axis=1, mode="promise_in_bounds")
                acc[i] = jnp.where(lines[i] == r, hit, acc[i])
        for i in range(4):
            picked[pl.ds(pl.multiple_of(v * 32, 32) + 8 * i, 8), :] = acc[i]
        return 0

    lax.fori_loop(0, 8, value, 0)
    for e in range(4):
        for h in range(2):
            out = None
            for w in range(4):
                v = 4 * h + w
                part = picked[v * 32 : v * 32 + 32, :]
                if w != e:
                    part = pltpu.roll(part, (32 * (w - e)) % NY, 1)
                out = part if out is None else jnp.where(group == w, part, out)
            send[32 * e : 32 * e + 32, NY * h : NY * h + NY] = out


def hazard_rows(got, spectra, scenario, out):
    scen = scenario.shape[1]
    turned = []
    for h in range(2):
        block = got[0:8, NY * h : NY * h + NY]
        turned.append(jnp.transpose(jnp.concatenate([block, jnp.zeros((NY - 8, NY), f32)], axis=0)))
    b = [spectra[i : i + 1, :] for i in range(4)]
    bx, by = (b[0], b[1]), (b[2], b[3])
    for j in range(4):
        weight = jnp.where(scenario[...] == j, 1.0, 0.25)
        for qb in range(4):
            z = []
            for v in range(8):
                first = (v % 4) * 32 + 8 * qb
                z.append(jnp.broadcast_to(turned[v // 4][first : first + 8, j : j + 1], (8, scen)))
            gx = cadd(cmul((z[0], z[1]), bx), cmul((z[2], z[3]), by))
            gy = cadd(cmul((z[4], z[5]), bx), cmul((z[6], z[7]), by))
            power = gx[0] * gx[0] + gx[1] * gx[1] + gy[0] * gy[0] + gy[1] * gy[1]
            row = 32 * j + 8 * qb
            out[row : row + 8, :] = weight * power


def neighbours(count):
    up = [(i, i + 1) for i in range(count - 1)]
    return up, [(j, i) for i, j in up]


def per_device(right_side, conductance, owned_cells, spectra, scenario_tile):
    up_z, down_z = neighbours(lax.axis_size("gz"))
    up_x, down_x = neighbours(lax.axis_size("gx"))
    block = (NF, NZL, CX, NY)
    slab = (NF, EZ, WX, NY)
    r = right_side.reshape(block)
    k = conductance
    side = ((NF + 1) * NZL * SIDE, NY)
    to_up, to_down = call(pack_x, [(side, f32)] * 2, n_in=2, moved=1 << 21)(r, k)
    left = lax.ppermute(to_up, "gx", up_x)
    right = lax.ppermute(to_down, "gx", down_x)
    deep = ((NF + 1) * REACH * (CX + 2 * SIDE), NY)
    to_up, to_down = call(pack_z, [(deep, f32)] * 2, n_in=4, moved=1 << 22)(r, k, left, right)
    below = lax.ppermute(to_up, "gz", up_z)
    above = lax.ppermute(to_down, "gz", down_z)
    wide = (NF, NZL, WX, NY)
    back = (NF, REACH, BACK, NY)
    space = pltpu.VMEM(slab, f32)
    b1, b2, b3w, m, to_up, to_down = call(
        first_half,
        [(block, f32), (block, f32), (wide, f32), ((2, EZ, WX, NY), f32), (back, f32), (back, f32)],
        [space] * 4 + [pltpu.VMEM((EZ, WX, NY), f32)],
        n_in=6,
        flops=1 << 25,
        moved=1 << 23,
    )(r, k, left, right, below, above)
    below = lax.ppermute(to_up, "gz", up_z)
    above = lax.ppermute(to_down, "gz", down_z)
    (part,) = call(low_gram, [((NY, NY), f32)], n_in=4, flops=1 << 24, moved=1 << 22)(r, b1, b2, b3w)
    b4, b5, send = call(
        second_half,
        [(block, f32), (block, f32), ((128, 2 * NY), f32)],
        [space] * 5 + [pltpu.VMEM((NY, NY), f32)],
        n_in=9,
        flops=1 << 25,
        moved=1 << 23,
    )(r, b1, b2, b3w, m, below, above, part, owned_cells[0])
    got = lax.all_to_all(send, ("gz", "gx"), 0, 0, tiled=True)
    tile = lax.axis_index("gx").astype(jnp.int32).reshape(1)
    x, send = pl.pallas_call(
        finish,
        out_shape=[jax.ShapeDtypeStruct(block, f32), jax.ShapeDtypeStruct((128, 2 * NY), f32)],
        in_specs=[pl.BlockSpec(memory_space=pltpu.SMEM)] + [VM] * 8,
        out_specs=[VM] * 2,
        scratch_shapes=[pltpu.VMEM((8 * CX, NY), f32)] * 2,
        compiler_params=pltpu.CompilerParams(vmem_limit_bytes=LIMIT),
    )(tile, got, r, b1, b2, b3w, b4, b5, m)
    got = lax.all_to_all(send, ("gz", "gx"), 0, 0, tiled=True)
    scen = spectra.shape[0]
    (hazard,) = call(hazard_rows, [((128, scen), f32)], n_in=3)(got, spectra.T, scenario_tile.reshape(1, scen))
    return x.reshape(right_side.shape), hazard


def solution(mesh):
    return jax.shard_map(
        per_device,
        mesh=mesh,
        in_specs=(
            P(None, None, None, "gz", "gx", None),
            P("gz", "gx", None),
            P(("gz", "gx"), None, None),
            P(),
            P(),
        ),
        out_specs=(P(None, None, None, "gz", "gx", None), P(("gz", "gx"), None)),
        check_vma=False,
    )
```

time: 1050 us -> 134 us (0.13)
  blocking collectives: 552 us -> 13.9 us
  waiting for transfers between devices: 319 us -> 46.3 us
  other arithmetic: 55.8 us -> 0 us
  starting transfers between devices: 68.3 us -> 30.8 us
  Pallas kernels: 0 us -> 30.2 us
  local copies, waits for them, and re-layouts: 28.6 us -> 11.1 us
  between operations: 15.8 us -> 0.8 us
    psum x8 -> x0, blocking collectives: 529 us -> none  [the longest x3 201 us: per_device(): lax.psum((bm_real, bm_imag, bent_local), ('gz', 'gx'))]
    psum x1 -> x0, waiting for transfers between devices: 260 us -> none  [from_root(): return lax.psum(block, axis)]
    ppermute x24 -> x6, starting transfers between devices: 68.2 us -> 17 us  [the longest x2 6.44 us: per_device(): below = lax.ppermute(to_up, 'gz', up_z)]
    pallas_call x0 -> x7, Pallas kernels: none -> 30.2 us  [the longest x1 11.7 us: per_device(): call(second_half, [(block, f32), (block, f32), ((128, 2 * NY), f32)], [sp...]
    sub x29 -> x0, other arithmetic: 23.4 us -> none  [the longest x8 13.1 us: cscale(): real_part = s_real * field[:, :, 0] - s_imag * field[:, :, 1]]
    all_gather x1 -> x0, blocking collectives: 22.9 us -> none  [per_device(): whole = lax.all_gather(tile, 'gx', axis=1, tiled=True)]
    ppermute x24 -> x6, waiting for transfers between devices: 58.7 us -> 36.6 us  [the longest x2 22.1 us: per_device(): below = lax.ppermute(to_up, 'gz', up_z)]
    all_to_all x0 -> x1, blocking collectives: none -> 13.9 us  [per_device(): got = lax.all_to_all(send, ('gz', 'gx'), 0, 0, tiled=True)]
  transfers between devices with their start and end apart: 25 -> 7, of which waited for: 19 -> 7; matrix products, arithmetic and copies ran while one was open for 1% -> 0% of each run, Pallas kernels for 0% -> 1%
where the time goes in v1:
time: 134 us; the launch traced here: 133 us
  waiting for transfers between devices  46.3 us (35%)
  starting transfers between devices  30.8 us (23%)
  Pallas kernels  30.2 us (23%)
  blocking collectives  13.9 us (10%)
  local copies, waits for them, and re-layouts  11.1 us (8%)
    ppermute x2, waiting for transfers between devices, per_device(): below = lax.ppermute(to_up, 'gz', up_z)  22.1 us
    all_to_all x1, blocking collectives, per_device(): got = lax.all_to_all(send, ('gz', 'gx'), 0, 0, tiled=True)  13.9 us
    all_to_all x1, starting transfers between devices, per_device(): got = lax.all_to_all(send, ('gz', 'gx'), 0, 0, tiled=True)  13.8 us
    pallas_call x1, Pallas kernels, per_device(): call(second_half, [(block, f32), (block, f32), ((128, 2 * NY), f32)], [sp...  11.7 us
    pallas_call x1, Pallas kernels, per_device(): call(first_half, [(block, f32), (block, f32), (wide, f32), ((2, EZ, WX, N...  10.6 us
    unnamed x32, local copies, waits for them, and re-layouts  10.2 us
    all_to_all x1, waiting for transfers between devices, per_device(): got = lax.all_to_all(send, ('gz', 'gx'), 0, 0, tiled=True)  9.71 us
    ppermute x2, waiting for transfers between devices, per_device(): above = lax.ppermute(to_down, 'gz', down_z)  8.3 us
  transfers between devices with their start and end apart: 7, of which 7 were waited for; matrix products, arithmetic and copies ran while one was open for 0% of the time, Pallas kernels for 1%

profile of v1, /device:TPU:1, one launch (start us, length us, event | category | flops | bytes accessed | tf_op | source)
XLA Modules:
  0.0 133.1 jit_solution(2736302231752163069)
XLA Ops:
  0.6 1.1 copy-done
  1.8 0.8 copy-done.10
  2.6 6.0 %collective-permute-start = (f32[312,128]{1,0:T(8,128)S(1)}, f32[312,128]{1,0:T(8,128)S(1)}, u32[]{:S(2)}, u32[]{:S(2)}) collective-permute-start(f32[312,128]{1,0:T(8,128)S(1)} %get-tuple-element.17), channel_id=1, source_target_pairs={{0,1},{1,2},{2,3},{4,5},{5,6},{6,7},{8,9},{9,10},{10,11},{12,13},{... | collective-permute-start | bytes 479240 | tf_op jit(solution)/shard_map/ppermute | solution.py:508
  8.7 1.9 %collective-permute-start.1 = (f32[312,128]{1,0:T(8,128)S(1)}, f32[312,128]{1,0:T(8,128)S(1)}, u32[]{:S(2)}, u32[]{:S(2)}) collective-permute-start(f32[312,128]{1,0:T(8,128)S(1)} %get-tuple-element.18), channel_id=1, source_target_pairs={{1,0},{2,1},{3,2},{5,4},{6,5},{7,6},{9,8},{10,9},{11,10},{13,12},{... | collective-permute-start | bytes 479240 | tf_op jit(solution)/shard_map/ppermute | solution.py:509
  10.6 0.3 collective-permute-done.left
  10.9 5.9 %collective-permute-done.1.right = f32[312,128]{1,0:T(8,128)S(1)} collective-permute-done((f32[312,128]{1,0:T(8,128)S(1)}, f32[312,128]{1,0:T(8,128)S(1)}, u32[]{:S(2)}, u32[]{:S(2)}) %collective-permute-start.1) | collective-permute-done | bytes 159776 | tf_op jit(solution)/shard_map/ppermute | solution.py:509
  16.9 3.3 %collective-permute-start.2 = (f32[1716,128]{1,0:T(8,128)S(1)}, f32[1716,128]{1,0:T(8,128)S(1)}, u32[]{:S(2)}, u32[]{:S(2)}) collective-permute-start(f32[1716,128]{1,0:T(8,128)S(1)} %get-tuple-element.19), channel_id=1, source_target_pairs={{0,4},{4,8},{8,12},{12,16},{16,20},{20,24},{24,28},{28,32},{32,36}... | collective-permute-start | bytes 2635784 | tf_op jit(solution)/shard_map/ppermute | solution.py:512
  20.2 1.3 collective-permute-start.3
  21.5 13.7 %collective-permute-done.2.below = f32[1716,128]{1,0:T(8,128)S(1)} collective-permute-done((f32[1716,128]{1,0:T(8,128)S(1)}, f32[1716,128]{1,0:T(8,128)S(1)}, u32[]{:S(2)}, u32[]{:S(2)}) %collective-permute-start.2) | collective-permute-done | bytes 878624 | tf_op jit(solution)/shard_map/ppermute | solution.py:512
  35.2 4.2 %collective-permute-done.3.above = f32[1716,128]{1,0:T(8,128)S(1)} collective-permute-done((f32[1716,128]{1,0:T(8,128)S(1)}, f32[1716,128]{1,0:T(8,128)S(1)}, u32[]{:S(2)}, u32[]{:S(2)}) %collective-permute-start.3) | collective-permute-done | bytes 878624 | tf_op jit(solution)/shard_map/ppermute | solution.py:513
  39.3 0.9 copy-done.14
  40.2 10.6 %shard_map.70 = (f32[12,4,32,128]{3,2,1,0:T(8,128)S(1)}, f32[12,4,32,128]{3,2,1,0:T(8,128)S(1)}, f32[12,4,48,128]{3,2,1,0:T(8,128)}, f32[2,10,48,128]{3,2,1,0:T(...) custom-call(f32[12,4,32,128]{3,2,1,0:T(8,128)S(1)} %bitcast.16, f32[4,32,128]{2,1,0:T(8,128)S(1)} %copy-done.10, ...), custom_call_target="tpu_custom_call" | custom-call | flops 33554432 | bytes 8388608 | tf_op jit(solution)/shard_map/pallas_call | solution.py:517
  50.8 3.2 %collective-permute-start.4 = (f32[12,3,40,128]{3,2,1,0:T(8,128)S(1)}, f32[12,3,40,128]{3,2,1,0:T(8,128)S(1)}, u32[]{:S(2)}, u32[]{:S(2)}) collective-permute-start(f32[12,3,40,128]{3,2,1,0:T(8,128)S(1)} %get-tuple-element.25), channel_id=1, source_target_pairs={{0,4},{4,8},{8,12},{12,16},{16,20},{20,24},{24,28},{28,32},{32,36}... | collective-permute-start | bytes 2211848 | tf_op jit(solution)/shard_map/ppermute | solution.py:525
  54.0 1.3 collective-permute-start.5
  55.3 1.3 copy-done.2
  56.6 1.2 shard_map.71.part
  57.8 8.4 %collective-permute-done.4.below = f32[12,3,40,128]{3,2,1,0:T(8,128)S(1)} collective-permute-done((f32[12,3,40,128]{3,2,1,0:T(8,128)S(1)}, f32[12,3,40,128]{3,2,1,0:T(8,128)S(1)}, u32[]{:S(2)}, u32[]{:S(2)}) %collective-permute-start.4) | collective-permute-done | bytes 737312 | tf_op jit(solution)/shard_map/ppermute | solution.py:525
  66.2 4.1 %collective-permute-done.5.above = f32[12,3,40,128]{3,2,1,0:T(8,128)S(1)} collective-permute-done((f32[12,3,40,128]{3,2,1,0:T(8,128)S(1)}, f32[12,3,40,128]{3,2,1,0:T(8,128)S(1)}, u32[]{:S(2)}, u32[]{:S(2)}) %collective-permute-start.5) | collective-permute-done | bytes 737312 | tf_op jit(solution)/shard_map/ppermute | solution.py:526
  70.3 11.7 %shard_map.72 = (f32[12,4,32,128]{3,2,1,0:T(8,128)S(1)}, f32[12,4,32,128]{3,2,1,0:T(8,128)S(1)}, f32[128,256]{1,0:T(8,128)S(1)}) custom-call(f32[12,4,32,128]{3,2,1,0:T(8,128)S(1)} %bitcast.18, f32[12,4,32,128]{3,2,1,0:T(8,128)S(1)} %get-tuple-element.21.b1, f32[12,4,32,128]{3,2,1,0:T(8,128)S(1)} %get-tuple-element.22.b2, ...), custom_call_target="tpu_custom_call" | custom-call | flops 33554432 | bytes 8388608 | tf_op jit(solution)/shard_map/pallas_call | solution.py:528
  82.0 0.9 copy-done.6
  82.9 0.9 copy-done.8
  83.8 0.8 copy.7
  84.6 13.8 %all-to-all-start = ((f32[128,1,256]{2,1,0:T(1,128)}), f32[128,1,256]{2,1,0:T(1,128)}, u32[]{:S(2)}, u32[]{:S(2)}) async-start(f32[128,1,256]{2,1,0:T(1,128)} %copy.7), calls=%async_computation | async-start | bytes 262144 | tf_op jit(solution)/shard_map/all_to_all | solution.py:536
  98.4 9.7 %all-to-all-done = f32[128,1,256]{2,1,0:T(1,128)} async-done(((f32[128,1,256]{2,1,0:T(1,128)}), f32[128,1,256]{2,1,0:T(1,128)}, u32[]{:S(2)}, u32[]{:S(2)}) %all-to-all-start) | async-done | bytes 131104 | tf_op jit(solution)/shard_map/all_to_all | solution.py:536
  108.2 0.9 copy.14
  109.1 1.0 copy-done.5
  110.1 1.1 copy-done.7
  111.3 1.1 copy-done.9
  112.4 5.4 %shard_map.73 = (f32[12,4,32,128]{3,2,1,0:T(8,128)}, f32[128,256]{1,0:T(8,128)S(1)}) custom-call(s32[1]{0:T(128)} %bitcast.tile, f32[128,256]{1,0:T(8,128)S(1)} %bitcast.20, f32[12,4,32,128]{3,2,1,0:T(8,128)S(1)} %bitcast.19, f32[12,4,32,128]{3,2,1,0:T(8,128)S(1)} %get-tuple-element.21.b1, f32[12,4,32,128]{3,2,1,0:T(8,128)S(1)} %get-tuple-element.22.b2, ...), custom_call_target="tpu_custom_call" | custom-call | tf_op jit(solution)/shard_map/pallas_call | solution.py:538
  117.8 0.1 copy.8
  117.9 13.9 %all_to_all.22 = f32[128,1,256]{2,1,0:T(1,128)S(1)} all-to-all(f32[128,1,256]{2,1,0:T(1,128)S(1)} %copy.8), channel_id=1, replica_groups=mesh['gz'=32,'gx'=4] {'gz','gx'}, dimensions={0} | all-to-all | bytes 262144 | tf_op jit(solution)/shard_map/all_to_all | solution.py:546
  131.9 1.2 shard_map.74
  (24 shorter events, 0.2 us)
Async XLA Ops:
  0.6 1.1 copy-start
  1.8 0.8 copy-start.10
  2.6 8.2 %collective-permute-start = (f32[312,128]{1,0:T(8,128)S(1)}, f32[312,128]{1,0:T(8,128)S(1)}, u32[]{:S(2)}, u32[]{:S(2)}) collective-permute-start(f32[312,128]{1,0:T(8,128)S(1)} %get-tuple-element.17), channel_id=1, source_target_pairs={{0,1},{1,2},{2,3},{4,5},{5,6},{6,7},{8,9},{9,10},{10,11},{12,13},{... | collective-permute-start | bytes 479240 | tf_op jit(solution)/shard_map/ppermute | solution.py:508
  8.7 8.1 %collective-permute-start.1 = (f32[312,128]{1,0:T(8,128)S(1)}, f32[312,128]{1,0:T(8,128)S(1)}, u32[]{:S(2)}, u32[]{:S(2)}) collective-permute-start(f32[312,128]{1,0:T(8,128)S(1)} %get-tuple-element.18), channel_id=1, source_target_pairs={{1,0},{2,1},{3,2},{5,4},{6,5},{7,6},{9,8},{10,9},{11,10},{13,12},{... | collective-permute-start | bytes 479240 | tf_op jit(solution)/shard_map/ppermute | solution.py:509
  16.9 18.2 %collective-permute-start.2 = (f32[1716,128]{1,0:T(8,128)S(1)}, f32[1716,128]{1,0:T(8,128)S(1)}, u32[]{:S(2)}, u32[]{:S(2)}) collective-permute-start(f32[1716,128]{1,0:T(8,128)S(1)} %get-tuple-element.19), channel_id=1, source_target_pairs={{0,4},{4,8},{8,12},{12,16},{16,20},{20,24},{24,28},{28,32},{32,36}... | collective-permute-start | bytes 2635784 | tf_op jit(solution)/shard_map/ppermute | solution.py:512
  20.2 19.1 %collective-permute-start.3 = (f32[1716,128]{1,0:T(8,128)S(1)}, f32[1716,128]{1,0:T(8,128)S(1)}, u32[]{:S(2)}, u32[]{:S(2)}) collective-permute-start(f32[1716,128]{1,0:T(8,128)S(1)} %get-tuple-element.20), channel_id=1, source_target_pairs={{4,0},{8,4},{12,8},{16,12},{20,16},{24,20},{28,24},{32,28},{36,32}... | collective-permute-start | bytes 2635784 | tf_op jit(solution)/shard_map/ppermute | solution.py:513
  39.3 0.9 copy-start.14
  50.8 19.5 %copy-start.4 = (f32[2,10,48,128]{3,2,1,0:T(8,128)}, f32[2,10,48,128]{3,2,1,0:T(8,128)S(1)}, u32[]{:S(2)}) copy-start(f32[2,10,48,128]{3,2,1,0:T(8,128)S(1)} %get-tuple-element.24.m) | copy-start | bytes 1474564
  50.8 15.4 %collective-permute-start.4 = (f32[12,3,40,128]{3,2,1,0:T(8,128)S(1)}, f32[12,3,40,128]{3,2,1,0:T(8,128)S(1)}, u32[]{:S(2)}, u32[]{:S(2)}) collective-permute-start(f32[12,3,40,128]{3,2,1,0:T(8,128)S(1)} %get-tuple-element.25), channel_id=1, source_target_pairs={{0,4},{4,8},{8,12},{12,16},{16,20},{20,24},{24,28},{28,32},{32,36}... | collective-permute-start | bytes 2211848 | tf_op jit(solution)/shard_map/ppermute | solution.py:525
  54.0 16.4 %collective-permute-start.5 = (f32[12,3,40,128]{3,2,1,0:T(8,128)S(1)}, f32[12,3,40,128]{3,2,1,0:T(8,128)S(1)}, u32[]{:S(2)}, u32[]{:S(2)}) collective-permute-start(f32[12,3,40,128]{3,2,1,0:T(8,128)S(1)} %get-tuple-element.26), channel_id=1, source_target_pairs={{4,0},{8,4},{12,8},{16,12},{20,16},{24,20},{28,24},{32,28},{36,32}... | collective-permute-start | bytes 2211848 | tf_op jit(solution)/shard_map/ppermute | solution.py:526
  55.3 1.3 copy-start.2
  56.6 13.8 %copy-start.12 = (s32[1,4,32]{2,1,0:T(4,128)S(1)}, s32[1,4,32]{2,1,0:T(4,128)}, u32[]{:S(2)}) copy-start(s32[1,4,32]{2,1,0:T(4,128)} %param.7) | copy-start | bytes 1540
  70.3 38.7 %copy-start.3 = (f32[12,4,48,128]{3,2,1,0:T(8,128)S(1)}, f32[12,4,48,128]{3,2,1,0:T(8,128)}, u32[]{:S(2)}) copy-start(f32[12,4,48,128]{3,2,1,0:T(8,128)} %get-tuple-element.23.b3w) | copy-start | bytes 3538948
  82.0 0.9 copy-start.6
  82.9 0.9 copy-start.8
  83.8 25.3 %copy-start.1 = (f32[2,3,2,4,32,128]{5,4,3,2,1,0:T(8,128)S(1)}, f32[2,3,2,4,32,128]{5,4,3,2,1,0:T(8,128)}, u32[]{:S(2)}) copy-start(f32[2,3,2,4,32,128]{5,4,3,2,1,0:T(8,128)} %param.5) | copy-start | bytes 2359300
  84.6 23.6 %all-to-all-start = ((f32[128,1,256]{2,1,0:T(1,128)}), f32[128,1,256]{2,1,0:T(1,128)}, u32[]{:S(2)}, u32[]{:S(2)}) async-start(f32[128,1,256]{2,1,0:T(1,128)} %copy.7), calls=%async_computation | async-start | bytes 262144 | tf_op jit(solution)/shard_map/all_to_all | solution.py:536
  109.1 1.0 copy-start.5
  110.1 1.1 copy-start.7
  111.3 1.1 copy-start.9
  112.4 19.5 %copy-start.11 = (f32[512,4]{0,1:T(4,128)S(1)}, f32[512,4]{0,1:T(4,128)}, u32[]{:S(2)}) copy-start(f32[512,4]{0,1:T(4,128)} %param.8) | copy-start | bytes 24580
  112.4 19.5 %copy-start.13 = (s32[512]{0:T(512)S(1)}, s32[512]{0:T(512)}, u32[]{:S(2)}) copy-start(s32[512]{0:T(512)} %param.9) | copy-start | bytes 6148

commit v2 on v1

v2 whole, which is shorter than its diff:
```python
import jax
import jax.numpy as jnp
from jax import lax
from jax.experimental import pallas as pl
from jax.experimental.pallas import tpu as pltpu
from jax.sharding import PartitionSpec as P

SHIFTS = (1.8, 0.6, 1.8, 0.6, 1.8, 0.6)
SCALE = 1.0
ITERS = 3
REACH = 3
SIDE = 2 * REACH
NF = 6
CX, NZL, NY = 32, 4, 128
WX = 48
EZ = NZL + 2 * REACH
BACK = CX + 2 * REACH
f32 = jnp.float32
VM = pl.BlockSpec(memory_space=pltpu.VMEM)
LIMIT = 14 * 1024 * 1024


HBM = pl.BlockSpec(memory_space=pltpu.HBM)


def call(body, ins, outs, scratch=(), flops=0, moved=0):
    return pl.pallas_call(
        body,
        out_shape=[jax.ShapeDtypeStruct(shape, f32) for shape, _ in outs],
        in_specs=ins,
        out_specs=[spec for _, spec in outs],
        scratch_shapes=list(scratch),
        compiler_params=pltpu.CompilerParams(vmem_limit_bytes=LIMIT),
        cost_estimate=pl.CostEstimate(flops=flops, bytes_accessed=moved, transcendentals=0),
    )


def odd(axis):
    return lax.rem(lax.axis_index(axis), 2) == 1


def either(flag, body, first, second):
    @pl.when(jnp.logical_not(flag))
    def _():
        body(first, second)

    @pl.when(flag)
    def _():
        body(second, first)


def start_all(pairs, sem, first=0):
    copies = [pltpu.make_async_copy(src, dst, sem.at[first + i]) for i, (src, dst) in enumerate(pairs)]
    for copy in copies:
        copy.start()
    return copies


def wait_all(copies):
    for copy in copies:
        copy.wait()


def pack_x(r, k, to_a, to_b, rim, rim_k, sem):
    pairs = []
    for i in range(2):
        src = pl.ds(i * (CX - 8), 8)
        pairs.append((r.at[:, :, src, :], rim.at[:, :, pl.ds(8 * i, 8), :]))
        pairs.append((k.at[:, src, :], rim_k.at[:, pl.ds(8 * i, 8), :]))
    wait_all(start_all(pairs, sem))

    def fill(up, down):
        for f in range(2 * NF + 1):
            for z in range(NZL):
                row = (f * NZL + z) * SIDE
                src = rim_k.at[z] if f == 2 * NF else rim.at[f, z]
                up[row : row + SIDE, :] = src[16 - SIDE : 16, :]
                down[row : row + SIDE, :] = src[0:SIDE, :]

    either(odd("gx"), fill, to_a, to_b)


def sides(from_a, from_b, near):
    a, b = from_a[near : near + SIDE, :], from_b[near : near + SIDE, :]
    flag = odd("gx")
    return jnp.where(flag, a, b), jnp.where(flag, b, a)


def pack_z(r, k, xa, xb, a_0, b_0, a_1, b_1):
    width = CX + 2 * SIDE

    def fill(first, second):
        outs = [((first[p], NZL - REACH), (second[p], 0)) for p in range(2)]
        for p in range(2):
            fields = [p * NF + i for i in range(NF)] + ([2 * NF] if p == 0 else [])
            for at, f in enumerate(fields):
                for z in range(NZL):
                    left, right = sides(xa, xb, (f * NZL + z) * SIDE)
                    src = k.at[z] if f == 2 * NF else r.at[f, z]
                    for out, low in outs[p]:
                        if low <= z < low + REACH:
                            row = (at * REACH + z - low) * width
                            out[row : row + SIDE, :] = left
                            out[row + SIDE : row + SIDE + CX, :] = src[:, :]
                            out[row + SIDE + CX : row + width, :] = right

    either(odd("gz"), fill, (a_0, a_1), (b_0, b_1))


def lanes():
    lane = lax.broadcasted_iota(jnp.int32, (WX, NY), 1)
    return lane == 0, lane == NY - 1


def next_y(a, last):
    return jnp.where(last, 0.0, pltpu.roll(a, NY - 1, 1))


def next_x(a):
    return pltpu.roll(a, WX - 1, 0)


def prev_x(a):
    return pltpu.roll(a, 1, 0)


def h_flat(y, base, z, last):
    ex, ey, ez = y[base, z], y[base + 2, z], y[base + 4, z]
    hx = next_y(ez, last) - ez - (y[base + 2, z + 1] - ey)
    hy = y[base, z + 1] - ex - (next_x(ez) - ez)
    return hx, hy


def smooth(b, y, m, base, z):
    mr, mi = m[0, z], m[1, z]
    for c in range(3):
        re, im = b[base + 2 * c, z], b[base + 2 * c + 1, z]
        y[base + 2 * c, z] = mr * re - mi * im
        y[base + 2 * c + 1, z] = mr * im + mi * re


def apply_k(b, y, bn, yn, m, lo, hi, shift, want_y):
    first, last = lanes()
    own = (1.0 - shift) / SCALE
    inv = 1.0 / SCALE

    def layer(z, prev):
        out = []
        for e in range(2):
            hxp, hyp = prev[e]
            ex, ey, ez = y[e, z], y[e + 2, z], y[e + 4, z]
            hx, hy = h_flat(y, e, z, last)
            hz = next_x(ey) - ey - (next_y(ex, last) - ex)
            cx = hz - jnp.where(first, -ex, pltpu.roll(hz, 1, 1)) - (hy - hyp)
            cy = hx - hxp - (hz - prev_x(hz))
            cz = hy - prev_x(hy) - (hx - jnp.where(first, ez, pltpu.roll(hx, 1, 1)))
            for c, (cur, old) in enumerate(((cx, ex), (cy, ey), (cz, ez))):
                new = cur - 4.0 * old
                if inv != 1.0:
                    new = new * inv
                bn[e + 2 * c, z] = new + own * b[e + 2 * c, z]
            out.append((hx, hy))
        if want_y:
            smooth(bn, yn, m, 0, z)
        return tuple(out)

    lax.fori_loop(lo, hi, layer, tuple(h_flat(y, e, lo - 1, last) for e in range(2)))


def all_smooth(b, y, m):
    def layer(z, _):
        smooth(b, y, m, 0, z)
        return 0

    lax.fori_loop(0, EZ, layer, 0)


def weights(k, xa, xb, za, zb, m, kx):
    extend([kx], [k], xa, xb, za, zb, 2 * NF, NF)

    def layer(z, _):
        kz = kx[z]
        inv = jnp.where(kz > 0.0, 1.0, 0.0) / (16.0 + kz * kz)
        m[0, z] = 4.0 * inv
        m[1, z] = -kz * inv
        return 0

    lax.fori_loop(0, EZ, layer, 0)


def extend(outs, srcs, xa, xb, za, zb, near, far):
    width = CX + 2 * SIDE
    x0 = 8 - SIDE
    zero = jnp.zeros((EZ, 8, NY), f32)
    for i, (dst, src) in enumerate(zip(outs, srcs)):
        dst[:, 0:8, :] = zero
        dst[:, WX - 8 : WX, :] = zero
        for z in range(NZL):
            left, right = sides(xa, xb, ((near + i) * NZL + z) * SIDE)
            dst[REACH + z, x0:8, :] = left
            dst[REACH + z, 8 : 8 + CX, :] = src[z]
            dst[REACH + z, 8 + CX : 8 + CX + SIDE, :] = right

    def fill(above, below):
        for i, dst in enumerate(outs):
            for z in range(REACH):
                row = ((far + i) * REACH + z) * width
                dst[z, x0 : x0 + width, :] = below[row : row + width, :]
                dst[REACH + NZL + z, x0 : x0 + width, :] = above[row : row + width, :]

    either(odd("gz"), fill, za, zb)


def keep(src, out):
    def field(f, _):
        out[f] = src[f, REACH : REACH + NZL, 8 : 8 + CX, :]
        return 0

    lax.fori_loop(0, NF, field, 0)


def first_steps(p, r, xa, xb, za, zb, b1, b2, b3w, to_a, to_b, b1_far, b2_far, m, ba, bb, ya, yb, sem):
    fields = range(NF)
    extend([ba.at[f] for f in fields], [r.at[p * NF + f] for f in fields], xa, xb, za, zb, p * NF, 0)
    all_smooth(ba, ya, m)
    apply_k(ba, ya, bb, yb, m, 1, EZ - 1, SHIFTS[0], True)
    keep(bb, b1)
    copies = start_all([(b1, b1_far)], sem)
    apply_k(bb, yb, ba, ya, m, 2, EZ - 2, SHIFTS[1], True)
    keep(ba, b2)
    copies += start_all([(b2, b2_far)], sem, 1)
    apply_k(ba, ya, bb, yb, m, 3, EZ - 3, SHIFTS[2], False)
    cut = (WX - BACK) // 2
    for f in fields:
        b3w[f] = bb[f, REACH : REACH + NZL]

    def fill(up, down):
        for f in fields:
            for z in range(REACH):
                row = (f * REACH + z) * BACK
                up[row : row + BACK, :] = bb[f, NZL + z, cut : cut + BACK, :]
                down[row : row + BACK, :] = bb[f, REACH + z, cut : cut + BACK, :]

    either(odd("gz"), fill, to_a, to_b)
    wait_all(copies)


def first_half_0(r, k, xa, xb, za, zb, b1, b2, b3w, to_a, to_b, b1_far, b2_far, m, ba, bb, ya, yb, sem, kx):
    weights(k, xa, xb, za, zb, m, kx)
    first_steps(0, r, xa, xb, za, zb, b1, b2, b3w, to_a, to_b, b1_far, b2_far, m, ba, bb, ya, yb, sem)


def first_half_1(r, m, xa, xb, za, zb, b1, b2, b3w, to_a, to_b, b1_far, b2_far, ba, bb, ya, yb, sem):
    first_steps(1, r, xa, xb, za, zb, b1, b2, b3w, to_a, to_b, b1_far, b2_far, m, ba, bb, ya, yb, sem)


PAIRS = [(i, j) for i in range(7) for j in range(i, 7)]
LOW = [pair for pair in PAIRS if pair[1] <= REACH]
HIGH = [pair for pair in PAIRS if pair[1] > REACH]
SLOT = {}
for _pair in LOW + HIGH:
    SLOT[_pair] = sum(1 if a == b else 2 for a, b in SLOT)


def gram(read, pairs, out):
    used = sorted({i for pair in pairs for i in pair})
    count = sum(1 if i == j else 2 for i, j in pairs)

    def block(step, acc):
        c, z = step // NZL, step % NZL
        acc = list(acc)
        for xb in range(CX // 8):
            vec = {i: (read(i, 2 * c, z, xb), read(i, 2 * c + 1, z, xb)) for i in used}
            at = 0
            for i, j in pairs:
                (ar, ai), (br, bi) = vec[i], vec[j]
                acc[at] = acc[at] + (ar * br + ai * bi)
                at += 1
                if i != j:
                    acc[at] = acc[at] + (ar * bi - ai * br)
                    at += 1
        return tuple(acc)

    acc = lax.fori_loop(0, 3 * NZL, block, (jnp.zeros((8, NY), f32),) * count)
    at = 0
    for i, j in pairs:
        for part in range(1 if i == j else 2):
            row = SLOT[i, j] + part
            out[row : row + 1, :] = jnp.sum(acc[at], axis=0, keepdims=True)
            at += 1


def low_gram(b0, b1_0, b2_0, b3w_0, b1_1, b2_1, b3w_1, part_0, part_1):
    for p, (b1, b2, b3w, part) in enumerate(((b1_0, b2_0, b3w_0, part_0), (b1_1, b2_1, b3w_1, part_1))):
        part[...] = jnp.zeros((64, NY), f32)
        gram(reader(p, b0, b1, b2, b3w), LOW, part)


def reader(p, b0, b1, b2, b3w, *slabs):
    def read(i, f, z, xb):
        if i == 0:
            return b0[p * NF + f, z, pl.ds(8 * xb, 8), :]
        if i < 3:
            return (b1, b2)[i - 1][f, z, pl.ds(8 * xb, 8), :]
        if i == 3:
            return b3w[f, z, pl.ds(8 + 8 * xb, 8), :]
        return slabs[i - 4][f, REACH + z, pl.ds(8 + 8 * xb, 8), :]

    return read


def second_steps(p, b0, b1, b2, b3w, m, za, zb, part, b3_far, b4_far, b5_far, total, ba, bb, bc, bd, ya, yb, sem):
    cut = (WX - BACK) // 2
    own = pl.ds(REACH, NZL)
    mid = pl.ds(8, CX)
    copies = start_all([(b3w.at[:, :, mid, :], b3_far)], sem)
    zero = jnp.zeros((REACH, 8, NY), f32)
    for f in range(NF):
        for first in (0, REACH + NZL):
            ba[f, first : first + REACH, 0:8, :] = zero
            ba[f, first : first + REACH, WX - 8 : WX, :] = zero
        ba[f, REACH : REACH + NZL] = b3w[f]

    def fill(above, below):
        for f in range(NF):
            for z in range(REACH):
                row = (f * REACH + z) * BACK
                ba[f, z, cut : cut + BACK, :] = below[row : row + BACK, :]
                ba[f, REACH + NZL + z, cut : cut + BACK, :] = above[row : row + BACK, :]

    either(odd("gz"), fill, za, zb)
    all_smooth(ba, ya, m)
    apply_k(ba, ya, bb, yb, m, 1, EZ - 1, SHIFTS[3], True)
    copies += start_all([(bb.at[:, own, mid, :], b4_far)], sem, 1)
    apply_k(bb, yb, bc, ya, m, 2, EZ - 2, SHIFTS[4], True)
    copies += start_all([(bc.at[:, own, mid, :], b5_far)], sem, 2)
    apply_k(bc, ya, bd, yb, m, 3, EZ - 3, SHIFTS[5], False)
    total[...] = part[...]
    gram(reader(p, b0, b1, b2, b3w, bb, bc, bd), HIGH, total)
    wait_all(copies)


def second_half_0(b0, b1, b2, b3w, m, za, zb, part, b3_far, b4_far, b5_far, total, *space):
    second_steps(0, b0, b1, b2, b3w, m, za, zb, part, b3_far, b4_far, b5_far, total, *space)


def second_half_1(b0, b1, b2, b3w, m, za, zb, part, other, owned, b3_far, b4_far, b5_far, send, total, *space):
    second_steps(1, b0, b1, b2, b3w, m, za, zb, part, b3_far, b4_far, b5_far, total, *space)
    both = jnp.concatenate([other[...], total[...]], axis=0)
    sums = jnp.sum(jnp.transpose(both), axis=0, keepdims=True)
    cells = jnp.concatenate([owned[j : j + 1, :] for j in range(4)], axis=1).astype(f32)
    send[...] = jnp.broadcast_to(jnp.concatenate([sums, cells], axis=1), (128, 2 * NY))


def cadd(a, b):
    return (a[0] + b[0], a[1] + b[1])


def csub(a, b):
    return (a[0] - b[0], a[1] - b[1])


def cmul(a, b):
    return (a[0] * b[0] - a[1] * b[1], a[0] * b[1] + a[1] * b[0])


def cconj_mul(a, b):
    return (a[0] * b[0] + a[1] * b[1], a[0] * b[1] - a[1] * b[0])


def cdiv(numer, denom, floor):
    size = jnp.maximum(denom[0] * denom[0] + denom[1] * denom[1], floor)
    return (
        (numer[0] * denom[0] + numer[1] * denom[1]) / size,
        (numer[1] * denom[0] - numer[0] * denom[1]) / size,
    )


def tree(terms):
    terms = list(terms)
    while len(terms) > 1:
        terms = [cadd(*terms[i : i + 2]) if i + 1 < len(terms) else terms[i] for i in range(0, len(terms), 2)]
    return terms[0]


def combine(a, scale, b):
    out = []
    for i in range(max(len(a), len(b))):
        if i >= len(b):
            out.append(a[i])
        elif i >= len(a):
            out.append(cmul(scale, b[i]))
        else:
            out.append(cadd(a[i], cmul(scale, b[i])))
    return out


def times_k(a):
    zero = (jnp.zeros_like(a[0][0]),) * 2
    out = [(SHIFTS[i] * v[0], SHIFTS[i] * v[1]) for i, v in enumerate(a)] + [zero]
    return [
        cadd(out[i], (SCALE * a[i - 1][0], SCALE * a[i - 1][1])) if i > 0 else out[i]
        for i in range(len(out))
    ]


def coefficients(entry):
    def g(i, j):
        if i > j:
            re, im = g(j, i)
            return (re, -im)
        if i == j:
            return (entry(SLOT[i, j]), 0.0)
        return (entry(SLOT[i, j]), entry(SLOT[i, j] + 1))

    def times_g(b, rows):
        return [tree([cmul(g(i, j), b[j]) for j in range(len(b))]) for i in range(rows)]

    def dot(a, gb):
        return tree([cconj_mul(a[i], gb[i]) for i in range(len(a))])

    def shadow(b):
        return tree([cmul(g(0, j), b[j]) for j in range(len(b))])

    one = jnp.ones_like(entry(0))
    residual = [(one, jnp.zeros_like(one))]
    direction = residual
    solution = []
    for step in range(ITERS):
        rho = shadow(residual)
        if step == 0:
            floor = 1e-06 * rho[0] * rho[0]
        else:
            beta = cmul(cdiv(rho, rho_prev, floor), cdiv(alpha, omega, 0.0001))
            minus = (-omega[0], -omega[1])
            direction = combine(residual, beta, combine(direction, minus, image))
        image = times_k(direction)
        alpha = cdiv(rho, shadow(image), floor)
        middle = combine(residual, (-alpha[0], -alpha[1]), image)
        bent = times_k(middle)
        seen = times_g(bent, len(bent))
        norm = dot(bent, seen)[0] + 1e-06
        against = dot(middle, seen)
        omega = (against[0] / norm, -against[1] / norm)
        solution = combine(combine(solution, alpha, direction), omega, middle)
        residual = combine(middle, (-omega[0], -omega[1]), bent)
        rho_prev = rho
    return solution


def impedance(x, z0, rows):
    def e(p, c, z):
        f = p * 6 + 2 * c
        return (x[f, z, rows, :], x[f + 1, z, rows, :])

    ex, ey, hx, hy = [], [], [], []
    for p in range(2):
        ex0, ey0 = e(p, 0, z0), e(p, 1, z0)
        ex1, ey1 = e(p, 0, z0 + 1), e(p, 1, z0 + 1)
        ex.append(ex0)
        ey.append(ey0)
        one_x, one_y = (1.0, 0.0) if p == 0 else (0.0, 1.0)
        hx.append((one_x - 2.0 * (ey1[0] - ey0[0]), -2.0 * (ey1[1] - ey0[1])))
        hy.append((one_y + 2.0 * (ex1[0] - ex0[0]), 2.0 * (ex1[1] - ex0[1])))
    det = csub(cmul(hx[0], hy[1]), cmul(hx[1], hy[0]))
    zxx = cdiv(csub(cmul(ex[0], hy[1]), cmul(ex[1], hy[0])), det, 0.25)
    zxy = cdiv(csub(cmul(ex[1], hx[0]), cmul(ex[0], hx[1])), det, 0.25)
    zyx = cdiv(csub(cmul(ey[0], hy[1]), cmul(ey[1], hy[0])), det, 0.25)
    zyy = cdiv(csub(cmul(ey[1], hx[0]), cmul(ey[0], hx[1])), det, 0.25)
    return [*zxx, *zxy, *zyx, *zyy]


def finish(got, k, *rest):
    fars, (x_far, send, basis, x, kv, surface, picked, sem) = rest[:11], rest[11:]
    pairs = [(k, kv), (fars[0], basis.at[0])]
    for p in range(2):
        pairs += [(fars[1 + 5 * p + i], basis.at[1 + i, pl.ds(p * NF, NF)]) for i in range(5)]
    copies = start_all(pairs, sem)
    sub = lax.broadcasted_iota(jnp.int32, (8, NY), 0)
    row = jnp.broadcast_to(jnp.sum(got[:, 0:NY], axis=0, keepdims=True), (8, NY))
    table = jnp.where(sub == 0, row, pltpu.roll(row, 64, 1))
    cache = {}

    def entry(slot):
        if slot not in cache:
            cache[slot] = jnp.broadcast_to(table[:, slot : slot + 1], (8, NY))
        return cache[slot]

    coefs = coefficients(entry)
    wait_all(copies)
    outs = []
    for p in range(2):
        scal = [tuple(jnp.broadcast_to(part[p : p + 1, :], (8, NY)) for part in c) for c in coefs]

        def block(z, _):
            for xb in range(CX // 8):
                rows = pl.ds(8 * xb, 8)
                kz = kv[z, rows, :]
                inv = 1.0 / (16.0 + kz * kz)
                weight = (4.0 * inv, -kz * inv)
                for f in range(p * NF, p * NF + NF, 2):
                    terms = [cmul(scal[i], (basis[i, f, z, rows, :], basis[i, f + 1, z, rows, :])) for i in range(6)]
                    y = cmul(weight, tree(terms))
                    x[f, z, rows, :] = y[0]
                    x[f + 1, z, rows, :] = y[1]
            return 0

        lax.fori_loop(0, NZL, block, 0)
        part = pl.ds(p * NF, NF)
        outs += start_all([(x.at[part], x_far.at[part])], sem, 12 + p)

    for xb in range(CX // 8):
        rows = pl.ds(8 * xb, 8)
        for v, value in enumerate(impedance(x, 0, rows)):
            surface[v * CX + 8 * xb : v * CX + 8 * xb + 8, :] = value
    mine = pltpu.roll(got[:, NY : 2 * NY], lax.rem(NY - 32 * lax.axis_index("gx"), NY), 1).astype(jnp.int32)
    group = lax.broadcasted_iota(jnp.int32, (32, NY), 1) // 32
    cells = mine[0:32, :]
    for e in range(1, 4):
        cells = jnp.where(group == e, pltpu.roll(mine[32 * e : 32 * e + 32, :], 32 * e, 1), cells)
    col = cells % NY
    line = cells // NY
    cols = [col[8 * i : 8 * i + 8, :] for i in range(4)]
    lines = [line[8 * i : 8 * i + 8, :] for i in range(4)]

    def value(v, _):
        acc = [jnp.zeros((8, NY), f32)] * 4
        for r in range(CX):
            src = jnp.broadcast_to(surface[pl.ds(v * CX + r, 1), :], (8, NY))
            for i in range(4):
                hit = jnp.take_along_axis(src, cols[i], axis=1, mode="promise_in_bounds")
                acc[i] = jnp.where(lines[i] == r, hit, acc[i])
        for i in range(4):
            picked[pl.ds(pl.multiple_of(v * 32, 32) + 8 * i, 8), :] = acc[i]
        return 0

    lax.fori_loop(0, 8, value, 0)
    for e in range(4):
        for h in range(2):
            out = None
            for w in range(4):
                v = 4 * h + w
                part = picked[v * 32 : v * 32 + 32, :]
                if w != e:
                    part = pltpu.roll(part, (32 * (w - e)) % NY, 1)
                out = part if out is None else jnp.where(group == w, part, out)
            send[32 * e : 32 * e + 32, NY * h : NY * h + NY] = out
    wait_all(outs)


def hazard_rows(got, spectra, scenario, out):
    scen = scenario.shape[1]
    turned = []
    for h in range(2):
        block = got[0:8, NY * h : NY * h + NY]
        turned.append(jnp.transpose(jnp.concatenate([block, jnp.zeros((NY - 8, NY), f32)], axis=0)))
    b = [spectra[i : i + 1, :] for i in range(4)]
    bx, by = (b[0], b[1]), (b[2], b[3])
    for j in range(4):
        weight = jnp.where(scenario[...] == j, 1.0, 0.25)
        for qb in range(4):
            z = []
            for v in range(8):
                first = (v % 4) * 32 + 8 * qb
                z.append(jnp.broadcast_to(turned[v // 4][first : first + 8, j : j + 1], (8, scen)))
            gx = cadd(cmul((z[0], z[1]), bx), cmul((z[2], z[3]), by))
            gy = cadd(cmul((z[4], z[5]), bx), cmul((z[6], z[7]), by))
            power = gx[0] * gx[0] + gx[1] * gx[1] + gy[0] * gy[0] + gy[1] * gy[1]
            row = 32 * j + 8 * qb
            out[row : row + 8, :] = weight * power


def partners(count):
    first = [(i, i ^ 1) for i in range(count)]
    second = [(i, ((i + 1) ^ 1) - 1) for i in range(1, count - 1)]
    return first, second


def exchange(to_a, to_b, axis):
    first, second = partners(lax.axis_size(axis))
    return lax.ppermute(to_a, axis, first), lax.ppermute(to_b, axis, second)


def per_device(right_side, conductance, owned_cells, spectra, scenario_tile):
    block = (NF, NZL, CX, NY)
    wide = (NF, NZL, WX, NY)
    whole = (2 * NF, NZL, CX, NY)
    dma = pltpu.SemaphoreType.DMA
    space = pltpu.VMEM((NF, EZ, WX, NY), f32)
    r = right_side.reshape(whole)
    k = conductance
    side = ((2 * NF + 1) * NZL * SIDE, NY)
    rims = [pltpu.VMEM((2 * NF, NZL, 16, NY), f32), pltpu.VMEM((NZL, 16, NY), f32), dma((4,))]
    near = exchange(*call(pack_x, [HBM] * 2, [(side, VM)] * 2, rims)(r, k), "gx")
    deep = [((n * REACH * (CX + 2 * SIDE), NY), VM) for n in (NF + 1, NF)]
    packed = call(pack_z, [VM] * 4, [deep[0]] * 2 + [deep[1]] * 2, moved=1 << 22)(r, k, *near)
    halo_0 = exchange(*packed[0:2], "gz")
    halo_1 = exchange(*packed[2:4], "gz")
    back = ((NF * REACH * BACK, NY), VM)
    firsts = [(block, VM), (block, VM), (wide, VM), back, back, (block, HBM), (block, HBM)]
    cost = {"flops": 1 << 24, "moved": 1 << 23}
    *b_0, to_a, to_b, b1_0, b2_0, m = call(
        first_half_0,
        [VM] * 6,
        firsts + [((2, EZ, WX, NY), VM)],
        [space] * 4 + [dma((2,)), pltpu.VMEM((EZ, WX, NY), f32)],
        **cost,
    )(r, k, *near, *halo_0)
    halo_0 = exchange(to_a, to_b, "gz")
    *b_1, to_a, to_b, b1_1, b2_1 = call(
        first_half_1, [VM] * 6, firsts, [space] * 4 + [dma((2,))], **cost
    )(r, m, *near, *halo_1)
    halo_1 = exchange(to_a, to_b, "gz")
    table = ((64, NY), VM)
    part_0, part_1 = call(low_gram, [VM] * 7, [table] * 2, **cost)(r, *b_0, *b_1)
    seconds = [(block, HBM)] * 3
    spaces = [space] * 6 + [dma((3,))]
    *high_0, total = call(
        second_half_0, [VM] * 8, seconds + [table], spaces, **cost
    )(r, *b_0, m, *halo_0, part_0)
    *high_1, send = call(
        second_half_1,
        [VM] * 10,
        seconds + [((128, 2 * NY), VM)],
        [pltpu.VMEM((64, NY), f32)] + spaces,
        **cost,
    )(r, *b_1, m, *halo_1, part_1, total, owned_cells[0])
    held = (send, k, r, b1_0, b2_0, *high_0, b1_1, b2_1, *high_1)
    send, *fars = lax.optimization_barrier(held)
    got = lax.all_to_all(send, ("gz", "gx"), 0, 0, tiled=True)
    x, send = call(
        finish,
        [VM] + [HBM] * 12,
        [(whole, HBM), ((128, 2 * NY), VM)],
        [
            pltpu.VMEM((6, *whole), f32),
            pltpu.VMEM(whole, f32),
            pltpu.VMEM((NZL, CX, NY), f32),
            pltpu.VMEM((8 * CX, NY), f32),
            pltpu.VMEM((8 * CX, NY), f32),
            dma((14,)),
        ],
    )(got, *fars)
    got = lax.all_to_all(send, ("gz", "gx"), 0, 0, tiled=True)
    scen = spectra.shape[0]
    (hazard,) = call(hazard_rows, [VM] * 3, [((128, scen), VM)])(got, spectra.T, scenario_tile.reshape(1, scen))
    return x.reshape(right_side.shape), hazard


def solution(mesh):
    return jax.shard_map(
        per_device,
        mesh=mesh,
        in_specs=(
            P(None, None, None, "gz", "gx", None),
            P("gz", "gx", None),
            P(("gz", "gx"), None, None),
            P(),
            P(),
        ),
        out_specs=(P(None, None, None, "gz", "gx", None), P(("gz", "gx"), None)),
        check_vma=False,
    )
```

time: 134 us -> 103 us (0.77)
  waiting for transfers between devices: 46.3 us -> 7.82 us
  blocking collectives: 13.9 us -> 37.7 us
  local copies, waits for them, and re-layouts: 11.1 us -> 3.61 us
  starting transfers between devices: 30.8 us -> 23.7 us
    ppermute x6 -> x10, waiting for transfers between devices: 36.6 us -> 7.82 us  [exchange(): return (lax.ppermute(to_a, axis, first), lax.ppermute(to_b, axis, second))]
    all_to_all x1 -> x2, blocking collectives: 13.9 us -> 37.7 us  [per_device(): got = lax.all_to_all(send, ('gz', 'gx'), 0, 0, tiled=True)]
    all_to_all x1 -> x0, starting transfers between devices: 13.8 us -> none  [per_device(): got = lax.all_to_all(send, ('gz', 'gx'), 0, 0, tiled=True)]
    all_to_all x1 -> x0, waiting for transfers between devices: 9.71 us -> none  [per_device(): got = lax.all_to_all(send, ('gz', 'gx'), 0, 0, tiled=True)]
    unnamed x32 -> x12, local copies, waits for them, and re-layouts: 10.2 us -> 3.34 us
    ppermute x6 -> x10, starting transfers between devices: 17 us -> 23.7 us  [exchange(): return (lax.ppermute(to_a, axis, first), lax.ppermute(to_b, axis, second))]
    pallas_call x7 -> x9, Pallas kernels: 30.2 us -> 29.1 us  [the longest x1 7.04 us: per_device(): call(finish, [VM] + [HBM] * 12, [(whole, HBM), ((128, 2 * NY), VM)], [plt...]
  transfers between devices with their start and end apart: 7 -> 10, of which waited for: 7 -> 2; matrix products, arithmetic and copies ran while one was open for 0% -> 0% of each run, Pallas kernels for 1% -> 15%
where the time goes in v2:
time: 103 us
  blocking collectives  37.7 us (37%)
  Pallas kernels  29.1 us (28%)
  starting transfers between devices  23.7 us (23%)
  waiting for transfers between devices  7.82 us (8%)
  local copies, waits for them, and re-layouts  3.61 us (4%)
    all_to_all x2, blocking collectives, per_device(): got = lax.all_to_all(send, ('gz', 'gx'), 0, 0, tiled=True)  37.7 us
    ppermute x10, starting transfers between devices, exchange(): return (lax.ppermute(to_a, axis, first), lax.ppermute(to_b, axis, second))  23.7 us
    ppermute x10, waiting for transfers between devices, exchange(): return (lax.ppermute(to_a, axis, first), lax.ppermute(to_b, axis, second))  7.82 us
    pallas_call x1, Pallas kernels, per_device(): call(finish, [VM] + [HBM] * 12, [(whole, HBM), ((128, 2 * NY), VM)], [plt...  7.04 us
    pallas_call x1, Pallas kernels, per_device(): call(second_half_1, [VM] * 10, seconds + [((128, 2 * NY), VM)], [pltpu.VM...  5.2 us
    pallas_call x1, Pallas kernels, per_device(): call(second_half_0, [VM] * 8, seconds + [table], spaces, **cost)  5.08 us
    pallas_call x1, Pallas kernels, per_device(): call(first_half_0, [VM] * 6, firsts + [((2, EZ, WX, NY), VM)], [space] *...  4.62 us
    pallas_call x1, Pallas kernels, per_device(): call(first_half_1, [VM] * 6, firsts, [space] * 4 + [dma((2,))], **cost)  4.45 us
  transfers between devices with their start and end apart: 10, of which 2 were waited for; matrix products, arithmetic and copies ran while one was open for 0% of the time, Pallas kernels for 15%

profile of v2, /device:TPU:1, one launch (start us, length us, event | category | flops | bytes accessed | tf_op | source)
XLA Modules:
  0.0 102.8 jit_solution(6511439963175456855)
XLA Ops:
  0.6 1.1 %copy-done = f32[2,3,2,4,32,128]{5,4,3,2,1,0:T(8,128)S(1)} copy-done((f32[2,3,2,4,32,128]{5,4,3,2,1,0:T(8,128)S(1)}, f32[2,3,2,4,32,128]{5,4,3,2,1,0:T(8,128)}, u32[]{:S(2)}) %copy-start) | copy-done | bytes 786456
  1.8 0.8 copy-done.1
  2.6 0.1 shard_map.68
  2.8 1.5 %collective-permute-start = (f32[312,128]{1,0:T(8,128)S(1)}, f32[312,128]{1,0:T(8,128)S(1)}, u32[]{:S(2)}, u32[]{:S(2)}) collective-permute-start(f32[312,128]{1,0:T(8,128)S(1)} %get-tuple-element.48), channel_id=1, source_target_pairs={{0,1},{1,0},{2,3},{3,2},{4,5},{5,4},{6,7},{7,6},{8,9},{9,8},{10,11... | collective-permute-start | bytes 479240 | tf_op jit(solution)/shard_map/ppermute | solution.py:581
  4.3 4.6 %collective-permute-start.1 = (f32[312,128]{1,0:T(8,128)S(1)}, f32[312,128]{1,0:T(8,128)S(1)}, u32[]{:S(2)}, u32[]{:S(2)}) collective-permute-start(f32[312,128]{1,0:T(8,128)S(1)} %get-tuple-element.49), channel_id=1, source_target_pairs={{1,2},{2,1},{5,6},{6,5},{9,10},{10,9},{13,14},{14,13},{17,18},{18,... | collective-permute-start | bytes 479240 | tf_op jit(solution)/shard_map/ppermute | solution.py:581
  8.9 0.0 collective-permute-done.xa
  8.9 3.4 %collective-permute-done.1.xb = f32[312,128]{1,0:T(8,128)S(1)} collective-permute-done((f32[312,128]{1,0:T(8,128)S(1)}, f32[312,128]{1,0:T(8,128)S(1)}, u32[]{:S(2)}, u32[]{:S(2)}) %collective-permute-start.1) | collective-permute-done | bytes 159776 | tf_op jit(solution)/shard_map/ppermute | solution.py:581
  12.3 0.1 shard_map.69
  12.5 1.5 %collective-permute-start.2 = (f32[924,128]{1,0:T(8,128)S(1)}, f32[924,128]{1,0:T(8,128)S(1)}, u32[]{:S(2)}, u32[]{:S(2)}) collective-permute-start(f32[924,128]{1,0:T(8,128)S(1)} %get-tuple-element.50), channel_id=1, source_target_pairs={{0,4},{4,0},{8,12},{12,8},{16,20},{20,16},{24,28},{28,24},{32,36},... | collective-permute-start | bytes 1419272 | tf_op jit(solution)/shard_map/ppermute | solution.py:581
  13.9 0.7 collective-permute-start.3
  14.6 3.6 %collective-permute-start.4 = (f32[792,128]{1,0:T(8,128)S(1)}, f32[792,128]{1,0:T(8,128)S(1)}, u32[]{:S(2)}, u32[]{:S(2)}) collective-permute-start(f32[792,128]{1,0:T(8,128)S(1)} %get-tuple-element.53), channel_id=1, source_target_pairs={{0,4},{4,0},{8,12},{12,8},{16,20},{20,16},{24,28},{28,24},{32,36},... | collective-permute-start | bytes 1216520 | tf_op jit(solution)/shard_map/ppermute | solution.py:581
  18.2 0.7 collective-permute-start.5
  18.9 4.4 %collective-permute-done.2.za = f32[924,128]{1,0:T(8,128)S(1)} collective-permute-done((f32[924,128]{1,0:T(8,128)S(1)}, f32[924,128]{1,0:T(8,128)S(1)}, u32[]{:S(2)}, u32[]{:S(2)}) %collective-permute-start.2) | collective-permute-done | bytes 473120 | tf_op jit(solution)/shard_map/ppermute | solution.py:581
  23.3 4.6 %shard_map.70 = (f32[6,4,32,128]{3,2,1,0:T(8,128)S(1)}, f32[6,4,32,128]{3,2,1,0:T(8,128)S(1)}, f32[6,4,48,128]{3,2,1,0:T(8,128)S(1)}, f32[684,128]{1,0:T(8,128)S...) custom-call(f32[12,4,32,128]{3,2,1,0:T(8,128)S(1)} %bitcast.15, ...), custom_call_target="tpu_custom_call" | custom-call | flops 16777216 | bytes 8388608 | tf_op jit(solution)/shard_map/pallas_call | solution.py:602
  27.9 4.5 %collective-permute-start.8 = (f32[684,128]{1,0:T(8,128)S(1)}, f32[684,128]{1,0:T(8,128)S(1)}, u32[]{:S(2)}, u32[]{:S(2)}) collective-permute-start(f32[684,128]{1,0:T(8,128)S(1)} %get-tuple-element.64), channel_id=1, source_target_pairs={{0,4},{4,0},{8,12},{12,8},{16,20},{20,16},{24,28},{28,24},{32,36},... | collective-permute-start | bytes 1050632 | tf_op jit(solution)/shard_map/ppermute | solution.py:581
  32.4 0.7 collective-permute-start.9
  33.1 4.4 %shard_map.71 = (f32[6,4,32,128]{3,2,1,0:T(8,128)S(1)}, f32[6,4,32,128]{3,2,1,0:T(8,128)S(1)}, f32[6,4,48,128]{3,2,1,0:T(8,128)S(1)}, f32[684,128]{1,0:T(8,128)S...) custom-call(f32[12,4,32,128]{3,2,1,0:T(8,128)S(1)} %bitcast.16, ...), custom_call_target="tpu_custom_call" | custom-call | flops 16777216 | bytes 8388608 | tf_op jit(solution)/shard_map/pallas_call | solution.py:610
  37.5 5.3 %collective-permute-start.6 = (f32[684,128]{1,0:T(8,128)S(1)}, f32[684,128]{1,0:T(8,128)S(1)}, u32[]{:S(2)}, u32[]{:S(2)}) collective-permute-start(f32[684,128]{1,0:T(8,128)S(1)} %get-tuple-element.58), channel_id=1, source_target_pairs={{0,4},{4,0},{8,12},{12,8},{16,20},{20,16},{24,28},{28,24},{32,36},... | collective-permute-start | bytes 1050632 | tf_op jit(solution)/shard_map/ppermute | solution.py:581
  42.9 0.7 collective-permute-start.7
  43.5 1.2 %shard_map.72 = (f32[64,128]{1,0:T(8,128)S(1)}, f32[64,128]{1,0:T(8,128)S(1)}) custom-call(f32[12,4,32,128]{3,2,1,0:T(8,128)S(1)} %bitcast.17, f32[6,4,32,128]{3,2,1,0:T(8,128)S(1)} %get-tuple-element.60.b1_0.b1, f32[6,4,32,128]{3,2,1,0:T(8,128)S(1)} %get-tuple-element.61.b2_0.b2, f32[6,4,48,128]{3,2,1,0:T(8,128)S(1)} %get-tuple-element.62.b3w_0.b3w, ...), custom_call_target="tpu_custom_call" | custom-call | flops 16777216 | bytes 8388608 | tf_op jit(solution)/shard_map/pallas_call | solution.py:615
  44.7 5.1 %shard_map.73 = (f32[6,4,32,128]{3,2,1,0:T(8,128)S(1)}, f32[6,4,32,128]{3,2,1,0:T(8,128)S(1)}, f32[6,4,32,128]{3,2,1,0:T(8,128)S(1)}, f32[64,128]{1,0:T(8,128)S(1)}) custom-call(f32[12,4,32,128]{3,2,1,0:T(8,128)S(1)} %bitcast.18, f32[6,4,32,128]{3,2,1,0:T(8,128)S(1)} %get-tuple-element.60.b1_0.b1, f32[6,4,32,128]{3,2,1,0:T(8,128)S(1)} %get-tuple-element.61.b2_0.b2, ...), custom_call_target="tpu_custom_call" | custom-call | flops 16777216 | bytes 8388608 | tf_op jit(solution)/shard_map/pallas_call | solution.py:618
  49.8 0.0 copy-start.3
  49.9 0.7 copy-done.3
  50.5 5.2 %shard_map.74 = (f32[6,4,32,128]{3,2,1,0:T(8,128)S(1)}, f32[6,4,32,128]{3,2,1,0:T(8,128)S(1)}, f32[6,4,32,128]{3,2,1,0:T(8,128)S(1)}, f32[128,256]{1,0:T(8,128)S(1)}) custom-call(f32[12,4,32,128]{3,2,1,0:T(8,128)S(1)} %bitcast.19, f32[6,4,32,128]{3,2,1,0:T(8,128)S(1)} %get-tuple-element.55.b1_1.b1, f32[6,4,32,128]{3,2,1,0:T(8,128)S(1)} %get-tuple-element.56.b2_1.b2, ...), custom_call_target="tpu_custom_call" | custom-call | flops 16777216 | bytes 8388608 | tf_op jit(solution)/shard_map/pallas_call | solution.py:621
  55.7 0.1 copy.7
  55.9 23.7 %all_to_all.22 = f32[128,1,256]{2,1,0:T(1,128)S(1)} all-to-all(f32[128,1,256]{2,1,0:T(1,128)S(1)} %copy.7), channel_id=1, replica_groups=mesh['gz'=32,'gx'=4] {'gz','gx'}, dimensions={0} | all-to-all | bytes 262144 | tf_op jit(solution)/shard_map/all_to_all | solution.py:630
  79.6 7.0 %shard_map.75 = (f32[12,4,32,128]{3,2,1,0:T(8,128)}, f32[128,256]{1,0:T(8,128)S(1)}) custom-call(f32[128,256]{1,0:T(8,128)S(1)} %bitcast.21, f32[4,32,128]{2,1,0:T(8,128)S(1)} %copy-done.1, f32[12,4,32,128]{3,2,1,0:T(8,128)S(1)} %bitcast.20, f32[6,4,32,128]{3,2,1,0:T(8,128)S(1)} %get-tuple-element.82.rest_1_, ...), custom_call_target="tpu_custom_call" | custom-call | tf_op jit(solution)/shard_map/pallas_call | solution.py:631
  86.6 0.1 copy.8
  86.8 14.0 %all_to_all.23 = f32[128,1,256]{2,1,0:T(1,128)S(1)} all-to-all(f32[128,1,256]{2,1,0:T(1,128)S(1)} %copy.8), channel_id=1, replica_groups=mesh['gz'=32,'gx'=4] {'gz','gx'}, dimensions={0} | all-to-all | bytes 262144 | tf_op jit(solution)/shard_map/all_to_all | solution.py:644
  100.8 0.0 copy-start.4
  100.8 0.7 copy-done.2
  101.5 1.2 %shard_map.76 = f32[128,512]{1,0:T(8,128)} custom-call(f32[128,256]{1,0:T(8,128)S(1)} %bitcast.22, f32[4,512]{1,0:T(4,128)S(1)} %bitcast.25, s32[1,512]{1,0:T(1,128)S(1)} %bitcast.27), custom_call_target="tpu_custom_call" | custom-call | tf_op jit(solution)/shard_map/pallas_call | solution.py:646
  (13 shorter events, 0.0 us)
Async XLA Ops:
  0.6 1.1 %copy-start = (f32[2,3,2,4,32,128]{5,4,3,2,1,0:T(8,128)S(1)}, f32[2,3,2,4,32,128]{5,4,3,2,1,0:T(8,128)}, u32[]{:S(2)}) copy-start(f32[2,3,2,4,32,128]{5,4,3,2,1,0:T(8,128)} %param.5) | copy-start | bytes 2359300
  1.8 0.8 copy-start.1
  2.8 6.1 %collective-permute-start = (f32[312,128]{1,0:T(8,128)S(1)}, f32[312,128]{1,0:T(8,128)S(1)}, u32[]{:S(2)}, u32[]{:S(2)}) collective-permute-start(f32[312,128]{1,0:T(8,128)S(1)} %get-tuple-element.48), channel_id=1, source_target_pairs={{0,1},{1,0},{2,3},{3,2},{4,5},{5,4},{6,7},{7,6},{8,9},{9,8},{10,11... | collective-permute-start | bytes 479240 | tf_op jit(solution)/shard_map/ppermute | solution.py:581
  4.3 8.1 %collective-permute-start.1 = (f32[312,128]{1,0:T(8,128)S(1)}, f32[312,128]{1,0:T(8,128)S(1)}, u32[]{:S(2)}, u32[]{:S(2)}) collective-permute-start(f32[312,128]{1,0:T(8,128)S(1)} %get-tuple-element.49), channel_id=1, source_target_pairs={{1,2},{2,1},{5,6},{6,5},{9,10},{10,9},{13,14},{14,13},{17,18},{18,... | collective-permute-start | bytes 479240 | tf_op jit(solution)/shard_map/ppermute | solution.py:581
  12.5 10.8 %collective-permute-start.2 = (f32[924,128]{1,0:T(8,128)S(1)}, f32[924,128]{1,0:T(8,128)S(1)}, u32[]{:S(2)}, u32[]{:S(2)}) collective-permute-start(f32[924,128]{1,0:T(8,128)S(1)} %get-tuple-element.50), channel_id=1, source_target_pairs={{0,4},{4,0},{8,12},{12,8},{16,20},{20,16},{24,28},{28,24},{32,36},... | collective-permute-start | bytes 1419272 | tf_op jit(solution)/shard_map/ppermute | solution.py:581
  13.9 9.3 %collective-permute-start.3 = (f32[924,128]{1,0:T(8,128)S(1)}, f32[924,128]{1,0:T(8,128)S(1)}, u32[]{:S(2)}, u32[]{:S(2)}) collective-permute-start(f32[924,128]{1,0:T(8,128)S(1)} %get-tuple-element.51), channel_id=1, source_target_pairs={{4,8},{8,4},{12,16},{16,12},{20,24},{24,20},{28,32},{32,28},{36,40... | collective-permute-start | bytes 1419272 | tf_op jit(solution)/shard_map/ppermute | solution.py:581
  14.6 18.4 %collective-permute-start.4 = (f32[792,128]{1,0:T(8,128)S(1)}, f32[792,128]{1,0:T(8,128)S(1)}, u32[]{:S(2)}, u32[]{:S(2)}) collective-permute-start(f32[792,128]{1,0:T(8,128)S(1)} %get-tuple-element.53), channel_id=1, source_target_pairs={{0,4},{4,0},{8,12},{12,8},{16,20},{20,16},{24,28},{28,24},{32,36},... | collective-permute-start | bytes 1216520 | tf_op jit(solution)/shard_map/ppermute | solution.py:581
  18.2 14.8 %collective-permute-start.5 = (f32[792,128]{1,0:T(8,128)S(1)}, f32[792,128]{1,0:T(8,128)S(1)}, u32[]{:S(2)}, u32[]{:S(2)}) collective-permute-start(f32[792,128]{1,0:T(8,128)S(1)} %get-tuple-element.54), channel_id=1, source_target_pairs={{4,8},{8,4},{12,16},{16,12},{20,24},{24,20},{28,32},{32,28},{36,40... | collective-permute-start | bytes 1216520 | tf_op jit(solution)/shard_map/ppermute | solution.py:581
  27.9 16.8 %collective-permute-start.8 = (f32[684,128]{1,0:T(8,128)S(1)}, f32[684,128]{1,0:T(8,128)S(1)}, u32[]{:S(2)}, u32[]{:S(2)}) collective-permute-start(f32[684,128]{1,0:T(8,128)S(1)} %get-tuple-element.64), channel_id=1, source_target_pairs={{0,4},{4,0},{8,12},{12,8},{16,20},{20,16},{24,28},{28,24},{32,36},... | collective-permute-start | bytes 1050632 | tf_op jit(solution)/shard_map/ppermute | solution.py:581
  32.4 12.3 %collective-permute-start.9 = (f32[684,128]{1,0:T(8,128)S(1)}, f32[684,128]{1,0:T(8,128)S(1)}, u32[]{:S(2)}, u32[]{:S(2)}) collective-permute-start(f32[684,128]{1,0:T(8,128)S(1)} %get-tuple-element.65), channel_id=1, source_target_pairs={{4,8},{8,4},{12,16},{16,12},{20,24},{24,20},{28,32},{32,28},{36,40... | collective-permute-start | bytes 1050632 | tf_op jit(solution)/shard_map/ppermute | solution.py:581
  37.5 12.3 %collective-permute-start.6 = (f32[684,128]{1,0:T(8,128)S(1)}, f32[684,128]{1,0:T(8,128)S(1)}, u32[]{:S(2)}, u32[]{:S(2)}) collective-permute-start(f32[684,128]{1,0:T(8,128)S(1)} %get-tuple-element.58), channel_id=1, source_target_pairs={{0,4},{4,0},{8,12},{12,8},{16,20},{20,16},{24,28},{28,24},{32,36},... | collective-permute-start | bytes 1050632 | tf_op jit(solution)/shard_map/ppermute | solution.py:581
  42.9 7.0 %collective-permute-start.7 = (f32[684,128]{1,0:T(8,128)S(1)}, f32[684,128]{1,0:T(8,128)S(1)}, u32[]{:S(2)}, u32[]{:S(2)}) collective-permute-start(f32[684,128]{1,0:T(8,128)S(1)} %get-tuple-element.59), channel_id=1, source_target_pairs={{4,8},{8,4},{12,16},{16,12},{20,24},{24,20},{28,32},{32,28},{36,40... | collective-permute-start | bytes 1050632 | tf_op jit(solution)/shard_map/ppermute | solution.py:581
  49.8 0.7 copy-start.3
  100.8 0.7 copy-start.2
  100.8 0.7 copy-start.4

commit v3 on v2

--- a/solution.py
+++ b/solution.py
@@ -61,20 +61,15 @@
         copy.wait()
 
 
-def pack_x(r, k, to_a, to_b, rim, rim_k, sem):
-    pairs = []
-    for i in range(2):
-        src = pl.ds(i * (CX - 8), 8)
-        pairs.append((r.at[:, :, src, :], rim.at[:, :, pl.ds(8 * i, 8), :]))
-        pairs.append((k.at[:, src, :], rim_k.at[:, pl.ds(8 * i, 8), :]))
-    wait_all(start_all(pairs, sem))
+def pack_x(r_far, k_far, to_a, to_b, r, k, sem):
+    wait_all(start_all([(r_far, r), (k_far, k)], sem))
 
     def fill(up, down):
         for f in range(2 * NF + 1):
             for z in range(NZL):
                 row = (f * NZL + z) * SIDE
-                src = rim_k.at[z] if f == 2 * NF else rim.at[f, z]
-                up[row : row + SIDE, :] = src[16 - SIDE : 16, :]
+                src = k.at[z] if f == 2 * NF else r.at[f, z]
+                up[row : row + SIDE, :] = src[CX - SIDE : CX, :]
                 down[row : row + SIDE, :] = src[0:SIDE, :]
 
     either(odd("gx"), fill, to_a, to_b)
@@ -124,13 +119,6 @@
     return pltpu.roll(a, 1, 0)
 
 
-def h_flat(y, base, z, last):
-    ex, ey, ez = y[base, z], y[base + 2, z], y[base + 4, z]
-    hx = next_y(ez, last) - ez - (y[base + 2, z + 1] - ey)
-    hy = y[base, z + 1] - ex - (next_x(ez) - ez)
-    return hx, hy
-
-
 def smooth(b, y, m, base, z):
     mr, mi = m[0, z], m[1, z]
     for c in range(3):
@@ -139,32 +127,30 @@
         y[base + 2 * c + 1, z] = mr * im + mi * re
 
 
-def apply_k(b, y, bn, yn, m, lo, hi, shift, want_y):
+def apply_k(b, y, bn, yn, hs, m, lo, hi, shift, want_y):
     first, last = lanes()
     own = (1.0 - shift) / SCALE
     inv = 1.0 / SCALE
-
-    def layer(z, prev):
-        out = []
+    for z in range(lo - 1, hi):
         for e in range(2):
-            hxp, hyp = prev[e]
             ex, ey, ez = y[e, z], y[e + 2, z], y[e + 4, z]
-            hx, hy = h_flat(y, e, z, last)
-            hz = next_x(ey) - ey - (next_y(ex, last) - ex)
-            cx = hz - jnp.where(first, -ex, pltpu.roll(hz, 1, 1)) - (hy - hyp)
-            cy = hx - hxp - (hz - prev_x(hz))
+            hs[e, z] = next_y(ez, last) - ez - (y[e + 2, z + 1] - ey)
+            hs[e + 2, z] = y[e, z + 1] - ex - (next_x(ez) - ez)
+            hs[e + 4, z] = next_x(ey) - ey - (next_y(ex, last) - ex)
+    for z in range(lo, hi):
+        for e in range(2):
+            hx, hy, hz = hs[e, z], hs[e + 2, z], hs[e + 4, z]
+            ex, ey, ez = y[e, z], y[e + 2, z], y[e + 4, z]
+            cx = hz - jnp.where(first, -ex, pltpu.roll(hz, 1, 1)) - (hy - hs[e + 2, z - 1])
+            cy = hx - hs[e, z - 1] - (hz - prev_x(hz))
             cz = hy - prev_x(hy) - (hx - jnp.where(first, ez, pltpu.roll(hx, 1, 1)))
             for c, (cur, old) in enumerate(((cx, ex), (cy, ey), (cz, ez))):
                 new = cur - 4.0 * old
                 if inv != 1.0:
                     new = new * inv
                 bn[e + 2 * c, z] = new + own * b[e + 2 * c, z]
-            out.append((hx, hy))
         if want_y:
             smooth(bn, yn, m, 0, z)
-        return tuple(out)
-
-    lax.fori_loop(lo, hi, layer, tuple(h_flat(y, e, lo - 1, last) for e in range(2)))
 
 
 def all_smooth(b, y, m):
@@ -219,17 +205,17 @@
     lax.fori_loop(0, NF, field, 0)
 
 
-def first_steps(p, r, xa, xb, za, zb, b1, b2, b3w, to_a, to_b, b1_far, b2_far, m, ba, bb, ya, yb, sem):
+def first_steps(p, r, xa, xb, za, zb, b1, b2, b3w, to_a, to_b, b1_far, b2_far, m, ba, bb, ya, yb, hs, sem):
     fields = range(NF)
     extend([ba.at[f] for f in fields], [r.at[p * NF + f] for f in fields], xa, xb, za, zb, p * NF, 0)
     all_smooth(ba, ya, m)
-    apply_k(ba, ya, bb, yb, m, 1, EZ - 1, SHIFTS[0], True)
+    apply_k(ba, ya, bb, yb, hs, m, 1, EZ - 1, SHIFTS[0], True)
     keep(bb, b1)
     copies = start_all([(b1, b1_far)], sem)
-    apply_k(bb, yb, ba, ya, m, 2, EZ - 2, SHIFTS[1], True)
+    apply_k(bb, yb, ba, ya, hs, m, 2, EZ - 2, SHIFTS[1], True)
     keep(ba, b2)
     copies += start_all([(b2, b2_far)], sem, 1)
-    apply_k(ba, ya, bb, yb, m, 3, EZ - 3, SHIFTS[2], False)
+    apply_k(ba, ya, bb, yb, hs, m, 3, EZ - 3, SHIFTS[2], False)
     cut = (WX - BACK) // 2
     for f in fields:
         b3w[f] = bb[f, REACH : REACH + NZL]
@@ -245,13 +231,13 @@
     wait_all(copies)
 
 
-def first_half_0(r, k, xa, xb, za, zb, b1, b2, b3w, to_a, to_b, b1_far, b2_far, m, ba, bb, ya, yb, sem, kx):
+def first_half_0(r, k, xa, xb, za, zb, b1, b2, b3w, to_a, to_b, b1_far, b2_far, m, ba, bb, ya, yb, hs, sem, kx):
     weights(k, xa, xb, za, zb, m, kx)
-    first_steps(0, r, xa, xb, za, zb, b1, b2, b3w, to_a, to_b, b1_far, b2_far, m, ba, bb, ya, yb, sem)
-
-
-def first_half_1(r, m, xa, xb, za, zb, b1, b2, b3w, to_a, to_b, b1_far, b2_far, ba, bb, ya, yb, sem):
-    first_steps(1, r, xa, xb, za, zb, b1, b2, b3w, to_a, to_b, b1_far, b2_far, m, ba, bb, ya, yb, sem)
+    first_steps(0, r, xa, xb, za, zb, b1, b2, b3w, to_a, to_b, b1_far, b2_far, m, ba, bb, ya, yb, hs, sem)
+
+
+def first_half_1(r, m, xa, xb, za, zb, b1, b2, b3w, to_a, to_b, b1_far, b2_far, ba, bb, ya, yb, hs, sem):
+    first_steps(1, r, xa, xb, za, zb, b1, b2, b3w, to_a, to_b, b1_far, b2_far, m, ba, bb, ya, yb, hs, sem)
 
 
 PAIRS = [(i, j) for i in range(7) for j in range(i, 7)]
@@ -309,7 +295,7 @@
     return read
 
 
-def second_steps(p, b0, b1, b2, b3w, m, za, zb, part, b3_far, b4_far, b5_far, total, ba, bb, bc, bd, ya, yb, sem):
+def second_steps(p, b0, b1, b2, b3w, m, za, zb, part, b3_far, b4_far, b5_far, total, ba, bb, bc, bd, ya, yb, hs, sem):
     cut = (WX - BACK) // 2
     own = pl.ds(REACH, NZL)
     mid = pl.ds(8, CX)
@@ -330,11 +316,11 @@
 
     either(odd("gz"), fill, za, zb)
     all_smooth(ba, ya, m)
-    apply_k(ba, ya, bb, yb, m, 1, EZ - 1, SHIFTS[3], True)
+    apply_k(ba, ya, bb, yb, hs, m, 1, EZ - 1, SHIFTS[3], True)
     copies += start_all([(bb.at[:, own, mid, :], b4_far)], sem, 1)
-    apply_k(bb, yb, bc, ya, m, 2, EZ - 2, SHIFTS[4], True)
+    apply_k(bb, yb, bc, ya, hs, m, 2, EZ - 2, SHIFTS[4], True)
     copies += start_all([(bc.at[:, own, mid, :], b5_far)], sem, 2)
-    apply_k(bc, ya, bd, yb, m, 3, EZ - 3, SHIFTS[5], False)
+    apply_k(bc, ya, bd, yb, hs, m, 3, EZ - 3, SHIFTS[5], False)
     total[...] = part[...]
     gram(reader(p, b0, b1, b2, b3w, bb, bc, bd), HIGH, total)
     wait_all(copies)
@@ -448,33 +434,44 @@
     return solution
 
 
-def impedance(x, z0, rows):
+def surface_power(x, rows):
     def e(p, c, z):
-        f = p * 6 + 2 * c
+        f = p * NF + 2 * c
         return (x[f, z, rows, :], x[f + 1, z, rows, :])
 
     ex, ey, hx, hy = [], [], [], []
     for p in range(2):
-        ex0, ey0 = e(p, 0, z0), e(p, 1, z0)
-        ex1, ey1 = e(p, 0, z0 + 1), e(p, 1, z0 + 1)
+        ex0, ey0 = e(p, 0, 0), e(p, 1, 0)
+        ex1, ey1 = e(p, 0, 1), e(p, 1, 1)
         ex.append(ex0)
         ey.append(ey0)
         one_x, one_y = (1.0, 0.0) if p == 0 else (0.0, 1.0)
         hx.append((one_x - 2.0 * (ey1[0] - ey0[0]), -2.0 * (ey1[1] - ey0[1])))
         hy.append((one_y + 2.0 * (ex1[0] - ex0[0]), 2.0 * (ex1[1] - ex0[1])))
     det = csub(cmul(hx[0], hy[1]), cmul(hx[1], hy[0]))
-    zxx = cdiv(csub(cmul(ex[0], hy[1]), cmul(ex[1], hy[0])), det, 0.25)
-    zxy = cdiv(csub(cmul(ex[1], hx[0]), cmul(ex[0], hx[1])), det, 0.25)
-    zyx = cdiv(csub(cmul(ey[0], hy[1]), cmul(ey[1], hy[0])), det, 0.25)
-    zyy = cdiv(csub(cmul(ey[1], hx[0]), cmul(ey[0], hx[1])), det, 0.25)
-    return [*zxx, *zxy, *zyx, *zyy]
+    zxx = csub(cmul(ex[0], hy[1]), cmul(ex[1], hy[0]))
+    zxy = csub(cmul(ex[1], hx[0]), cmul(ex[0], hx[1]))
+    zyx = csub(cmul(ey[0], hy[1]), cmul(ey[1], hy[0]))
+    zyy = csub(cmul(ey[1], hx[0]), cmul(ey[0], hx[1]))
+    size = det[0] * det[0] + det[1] * det[1]
+    inv = 1.0 / jnp.maximum(size, 0.25)
+    scale = size * inv * inv
+    cross = cadd(cconj_mul(zxx, zxy), cconj_mul(zyx, zyy))
+    first = zxx[0] * zxx[0] + zxx[1] * zxx[1] + (zyx[0] * zyx[0] + zyx[1] * zyx[1])
+    second = zxy[0] * zxy[0] + zxy[1] * zxy[1] + (zyy[0] * zyy[0] + zyy[1] * zyy[1])
+    return [scale * first, scale * second, scale * cross[0], scale * cross[1]]
 
 
 def finish(got, k, *rest):
     fars, (x_far, send, basis, x, kv, surface, picked, sem) = rest[:11], rest[11:]
-    pairs = [(k, kv), (fars[0], basis.at[0])]
-    for p in range(2):
-        pairs += [(fars[1 + 5 * p + i], basis.at[1 + i, pl.ds(p * NF, NF)]) for i in range(5)]
+    pairs = []
+    for z in (0, 2):
+        part = pl.ds(z, 2)
+        pairs.append((k.at[part], kv.at[part]))
+        pairs.append((fars[0].at[:, part], basis.at[0, :, part]))
+        for p in range(2):
+            for i in range(5):
+                pairs.append((fars[1 + 5 * p + i].at[:, part], basis.at[1 + i, pl.ds(p * NF, NF), part]))
     copies = start_all(pairs, sem)
     sub = lax.broadcasted_iota(jnp.int32, (8, NY), 0)
     row = jnp.broadcast_to(jnp.sum(got[:, 0:NY], axis=0, keepdims=True), (8, NY))
@@ -487,32 +484,8 @@
         return cache[slot]
 
     coefs = coefficients(entry)
-    wait_all(copies)
-    outs = []
-    for p in range(2):
-        scal = [tuple(jnp.broadcast_to(part[p : p + 1, :], (8, NY)) for part in c) for c in coefs]
-
-        def block(z, _):
-            for xb in range(CX // 8):
-                rows = pl.ds(8 * xb, 8)
-                kz = kv[z, rows, :]
-                inv = 1.0 / (16.0 + kz * kz)
-                weight = (4.0 * inv, -kz * inv)
-                for f in range(p * NF, p * NF + NF, 2):
-                    terms = [cmul(scal[i], (basis[i, f, z, rows, :], basis[i, f + 1, z, rows, :])) for i in range(6)]
-                    y = cmul(weight, tree(terms))
-                    x[f, z, rows, :] = y[0]
-                    x[f + 1, z, rows, :] = y[1]
-            return 0
-
-        lax.fori_loop(0, NZL, block, 0)
-        part = pl.ds(p * NF, NF)
-        outs += start_all([(x.at[part], x_far.at[part])], sem, 12 + p)
-
-    for xb in range(CX // 8):
-        rows = pl.ds(8 * xb, 8)
-        for v, value in enumerate(impedance(x, 0, rows)):
-            surface[v * CX + 8 * xb : v * CX + 8 * xb + 8, :] = value
+    scal = [[tuple(jnp.broadcast_to(half[p : p + 1, :], (8, NY)) for half in c) for c in coefs] for p in range(2)]
+
     mine = pltpu.roll(got[:, NY : 2 * NY], lax.rem(NY - 32 * lax.axis_index("gx"), NY), 1).astype(jnp.int32)
     group = lax.broadcasted_iota(jnp.int32, (32, NY), 1) // 32
     cells = mine[0:32, :]
@@ -523,51 +496,79 @@
     cols = [col[8 * i : 8 * i + 8, :] for i in range(4)]
     lines = [line[8 * i : 8 * i + 8, :] for i in range(4)]
 
-    def value(v, _):
+    def layer(p, z):
+        for xb in range(CX // 8):
+            rows = pl.ds(8 * xb, 8)
+            kz = kv[z, rows, :]
+            inv = 1.0 / (16.0 + kz * kz)
+            weight = (4.0 * inv, -kz * inv)
+            for f in range(p * NF, p * NF + NF, 2):
+                terms = [cmul(scal[p][i], (basis[i, f, z, rows, :], basis[i, f + 1, z, rows, :])) for i in range(6)]
+                y = cmul(weight, tree(terms))
+                x[f, z, rows, :] = y[0]
+                x[f + 1, z, rows, :] = y[1]
+
+    outs = []
+
+    def leave(p, z, count):
+        part = pl.ds(p * NF, NF), pl.ds(z, count)
+        outs.extend(start_all([(x.at[part], x_far.at[part])], sem, len(pairs) + len(outs)))
+
+    half = len(pairs) // 2
+    wait_all(copies[:half])
+    for p in range(2):
+        for z in range(2):
+            layer(p, z)
+        leave(p, 0, 2)
+    for xb in range(CX // 8):
+        for v, value in enumerate(surface_power(x, pl.ds(8 * xb, 8))):
+            surface[v * CX + 8 * xb : v * CX + 8 * xb + 8, :] = value
+    wait_all(copies[half:])
+    for v in range(4):
         acc = [jnp.zeros((8, NY), f32)] * 4
         for r in range(CX):
-            src = jnp.broadcast_to(surface[pl.ds(v * CX + r, 1), :], (8, NY))
+            src = jnp.broadcast_to(surface[v * CX + r : v * CX + r + 1, :], (8, NY))
             for i in range(4):
                 hit = jnp.take_along_axis(src, cols[i], axis=1, mode="promise_in_bounds")
                 acc[i] = jnp.where(lines[i] == r, hit, acc[i])
         for i in range(4):
-            picked[pl.ds(pl.multiple_of(v * 32, 32) + 8 * i, 8), :] = acc[i]
-        return 0
-
-    lax.fori_loop(0, 8, value, 0)
+            picked[v * 32 + 8 * i : v * 32 + 8 * i + 8, :] = acc[i]
+        p, z = v // 2, 2 + v % 2
+        layer(p, z)
+        leave(p, z, 1)
     for e in range(4):
-        for h in range(2):
-            out = None
-            for w in range(4):
-                v = 4 * h + w
-                part = picked[v * 32 : v * 32 + 32, :]
-                if w != e:
-                    part = pltpu.roll(part, (32 * (w - e)) % NY, 1)
-                out = part if out is None else jnp.where(group == w, part, out)
-            send[32 * e : 32 * e + 32, NY * h : NY * h + NY] = out
+        out = None
+        for v in range(4):
+            part = picked[v * 32 : v * 32 + 32, :]
+            if v != e:
+                part = pltpu.roll(part, (32 * (v - e)) % NY, 1)
+            out = part if out is None else jnp.where(group == v, part, out)
+        send[32 * e : 32 * e + 32, :] = out
     wait_all(outs)
 
 
 def hazard_rows(got, spectra, scenario, out):
     scen = scenario.shape[1]
-    turned = []
-    for h in range(2):
-        block = got[0:8, NY * h : NY * h + NY]
-        turned.append(jnp.transpose(jnp.concatenate([block, jnp.zeros((NY - 8, NY), f32)], axis=0)))
-    b = [spectra[i : i + 1, :] for i in range(4)]
-    bx, by = (b[0], b[1]), (b[2], b[3])
+    block = jnp.concatenate([got[0:8, :], jnp.zeros((NY - 8, NY), f32)], axis=0)
+    turned = jnp.transpose(block)
+    xr, xi, yr, yi = [spectra[i : i + 1, :] for i in range(4)]
+    base = [
+        xr * xr + xi * xi,
+        yr * yr + yi * yi,
+        2.0 * (xr * yr + xi * yi),
+        2.0 * (xi * yr - xr * yi),
+    ]
     for j in range(4):
         weight = jnp.where(scenario[...] == j, 1.0, 0.25)
+        power = [weight * value for value in base]
         for qb in range(4):
-            z = []
-            for v in range(8):
-                first = (v % 4) * 32 + 8 * qb
-                z.append(jnp.broadcast_to(turned[v // 4][first : first + 8, j : j + 1], (8, scen)))
-            gx = cadd(cmul((z[0], z[1]), bx), cmul((z[2], z[3]), by))
-            gy = cadd(cmul((z[4], z[5]), bx), cmul((z[6], z[7]), by))
-            power = gx[0] * gx[0] + gx[1] * gx[1] + gy[0] * gy[0] + gy[1] * gy[1]
+            total = None
+            for v in range(4):
+                first = v * 32 + 8 * qb
+                term = jnp.broadcast_to(turned[first : first + 8, j : j + 1], (8, scen)) * power[v]
+                total = term if total is None else total + term
             row = 32 * j + 8 * qb
-            out[row : row + 8, :] = weight * power
+            out[row : row + 8, :] = total
 
 
 def partners(count):
@@ -587,11 +588,11 @@
     whole = (2 * NF, NZL, CX, NY)
     dma = pltpu.SemaphoreType.DMA
     space = pltpu.VMEM((NF, EZ, WX, NY), f32)
-    r = right_side.reshape(whole)
-    k = conductance
-    side = ((2 * NF + 1) * NZL * SIDE, NY)
-    rims = [pltpu.VMEM((2 * NF, NZL, 16, NY), f32), pltpu.VMEM((NZL, 16, NY), f32), dma((4,))]
-    near = exchange(*call(pack_x, [HBM] * 2, [(side, VM)] * 2, rims)(r, k), "gx")
+    r_far = right_side.reshape(whole)
+    side = (((2 * NF + 1) * NZL * SIDE, NY), VM)
+    loaded = [(whole, VM), ((NZL, CX, NY), VM)]
+    to_a, to_b, r, k = call(pack_x, [HBM] * 2, [side] * 2 + loaded, [dma((2,))])(r_far, conductance)
+    near = exchange(to_a, to_b, "gx")
     deep = [((n * REACH * (CX + 2 * SIDE), NY), VM) for n in (NF + 1, NF)]
     packed = call(pack_z, [VM] * 4, [deep[0]] * 2 + [deep[1]] * 2, moved=1 << 22)(r, k, *near)
     halo_0 = exchange(*packed[0:2], "gz")
@@ -603,18 +604,18 @@
         first_half_0,
         [VM] * 6,
         firsts + [((2, EZ, WX, NY), VM)],
-        [space] * 4 + [dma((2,)), pltpu.VMEM((EZ, WX, NY), f32)],
+        [space] * 5 + [dma((2,)), pltpu.VMEM((EZ, WX, NY), f32)],
         **cost,
     )(r, k, *near, *halo_0)
     halo_0 = exchange(to_a, to_b, "gz")
     *b_1, to_a, to_b, b1_1, b2_1 = call(
-        first_half_1, [VM] * 6, firsts, [space] * 4 + [dma((2,))], **cost
+        first_half_1, [VM] * 6, firsts, [space] * 5 + [dma((2,))], **cost
     )(r, m, *near, *halo_1)
     halo_1 = exchange(to_a, to_b, "gz")
     table = ((64, NY), VM)
     part_0, part_1 = call(low_gram, [VM] * 7, [table] * 2, **cost)(r, *b_0, *b_1)
     seconds = [(block, HBM)] * 3
-    spaces = [space] * 6 + [dma((3,))]
+    spaces = [space] * 7 + [dma((3,))]
     *high_0, total = call(
         second_half_0, [VM] * 8, seconds + [table], spaces, **cost
     )(r, *b_0, m, *halo_0, part_0)
@@ -625,20 +626,20 @@
         [pltpu.VMEM((64, NY), f32)] + spaces,
         **cost,
     )(r, *b_1, m, *halo_1, part_1, total, owned_cells[0])
-    held = (send, k, r, b1_0, b2_0, *high_0, b1_1, b2_1, *high_1)
+    held = (send, conductance, r_far, b1_0, b2_0, *high_0, b1_1, b2_1, *high_1)
     send, *fars = lax.optimization_barrier(held)
     got = lax.all_to_all(send, ("gz", "gx"), 0, 0, tiled=True)
     x, send = call(
         finish,
         [VM] + [HBM] * 12,
-        [(whole, HBM), ((128, 2 * NY), VM)],
+        [(whole, HBM), ((128, NY), VM)],
         [
             pltpu.VMEM((6, *whole), f32),
             pltpu.VMEM(whole, f32),
             pltpu.VMEM((NZL, CX, NY), f32),
-            pltpu.VMEM((8 * CX, NY), f32),
-            pltpu.VMEM((8 * CX, NY), f32),
-            dma((14,)),
+            pltpu.VMEM((4 * CX, NY), f32),
+            pltpu.VMEM((4 * CX, NY), f32),
+            dma((30,)),
         ],
     )(got, *fars)
     got = lax.all_to_all(send, ("gz", "gx"), 0, 0, tiled=True)

time: 103 us -> 95 us (0.922)
  Pallas kernels: 29.1 us -> 19 us
  blocking collectives: 37.7 us -> 39.8 us
  waiting for transfers between devices: 7.82 us -> 8.93 us
  starting transfers between devices: 23.7 us -> 22.6 us
    pallas_call x3, Pallas kernels: 11.6 us -> 7.46 us  [the longest x1 4.69 us: per_device(): call(finish, [VM] + [HBM] * 12, [(whole, HBM), ((128, NY), VM)], [pltpu.V...]
    all_to_all x2, blocking collectives: 37.7 us -> 39.8 us  [per_device(): got = lax.all_to_all(send, ('gz', 'gx'), 0, 0, tiled=True)]
    pallas_call x1, Pallas kernels: 4.62 us -> 2.74 us  [per_device(): call(first_half_0, [VM] * 6, firsts + [((2, EZ, WX, NY), VM)], [space] *...]
    pallas_call x1, Pallas kernels: 5.2 us -> 3.33 us  [per_device(): call(second_half_1, [VM] * 10, seconds + [((128, 2 * NY), VM)], [pltpu.VM...]
    pallas_call x1, Pallas kernels: 5.08 us -> 3.22 us  [per_device(): call(second_half_0, [VM] * 8, seconds + [table], spaces, **cost)]
    ppermute x10, waiting for transfers between devices: 7.82 us -> 8.93 us  [exchange(): return (lax.ppermute(to_a, axis, first), lax.ppermute(to_b, axis, second))]
    ppermute x10, starting transfers between devices: 23.7 us -> 22.6 us  [exchange(): return (lax.ppermute(to_a, axis, first), lax.ppermute(to_b, axis, second))]
    unnamed x12 -> x15, local copies, waits for them, and re-layouts: 3.34 us -> 3.35 us
  transfers between devices with their start and end apart: 10 -> 10, of which waited for: 2 -> 3; matrix products, arithmetic and copies ran while one was open for 0% -> 0% of each run, Pallas kernels for 15% -> 10%
where the time goes in v3:
time: 95 us; the launch traced here: 94.6 us
  blocking collectives  39.8 us (42%)
  starting transfers between devices  22.6 us (24%)
  Pallas kernels  19 us (20%)
  waiting for transfers between devices  8.93 us (9%)
  local copies, waits for them, and re-layouts  3.49 us (4%)
    all_to_all x2, blocking collectives, per_device(): got = lax.all_to_all(send, ('gz', 'gx'), 0, 0, tiled=True)  39.8 us
    ppermute x10, starting transfers between devices, exchange(): return (lax.ppermute(to_a, axis, first), lax.ppermute(to_b, axis, second))  22.6 us
    ppermute x10, waiting for transfers between devices, exchange(): return (lax.ppermute(to_a, axis, first), lax.ppermute(to_b, axis, second))  8.93 us
    pallas_call x1, Pallas kernels, per_device(): call(finish, [VM] + [HBM] * 12, [(whole, HBM), ((128, NY), VM)], [pltpu.V...  4.69 us
    unnamed x15, local copies, waits for them, and re-layouts  3.35 us
    pallas_call x1, Pallas kernels, per_device(): call(second_half_1, [VM] * 10, seconds + [((128, 2 * NY), VM)], [pltpu.VM...  3.33 us
    pallas_call x1, Pallas kernels, per_device(): call(second_half_0, [VM] * 8, seconds + [table], spaces, **cost)  3.22 us
    pallas_call x1, Pallas kernels, per_device(): call(first_half_0, [VM] * 6, firsts + [((2, EZ, WX, NY), VM)], [space] *...  2.74 us
  transfers between devices with their start and end apart: 10, of which 3 were waited for; matrix products, arithmetic and copies ran while one was open for 0% of the time, Pallas kernels for 10%

profile of v3, /device:TPU:1, one launch (start us, length us, event | category | flops | bytes accessed | tf_op | source)
XLA Modules:
  0.0 94.6 jit_solution(17992538148590960838)
XLA Ops:
  0.6 0.0 copy-start
  0.6 1.1 %copy-done = f32[2,3,2,4,32,128]{5,4,3,2,1,0:T(8,128)S(1)} copy-done((f32[2,3,2,4,32,128]{5,4,3,2,1,0:T(8,128)S(1)}, f32[2,3,2,4,32,128]{5,4,3,2,1,0:T(8,128)}, u32[]{:S(2)}) %copy-start) | copy-done | bytes 786456
  1.8 0.8 copy-done.2
  2.6 0.2 shard_map.68
  2.8 1.5 %collective-permute-start = (f32[312,128]{1,0:T(8,128)S(1)}, f32[312,128]{1,0:T(8,128)S(1)}, u32[]{:S(2)}, u32[]{:S(2)}) collective-permute-start(f32[312,128]{1,0:T(8,128)S(1)} %get-tuple-element.52), channel_id=1, source_target_pairs={{0,1},{1,0},{2,3},{3,2},{4,5},{5,4},{6,7},{7,6},{8,9},{9,8},{10,11... | collective-permute-start | bytes 479240 | tf_op jit(solution)/shard_map/ppermute | solution.py:582
  4.3 4.6 %collective-permute-start.1 = (f32[312,128]{1,0:T(8,128)S(1)}, f32[312,128]{1,0:T(8,128)S(1)}, u32[]{:S(2)}, u32[]{:S(2)}) collective-permute-start(f32[312,128]{1,0:T(8,128)S(1)} %get-tuple-element.53), channel_id=1, source_target_pairs={{1,2},{2,1},{5,6},{6,5},{9,10},{10,9},{13,14},{14,13},{17,18},{18,... | collective-permute-start | bytes 479240 | tf_op jit(solution)/shard_map/ppermute | solution.py:582
  9.0 3.4 %collective-permute-done.1.xb = f32[312,128]{1,0:T(8,128)S(1)} collective-permute-done((f32[312,128]{1,0:T(8,128)S(1)}, f32[312,128]{1,0:T(8,128)S(1)}, u32[]{:S(2)}, u32[]{:S(2)}) %collective-permute-start.1) | collective-permute-done | bytes 159776 | tf_op jit(solution)/shard_map/ppermute | solution.py:582
  12.4 0.1 shard_map.69
  12.6 1.5 %collective-permute-start.2 = (f32[924,128]{1,0:T(8,128)S(1)}, f32[924,128]{1,0:T(8,128)S(1)}, u32[]{:S(2)}, u32[]{:S(2)}) collective-permute-start(f32[924,128]{1,0:T(8,128)S(1)} %get-tuple-element.54), channel_id=1, source_target_pairs={{0,4},{4,0},{8,12},{12,8},{16,20},{20,16},{24,28},{28,24},{32,36},... | collective-permute-start | bytes 1419272 | tf_op jit(solution)/shard_map/ppermute | solution.py:582
  14.0 0.7 collective-permute-start.3
  14.7 3.6 %collective-permute-start.4 = (f32[792,128]{1,0:T(8,128)S(1)}, f32[792,128]{1,0:T(8,128)S(1)}, u32[]{:S(2)}, u32[]{:S(2)}) collective-permute-start(f32[792,128]{1,0:T(8,128)S(1)} %get-tuple-element.57), channel_id=1, source_target_pairs={{0,4},{4,0},{8,12},{12,8},{16,20},{20,16},{24,28},{28,24},{32,36},... | collective-permute-start | bytes 1216520 | tf_op jit(solution)/shard_map/ppermute | solution.py:582
  18.3 0.7 collective-permute-start.5
  19.0 5.3 %collective-permute-done.2.za = f32[924,128]{1,0:T(8,128)S(1)} collective-permute-done((f32[924,128]{1,0:T(8,128)S(1)}, f32[924,128]{1,0:T(8,128)S(1)}, u32[]{:S(2)}, u32[]{:S(2)}) %collective-permute-start.2) | collective-permute-done | bytes 473120 | tf_op jit(solution)/shard_map/ppermute | solution.py:582
  24.3 2.7 %shard_map.70 = (f32[6,4,32,128]{3,2,1,0:T(8,128)S(1)}, f32[6,4,32,128]{3,2,1,0:T(8,128)S(1)}, f32[6,4,48,128]{3,2,1,0:T(8,128)S(1)}, f32[684,128]{1,0:T(8,128)S...) custom-call(f32[12,4,32,128]{3,2,1,0:T(8,128)S(1)} %get-tuple-elemen, ...), custom_call_target="tpu_custom_call" | custom-call | flops 16777216 | bytes 8388608 | tf_op jit(solution)/shard_map/pallas_call | solution.py:603
  27.0 3.6 %collective-permute-start.8 = (f32[684,128]{1,0:T(8,128)S(1)}, f32[684,128]{1,0:T(8,128)S(1)}, u32[]{:S(2)}, u32[]{:S(2)}) collective-permute-start(f32[684,128]{1,0:T(8,128)S(1)} %get-tuple-element.68), channel_id=1, source_target_pairs={{0,4},{4,0},{8,12},{12,8},{16,20},{20,16},{24,28},{28,24},{32,36},... | collective-permute-start | bytes 1050632 | tf_op jit(solution)/shard_map/ppermute | solution.py:582
  30.6 0.7 collective-permute-start.9
  31.3 0.2 collective-permute-done.4.za
  31.5 2.6 %shard_map.71 = (f32[6,4,32,128]{3,2,1,0:T(8,128)S(1)}, f32[6,4,32,128]{3,2,1,0:T(8,128)S(1)}, f32[6,4,48,128]{3,2,1,0:T(8,128)S(1)}, f32[684,128]{1,0:T(8,128)S...) custom-call(f32[12,4,32,128]{3,2,1,0:T(8,128)S(1)} %get-tuple-element.50.r.b0, ...), custom_call_target="tpu_custom_call" | custom-call | flops 16777216 | bytes 8388608 | tf_op jit(solution)/shard_map/pallas_call | solution.py:611
  34.0 5.1 %collective-permute-start.6 = (f32[684,128]{1,0:T(8,128)S(1)}, f32[684,128]{1,0:T(8,128)S(1)}, u32[]{:S(2)}, u32[]{:S(2)}) collective-permute-start(f32[684,128]{1,0:T(8,128)S(1)} %get-tuple-element.62), channel_id=1, source_target_pairs={{0,4},{4,0},{8,12},{12,8},{16,20},{20,16},{24,28},{28,24},{32,36},... | collective-permute-start | bytes 1050632 | tf_op jit(solution)/shard_map/ppermute | solution.py:582
  39.2 0.7 collective-permute-start.7
  39.9 1.2 %shard_map.72 = (f32[64,128]{1,0:T(8,128)S(1)}, f32[64,128]{1,0:T(8,128)S(1)}) custom-call(f32[12,4,32,128]{3,2,1,0:T(8,128)S(1)} %get-tuple-element.50.r.b0, f32[6,4,32,128]{3,2,1,0:T(8,128)S(1)} %get-tuple-element.64.b1_0.b1, f32[6,4,32,128]{3,2,1,0:T(8,128)S(1)} %get-tuple-element.65.b2_0.b2, f32[6,4,48,128]{3,2,1,0:T(8,128)S(1)} %get-tuple-element.66.b3w_0.b3w, ...), custom_call_target="tpu_custom_call" | custom-call | flops 16777216 | bytes 8388608 | tf_op jit(solution)/shard_map/pallas_call | solution.py:616
  41.0 3.2 %shard_map.73 = (f32[6,4,32,128]{3,2,1,0:T(8,128)S(1)}, f32[6,4,32,128]{3,2,1,0:T(8,128)S(1)}, f32[6,4,32,128]{3,2,1,0:T(8,128)S(1)}, f32[64,128]{1,0:T(8,128)S(1)}) custom-call(f32[12,4,32,128]{3,2,1,0:T(8,128)S(1)} %get-tuple-element.50.r.b0, f32[6,4,32,128]{3,2,1,0:T(8,128)S(1)} %get-tuple-element.64.b1_0.b1, ...), custom_call_target="tpu_custom_call" | custom-call | flops 16777216 | bytes 8388608 | tf_op jit(solution)/shard_map/pallas_call | solution.py:619
  44.3 0.0 copy-start.5
  44.3 0.7 copy-done.5
  45.0 3.3 %shard_map.74 = (f32[6,4,32,128]{3,2,1,0:T(8,128)S(1)}, f32[6,4,32,128]{3,2,1,0:T(8,128)S(1)}, f32[6,4,32,128]{3,2,1,0:T(8,128)S(1)}, f32[128,256]{1,0:T(8,128)S(1)}) custom-call(f32[12,4,32,128]{3,2,1,0:T(8,128)S(1)} %get-tuple-element.50.r.b0, f32[6,4,32,128]{3,2,1,0:T(8,128)S(1)} %get-tuple-element.59.b1_1.b1, ...), custom_call_target="tpu_custom_call" | custom-call | flops 16777216 | bytes 8388608 | tf_op jit(solution)/shard_map/pallas_call | solution.py:622
  48.3 0.0 copy-start.1
  48.3 0.1 copy.7
  48.5 26.3 %all_to_all.22 = f32[128,1,256]{2,1,0:T(1,128)S(1)} all-to-all(f32[128,1,256]{2,1,0:T(1,128)S(1)} %copy.7), channel_id=1, replica_groups=mesh['gz'=32,'gx'=4] {'gz','gx'}, dimensions={0} | all-to-all | bytes 262144 | tf_op jit(solution)/shard_map/all_to_all | solution.py:631
  74.8 4.7 %shard_map.75 = (f32[12,4,32,128]{3,2,1,0:T(8,128)}, f32[128,128]{1,0:T(8,128)S(1)}) custom-call(f32[128,256]{1,0:T(8,128)S(1)} %bitcast.15, f32[4,32,128]{2,1,0:T(8,128)S(1)} %copy-done.3, f32[12,4,32,128]{3,2,1,0:T(8,128)S(1)} %bitcast.14, f32[6,4,32,128]{3,2,1,0:T(8,128)S(1)} %get-tuple-element.86.rest_1_, ...), custom_call_target="tpu_custom_call" | custom-call | tf_op jit(solution)/shard_map/pallas_call | solution.py:632
  79.5 13.5 %all_to_all.23 = f32[128,1,128]{2,1,0:T(1,128)S(1)} all-to-all(f32[128,1,128]{2,1,0:T(1,128)S(1)} %bitcast.18), channel_id=1, replica_groups=mesh['gz'=32,'gx'=4] {'gz','gx'}, dimensions={0} | all-to-all | bytes 131072 | tf_op jit(solution)/shard_map/all_to_all | solution.py:645
  93.0 0.7 copy-done.6
  93.7 1.0 %shard_map.76 = f32[128,512]{1,0:T(8,128)} custom-call(f32[128,128]{1,0:T(8,128)S(1)} %bitcast.16, f32[4,512]{1,0:T(4,128)S(1)} %bitcast.19, s32[1,512]{1,0:T(1,128)S(1)} %bitcast.21), custom_call_target="tpu_custom_call" | custom-call | tf_op jit(solution)/shard_map/pallas_call | solution.py:647
  (15 shorter events, 0.0 us)
Async XLA Ops:
  0.6 1.1 %copy-start = (f32[2,3,2,4,32,128]{5,4,3,2,1,0:T(8,128)S(1)}, f32[2,3,2,4,32,128]{5,4,3,2,1,0:T(8,128)}, u32[]{:S(2)}) copy-start(f32[2,3,2,4,32,128]{5,4,3,2,1,0:T(8,128)} %param.5) | copy-start | bytes 2359300
  1.8 0.8 copy-start.2
  2.8 6.1 %collective-permute-start = (f32[312,128]{1,0:T(8,128)S(1)}, f32[312,128]{1,0:T(8,128)S(1)}, u32[]{:S(2)}, u32[]{:S(2)}) collective-permute-start(f32[312,128]{1,0:T(8,128)S(1)} %get-tuple-element.52), channel_id=1, source_target_pairs={{0,1},{1,0},{2,3},{3,2},{4,5},{5,4},{6,7},{7,6},{8,9},{9,8},{10,11... | collective-permute-start | bytes 479240 | tf_op jit(solution)/shard_map/ppermute | solution.py:582
  4.3 8.1 %collective-permute-start.1 = (f32[312,128]{1,0:T(8,128)S(1)}, f32[312,128]{1,0:T(8,128)S(1)}, u32[]{:S(2)}, u32[]{:S(2)}) collective-permute-start(f32[312,128]{1,0:T(8,128)S(1)} %get-tuple-element.53), channel_id=1, source_target_pairs={{1,2},{2,1},{5,6},{6,5},{9,10},{10,9},{13,14},{14,13},{17,18},{18,... | collective-permute-start | bytes 479240 | tf_op jit(solution)/shard_map/ppermute | solution.py:582
  12.6 11.7 %collective-permute-start.2 = (f32[924,128]{1,0:T(8,128)S(1)}, f32[924,128]{1,0:T(8,128)S(1)}, u32[]{:S(2)}, u32[]{:S(2)}) collective-permute-start(f32[924,128]{1,0:T(8,128)S(1)} %get-tuple-element.54), channel_id=1, source_target_pairs={{0,4},{4,0},{8,12},{12,8},{16,20},{20,16},{24,28},{28,24},{32,36},... | collective-permute-start | bytes 1419272 | tf_op jit(solution)/shard_map/ppermute | solution.py:582
  14.0 10.2 %collective-permute-start.3 = (f32[924,128]{1,0:T(8,128)S(1)}, f32[924,128]{1,0:T(8,128)S(1)}, u32[]{:S(2)}, u32[]{:S(2)}) collective-permute-start(f32[924,128]{1,0:T(8,128)S(1)} %get-tuple-element.55), channel_id=1, source_target_pairs={{4,8},{8,4},{12,16},{16,12},{20,24},{24,20},{28,32},{32,28},{36,40... | collective-permute-start | bytes 1419272 | tf_op jit(solution)/shard_map/ppermute | solution.py:582
  14.7 16.8 %collective-permute-start.4 = (f32[792,128]{1,0:T(8,128)S(1)}, f32[792,128]{1,0:T(8,128)S(1)}, u32[]{:S(2)}, u32[]{:S(2)}) collective-permute-start(f32[792,128]{1,0:T(8,128)S(1)} %get-tuple-element.57), channel_id=1, source_target_pairs={{0,4},{4,0},{8,12},{12,8},{16,20},{20,16},{24,28},{28,24},{32,36},... | collective-permute-start | bytes 1216520 | tf_op jit(solution)/shard_map/ppermute | solution.py:582
  18.3 13.2 %collective-permute-start.5 = (f32[792,128]{1,0:T(8,128)S(1)}, f32[792,128]{1,0:T(8,128)S(1)}, u32[]{:S(2)}, u32[]{:S(2)}) collective-permute-start(f32[792,128]{1,0:T(8,128)S(1)} %get-tuple-element.58), channel_id=1, source_target_pairs={{4,8},{8,4},{12,16},{16,12},{20,24},{24,20},{28,32},{32,28},{36,40... | collective-permute-start | bytes 1216520 | tf_op jit(solution)/shard_map/ppermute | solution.py:582
  27.0 14.0 %collective-permute-start.8 = (f32[684,128]{1,0:T(8,128)S(1)}, f32[684,128]{1,0:T(8,128)S(1)}, u32[]{:S(2)}, u32[]{:S(2)}) collective-permute-start(f32[684,128]{1,0:T(8,128)S(1)} %get-tuple-element.68), channel_id=1, source_target_pairs={{0,4},{4,0},{8,12},{12,8},{16,20},{20,16},{24,28},{28,24},{32,36},... | collective-permute-start | bytes 1050632 | tf_op jit(solution)/shard_map/ppermute | solution.py:582
  30.6 10.5 %collective-permute-start.9 = (f32[684,128]{1,0:T(8,128)S(1)}, f32[684,128]{1,0:T(8,128)S(1)}, u32[]{:S(2)}, u32[]{:S(2)}) collective-permute-start(f32[684,128]{1,0:T(8,128)S(1)} %get-tuple-element.69), channel_id=1, source_target_pairs={{4,8},{8,4},{12,16},{16,12},{20,24},{24,20},{28,32},{32,28},{36,40... | collective-permute-start | bytes 1050632 | tf_op jit(solution)/shard_map/ppermute | solution.py:582
  34.0 10.2 %collective-permute-start.6 = (f32[684,128]{1,0:T(8,128)S(1)}, f32[684,128]{1,0:T(8,128)S(1)}, u32[]{:S(2)}, u32[]{:S(2)}) collective-permute-start(f32[684,128]{1,0:T(8,128)S(1)} %get-tuple-element.62), channel_id=1, source_target_pairs={{0,4},{4,0},{8,12},{12,8},{16,20},{20,16},{24,28},{28,24},{32,36},... | collective-permute-start | bytes 1050632 | tf_op jit(solution)/shard_map/ppermute | solution.py:582
  39.2 5.1 %collective-permute-start.7 = (f32[684,128]{1,0:T(8,128)S(1)}, f32[684,128]{1,0:T(8,128)S(1)}, u32[]{:S(2)}, u32[]{:S(2)}) collective-permute-start(f32[684,128]{1,0:T(8,128)S(1)} %get-tuple-element.63), channel_id=1, source_target_pairs={{4,8},{8,4},{12,16},{16,12},{20,24},{24,20},{28,32},{32,28},{36,40... | collective-permute-start | bytes 1050632 | tf_op jit(solution)/shard_map/ppermute | solution.py:582
  44.3 0.7 copy-start.5
  45.0 29.8 %copy-start.3 = (f32[4,32,128]{2,1,0:T(8,128)S(1)}, f32[4,32,128]{2,1,0:T(8,128)}, u32[]{:S(2)}) copy-start(f32[4,32,128]{2,1,0:T(8,128)} %k) | copy-start | bytes 196612
  48.3 26.5 %copy-start.1 = (f32[2,3,2,4,32,128]{5,4,3,2,1,0:T(8,128)S(1)}, f32[2,3,2,4,32,128]{5,4,3,2,1,0:T(8,128)}, u32[]{:S(2)}) copy-start(f32[2,3,2,4,32,128]{5,4,3,2,1,0:T(8,128)} %param.5) | copy-start | bytes 2359300
  79.5 13.5 %copy-start.4 = (f32[512,4]{0,1:T(4,128)S(1)}, f32[512,4]{0,1:T(4,128)}, u32[]{:S(2)}) copy-start(f32[512,4]{0,1:T(4,128)} %param.8) | copy-start | bytes 24580
  93.0 0.7 copy-start.6

commit v4 on v3

--- a/solution.py
+++ b/solution.py
@@ -14,23 +14,23 @@
 CX, NZL, NY = 32, 4, 128
 WX = 48
 EZ = NZL + 2 * REACH
-BACK = CX + 2 * REACH
 f32 = jnp.float32
 VM = pl.BlockSpec(memory_space=pltpu.VMEM)
 LIMIT = 14 * 1024 * 1024
+FIRST_LIMIT = 60 * 1024 * 1024
 
 
 HBM = pl.BlockSpec(memory_space=pltpu.HBM)
 
 
-def call(body, ins, outs, scratch=(), flops=0, moved=0):
+def call(body, ins, outs, scratch=(), flops=0, moved=0, limit=LIMIT):
     return pl.pallas_call(
         body,
         out_shape=[jax.ShapeDtypeStruct(shape, f32) for shape, _ in outs],
         in_specs=ins,
         out_specs=[spec for _, spec in outs],
         scratch_shapes=list(scratch),
-        compiler_params=pltpu.CompilerParams(vmem_limit_bytes=LIMIT),
+        compiler_params=pltpu.CompilerParams(vmem_limit_bytes=limit),
         cost_estimate=pl.CostEstimate(flops=flops, bytes_accessed=moved, transcendentals=0),
     )
 
@@ -61,18 +61,35 @@
         copy.wait()
 
 
-def pack_x(r_far, k_far, to_a, to_b, r, k, sem):
-    wait_all(start_all([(r_far, r), (k_far, k)], sem))
+def pack_x(r, k, spectra, scenario, to_a, to_b, power, rim, rim_k, spec, scen, sem):
+    pairs = []
+    for i in range(2):
+        src = pl.ds(i * (CX - 8), 8)
+        pairs.append((r.at[:, :, src, :], rim.at[:, :, pl.ds(8 * i, 8), :]))
+        pairs.append((k.at[:, src, :], rim_k.at[:, pl.ds(8 * i, 8), :]))
+    pairs += [(spectra, spec), (scenario, scen)]
+    wait_all(start_all(pairs, sem))
 
     def fill(up, down):
         for f in range(2 * NF + 1):
             for z in range(NZL):
                 row = (f * NZL + z) * SIDE
-                src = k.at[z] if f == 2 * NF else r.at[f, z]
-                up[row : row + SIDE, :] = src[CX - SIDE : CX, :]
+                src = rim_k.at[z] if f == 2 * NF else rim.at[f, z]
+                up[row : row + SIDE, :] = src[16 - SIDE : 16, :]
                 down[row : row + SIDE, :] = src[0:SIDE, :]
 
     either(odd("gx"), fill, to_a, to_b)
+    xr, xi, yr, yi = [spec[i : i + 1, :] for i in range(4)]
+    base = [
+        xr * xr + xi * xi,
+        yr * yr + yi * yi,
+        2.0 * (xr * yr + xi * yi),
+        2.0 * (xi * yr - xr * yi),
+    ]
+    for j in range(4):
+        weight = jnp.where(scen[...] == j, 1.0, 0.25)
+        for v in range(4):
+            power[4 * j + v : 4 * j + v + 1, :] = weight * base[v]
 
 
 def sides(from_a, from_b, near):
@@ -81,25 +98,132 @@
     return jnp.where(flag, a, b), jnp.where(flag, b, a)
 
 
-def pack_z(r, k, xa, xb, a_0, b_0, a_1, b_1):
-    width = CX + 2 * SIDE
+def spans(margin):
+    low, high = margin + REACH, CX - 1 + margin
+    below = ((1 - low, high + 3), (2 - low, high + 3), (3 - low, high + 2))
+    above = ((-low, high + 2), (-low, high + 1), (-low, high))
+    return below, above
+
+
+def layout(span, with_k):
+    near, row = {}, 0
+    for i in range(REACH - 1):
+        for f in range(NF):
+            near[i, f] = row
+            row += span[i][1] - span[i][0] + 1
+    far = []
+    for _ in range(4):
+        far.append(row)
+        row += span[-1][1] - span[-1][0] + 1
+    k = []
+    for i in range(REACH - 1 if with_k else 0):
+        k.append(row)
+        row += span[i][1] - span[i][0] + 1
+    return near, far, k, row
+
+
+def rows_of(margin, with_k):
+    return max(layout(span, with_k)[3] for span in spans(margin))
+
+
+def cut(span):
+    return slice(8 + span[0], 9 + span[1]), span[1] - span[0] + 1
+
+
+def far_fields(b, first, weight, far):
+    _, last = lanes()
+
+    def y(z, c):
+        mr, mi = weight(z)
+        re, im = b[2 * c, first + z], b[2 * c + 1, first + z]
+        return mr * re - mi * im, mr * im + mi * re
+
+    ex, ey, ez = [y(NZL - REACH, c) for c in range(3)]
+    for q in range(2):
+        far[q] = ex[q] + (next_x(ez[q]) - ez[q])
+        far[2 + q] = ey[q] + (next_y(ez[q], last) - ez[q])
+    for c in range(2):
+        far[4 + 2 * c], far[5 + 2 * c] = y(REACH - 1, c)
+
+
+def fill_messages(b, first, far, k, margin, up, down):
+    for side, (out, span) in enumerate(zip((up, down), spans(margin))):
+        near, far_rows, k_rows, _ = layout(span, k is not None)
+        for i in range(REACH - 1):
+            z = first + (NZL - 1 - i if side == 0 else i)
+            cols, n = cut(span[i])
+            for f in range(NF):
+                out[near[i, f] : near[i, f] + n, :] = b[f, z, cols, :]
+            if k is not None:
+                out[k_rows[i] : k_rows[i] + n, :] = k[z, cols, :]
+        cols, n = cut(span[-1])
+        for j, row in enumerate(far_rows):
+            out[row : row + n, :] = far[4 * side + j, cols, :]
+
+
+def take_messages(b, y, k, margin, above, below):
+    for side, (src, span) in enumerate(zip((below, above), spans(margin))):
+        near, far_rows, k_rows, _ = layout(span, k is not None)
+        for i in range(REACH - 1):
+            z = REACH - 1 - i if side == 0 else REACH + NZL + i
+            cols, n = cut(span[i])
+            for f in range(NF):
+                b[f, z, cols, :] = src[near[i, f] : near[i, f] + n, :]
+            if k is not None:
+                k[z, cols, :] = src[k_rows[i] : k_rows[i] + n, :]
+        cols, n = cut(span[-1])
+        z = 0 if side == 0 else EZ - 1
+        for j, row in enumerate(far_rows):
+            y[j, z, cols, :] = src[row : row + n, :]
+
+
+def clear_sides(ref):
+    zero = jnp.zeros((EZ, 8, NY), f32)
+    ref[:, 0:8, :] = zero
+    ref[:, WX - 8 : WX, :] = zero
+
+
+def clear_far(y):
+    for f in range(NF):
+        for z in (0, EZ - 1):
+            if f < 4:
+                y[f, z, 0:8, :] = jnp.zeros((8, NY), f32)
+                y[f, z, WX - 8 : WX, :] = jnp.zeros((8, NY), f32)
+            else:
+                y[f, z] = jnp.zeros((WX, NY), f32)
+
+
+def own_layers(dst, first, src, xa, xb, near):
+    for z in range(NZL):
+        left, right = sides(xa, xb, (near * NZL + z) * SIDE)
+        dst[first + z, 8 - SIDE : 8, :] = left
+        dst[first + z, 8 : 8 + CX, :] = src[z]
+        dst[first + z, 8 + CX : 8 + CX + SIDE, :] = right
+
+
+def weight_of(kz):
+    inv = jnp.where(kz > 0.0, 1.0, 0.0) / (16.0 + kz * kz)
+    return 4.0 * inv, -kz * inv
+
+
+def pack_z(r, k, xa, xb, owned, a_0, b_0, a_1, b_1, cells, b, kx, far):
+    for f in range(2 * NF + 1):
+        dst = kx if f == 2 * NF else b.at[f]
+        zero = jnp.zeros((NZL, 8, NY), f32)
+        dst[:, 0:8, :] = zero
+        dst[:, WX - 8 : WX, :] = zero
+        own_layers(dst, 0, k if f == 2 * NF else r.at[f], xa, xb, f)
+    weights = {z: weight_of(kx[z]) for z in (NZL - REACH, REACH - 1)}
+    for p in range(2):
+        far_fields(b.at[pl.ds(p * NF, NF)], 0, lambda z: weights[z], far.at[p])
 
     def fill(first, second):
-        outs = [((first[p], NZL - REACH), (second[p], 0)) for p in range(2)]
         for p in range(2):
-            fields = [p * NF + i for i in range(NF)] + ([2 * NF] if p == 0 else [])
-            for at, f in enumerate(fields):
-                for z in range(NZL):
-                    left, right = sides(xa, xb, (f * NZL + z) * SIDE)
-                    src = k.at[z] if f == 2 * NF else r.at[f, z]
-                    for out, low in outs[p]:
-                        if low <= z < low + REACH:
-                            row = (at * REACH + z - low) * width
-                            out[row : row + SIDE, :] = left
-                            out[row + SIDE : row + SIDE + CX, :] = src[:, :]
-                            out[row + SIDE + CX : row + width, :] = right
+            own = b.at[pl.ds(p * NF, NF)]
+            fill_messages(own, 0, far.at[p], kx if p == 0 else None, REACH, first[p], second[p])
 
     either(odd("gz"), fill, (a_0, a_1), (b_0, b_1))
+    cells[...] = jnp.concatenate([owned[j : j + 1, :] for j in range(4)], axis=1).astype(f32)
 
 
 def lanes():
@@ -158,43 +282,7 @@
         smooth(b, y, m, 0, z)
         return 0
 
-    lax.fori_loop(0, EZ, layer, 0)
-
-
-def weights(k, xa, xb, za, zb, m, kx):
-    extend([kx], [k], xa, xb, za, zb, 2 * NF, NF)
-
-    def layer(z, _):
-        kz = kx[z]
-        inv = jnp.where(kz > 0.0, 1.0, 0.0) / (16.0 + kz * kz)
-        m[0, z] = 4.0 * inv
-        m[1, z] = -kz * inv
-        return 0
-
-    lax.fori_loop(0, EZ, layer, 0)
-
-
-def extend(outs, srcs, xa, xb, za, zb, near, far):
-    width = CX + 2 * SIDE
-    x0 = 8 - SIDE
-    zero = jnp.zeros((EZ, 8, NY), f32)
-    for i, (dst, src) in enumerate(zip(outs, srcs)):
-        dst[:, 0:8, :] = zero
-        dst[:, WX - 8 : WX, :] = zero
-        for z in range(NZL):
-            left, right = sides(xa, xb, ((near + i) * NZL + z) * SIDE)
-            dst[REACH + z, x0:8, :] = left
-            dst[REACH + z, 8 : 8 + CX, :] = src[z]
-            dst[REACH + z, 8 + CX : 8 + CX + SIDE, :] = right
-
-    def fill(above, below):
-        for i, dst in enumerate(outs):
-            for z in range(REACH):
-                row = ((far + i) * REACH + z) * width
-                dst[z, x0 : x0 + width, :] = below[row : row + width, :]
-                dst[REACH + NZL + z, x0 : x0 + width, :] = above[row : row + width, :]
-
-    either(odd("gz"), fill, za, zb)
+    lax.fori_loop(1, EZ - 1, layer, 0)
 
 
 def keep(src, out):
@@ -205,9 +293,26 @@
     lax.fori_loop(0, NF, field, 0)
 
 
-def first_steps(p, r, xa, xb, za, zb, b1, b2, b3w, to_a, to_b, b1_far, b2_far, m, ba, bb, ya, yb, hs, sem):
-    fields = range(NF)
-    extend([ba.at[f] for f in fields], [r.at[p * NF + f] for f in fields], xa, xb, za, zb, p * NF, 0)
+def first_steps(p, r, k, kx, xa, xb, za, zb, b1, b2, b3w, to_a, to_b, b1_far, b2_far, m, ba, bb, ya, yb, hs, far, sem):
+    for f in range(NF):
+        clear_sides(ba.at[f])
+        own_layers(ba.at[f], REACH, r.at[p * NF + f], xa, xb, p * NF + f)
+    clear_far(ya)
+    if p == 0:
+        clear_sides(kx)
+        own_layers(kx, REACH, k, xa, xb, 2 * NF)
+
+    def take(above, below):
+        take_messages(ba, ya, kx if p == 0 else None, REACH, above, below)
+
+    either(odd("gz"), take, za, zb)
+    if p == 0:
+
+        def layer(z, _):
+            m[0, z], m[1, z] = weight_of(kx[z])
+            return 0
+
+        lax.fori_loop(1, EZ - 1, layer, 0)
     all_smooth(ba, ya, m)
     apply_k(ba, ya, bb, yb, hs, m, 1, EZ - 1, SHIFTS[0], True)
     keep(bb, b1)
@@ -216,28 +321,19 @@
     keep(ba, b2)
     copies += start_all([(b2, b2_far)], sem, 1)
     apply_k(ba, ya, bb, yb, hs, m, 3, EZ - 3, SHIFTS[2], False)
-    cut = (WX - BACK) // 2
-    for f in fields:
+    for f in range(NF):
         b3w[f] = bb[f, REACH : REACH + NZL]
-
-    def fill(up, down):
-        for f in fields:
-            for z in range(REACH):
-                row = (f * REACH + z) * BACK
-                up[row : row + BACK, :] = bb[f, NZL + z, cut : cut + BACK, :]
-                down[row : row + BACK, :] = bb[f, REACH + z, cut : cut + BACK, :]
-
-    either(odd("gz"), fill, to_a, to_b)
+    far_fields(bb, REACH, lambda z: (m[0, REACH + z], m[1, REACH + z]), far)
+    either(odd("gz"), lambda up, down: fill_messages(bb, REACH, far, None, 0, up, down), to_a, to_b)
     wait_all(copies)
 
 
-def first_half_0(r, k, xa, xb, za, zb, b1, b2, b3w, to_a, to_b, b1_far, b2_far, m, ba, bb, ya, yb, hs, sem, kx):
-    weights(k, xa, xb, za, zb, m, kx)
-    first_steps(0, r, xa, xb, za, zb, b1, b2, b3w, to_a, to_b, b1_far, b2_far, m, ba, bb, ya, yb, hs, sem)
-
-
-def first_half_1(r, m, xa, xb, za, zb, b1, b2, b3w, to_a, to_b, b1_far, b2_far, ba, bb, ya, yb, hs, sem):
-    first_steps(1, r, xa, xb, za, zb, b1, b2, b3w, to_a, to_b, b1_far, b2_far, m, ba, bb, ya, yb, hs, sem)
+def first_half_0(r, k, xa, xb, za, zb, b1, b2, b3w, to_a, to_b, b1_far, b2_far, m, kx, *space):
+    first_steps(0, r, k, kx, xa, xb, za, zb, b1, b2, b3w, to_a, to_b, b1_far, b2_far, m, *space)
+
+
+def first_half_1(r, m, xa, xb, za, zb, b1, b2, b3w, to_a, to_b, b1_far, b2_far, *space):
+    first_steps(1, r, None, None, xa, xb, za, zb, b1, b2, b3w, to_a, to_b, b1_far, b2_far, m, *space)
 
 
 PAIRS = [(i, j) for i in range(7) for j in range(i, 7)]
@@ -296,25 +392,14 @@
 
 
 def second_steps(p, b0, b1, b2, b3w, m, za, zb, part, b3_far, b4_far, b5_far, total, ba, bb, bc, bd, ya, yb, hs, sem):
-    cut = (WX - BACK) // 2
     own = pl.ds(REACH, NZL)
     mid = pl.ds(8, CX)
     copies = start_all([(b3w.at[:, :, mid, :], b3_far)], sem)
-    zero = jnp.zeros((REACH, 8, NY), f32)
     for f in range(NF):
-        for first in (0, REACH + NZL):
-            ba[f, first : first + REACH, 0:8, :] = zero
-            ba[f, first : first + REACH, WX - 8 : WX, :] = zero
+        clear_sides(ba.at[f])
         ba[f, REACH : REACH + NZL] = b3w[f]
-
-    def fill(above, below):
-        for f in range(NF):
-            for z in range(REACH):
-                row = (f * REACH + z) * BACK
-                ba[f, z, cut : cut + BACK, :] = below[row : row + BACK, :]
-                ba[f, REACH + NZL + z, cut : cut + BACK, :] = above[row : row + BACK, :]
-
-    either(odd("gz"), fill, za, zb)
+    clear_far(ya)
+    either(odd("gz"), lambda above, below: take_messages(ba, ya, None, 0, above, below), za, zb)
     all_smooth(ba, ya, m)
     apply_k(ba, ya, bb, yb, hs, m, 1, EZ - 1, SHIFTS[3], True)
     copies += start_all([(bb.at[:, own, mid, :], b4_far)], sem, 1)
@@ -330,12 +415,11 @@
     second_steps(0, b0, b1, b2, b3w, m, za, zb, part, b3_far, b4_far, b5_far, total, *space)
 
 
-def second_half_1(b0, b1, b2, b3w, m, za, zb, part, other, owned, b3_far, b4_far, b5_far, send, total, *space):
+def second_half_1(b0, b1, b2, b3w, m, za, zb, part, other, cells, b3_far, b4_far, b5_far, send, total, *space):
     second_steps(1, b0, b1, b2, b3w, m, za, zb, part, b3_far, b4_far, b5_far, total, *space)
     both = jnp.concatenate([other[...], total[...]], axis=0)
     sums = jnp.sum(jnp.transpose(both), axis=0, keepdims=True)
-    cells = jnp.concatenate([owned[j : j + 1, :] for j in range(4)], axis=1).astype(f32)
-    send[...] = jnp.broadcast_to(jnp.concatenate([sums, cells], axis=1), (128, 2 * NY))
+    send[...] = jnp.broadcast_to(jnp.concatenate([sums, cells[...]], axis=1), (128, 2 * NY))
 
 
 def cadd(a, b):
@@ -463,16 +547,7 @@
 
 
 def finish(got, k, *rest):
-    fars, (x_far, send, basis, x, kv, surface, picked, sem) = rest[:11], rest[11:]
-    pairs = []
-    for z in (0, 2):
-        part = pl.ds(z, 2)
-        pairs.append((k.at[part], kv.at[part]))
-        pairs.append((fars[0].at[:, part], basis.at[0, :, part]))
-        for p in range(2):
-            for i in range(5):
-                pairs.append((fars[1 + 5 * p + i].at[:, part], basis.at[1 + i, pl.ds(p * NF, NF), part]))
-    copies = start_all(pairs, sem)
+    fars, (x_far, send, x, surface, picked, sem) = rest[:11], rest[11:]
     sub = lax.broadcasted_iota(jnp.int32, (8, NY), 0)
     row = jnp.broadcast_to(jnp.sum(got[:, 0:NY], axis=0, keepdims=True), (8, NY))
     table = jnp.where(sub == 0, row, pltpu.roll(row, 64, 1))
@@ -499,23 +574,26 @@
     def layer(p, z):
         for xb in range(CX // 8):
             rows = pl.ds(8 * xb, 8)
-            kz = kv[z, rows, :]
+            kz = k[z, rows, :]
             inv = 1.0 / (16.0 + kz * kz)
             weight = (4.0 * inv, -kz * inv)
             for f in range(p * NF, p * NF + NF, 2):
-                terms = [cmul(scal[p][i], (basis[i, f, z, rows, :], basis[i, f + 1, z, rows, :])) for i in range(6)]
+                terms = [cmul(scal[p][i], (basis(i, f, z, rows), basis(i, f + 1, z, rows))) for i in range(6)]
                 y = cmul(weight, tree(terms))
                 x[f, z, rows, :] = y[0]
                 x[f + 1, z, rows, :] = y[1]
 
+    def basis(i, f, z, rows):
+        if i == 0:
+            return fars[0][f, z, rows, :]
+        return fars[5 * (f // NF) + i][f % NF, z, rows, :]
+
     outs = []
 
     def leave(p, z, count):
         part = pl.ds(p * NF, NF), pl.ds(z, count)
-        outs.extend(start_all([(x.at[part], x_far.at[part])], sem, len(pairs) + len(outs)))
-
-    half = len(pairs) // 2
-    wait_all(copies[:half])
+        outs.extend(start_all([(x.at[part], x_far.at[part])], sem, len(outs)))
+
     for p in range(2):
         for z in range(2):
             layer(p, z)
@@ -523,17 +601,16 @@
     for xb in range(CX // 8):
         for v, value in enumerate(surface_power(x, pl.ds(8 * xb, 8))):
             surface[v * CX + 8 * xb : v * CX + 8 * xb + 8, :] = value
-    wait_all(copies[half:])
-    for v in range(4):
+    for i in range(4):
         acc = [jnp.zeros((8, NY), f32)] * 4
         for r in range(CX):
-            src = jnp.broadcast_to(surface[v * CX + r : v * CX + r + 1, :], (8, NY))
-            for i in range(4):
+            for v in range(4):
+                src = jnp.broadcast_to(surface[v * CX + r : v * CX + r + 1, :], (8, NY))
                 hit = jnp.take_along_axis(src, cols[i], axis=1, mode="promise_in_bounds")
-                acc[i] = jnp.where(lines[i] == r, hit, acc[i])
-        for i in range(4):
-            picked[v * 32 + 8 * i : v * 32 + 8 * i + 8, :] = acc[i]
-        p, z = v // 2, 2 + v % 2
+                acc[v] = jnp.where(lines[i] == r, hit, acc[v])
+        for v in range(4):
+            picked[v * 32 + 8 * i : v * 32 + 8 * i + 8, :] = acc[v]
+        p, z = i // 2, 2 + i % 2
         layer(p, z)
         leave(p, z, 1)
     for e in range(4):
@@ -547,25 +624,16 @@
     wait_all(outs)
 
 
-def hazard_rows(got, spectra, scenario, out):
-    scen = scenario.shape[1]
+def hazard_rows(got, power, out):
     block = jnp.concatenate([got[0:8, :], jnp.zeros((NY - 8, NY), f32)], axis=0)
     turned = jnp.transpose(block)
-    xr, xi, yr, yi = [spectra[i : i + 1, :] for i in range(4)]
-    base = [
-        xr * xr + xi * xi,
-        yr * yr + yi * yi,
-        2.0 * (xr * yr + xi * yi),
-        2.0 * (xi * yr - xr * yi),
-    ]
     for j in range(4):
-        weight = jnp.where(scenario[...] == j, 1.0, 0.25)
-        power = [weight * value for value in base]
         for qb in range(4):
             total = None
             for v in range(4):
                 first = v * 32 + 8 * qb
-                term = jnp.broadcast_to(turned[first : first + 8, j : j + 1], (8, scen)) * power[v]
+                column = jnp.broadcast_to(turned[first : first + 8, j : j + 1], (8, power.shape[1]))
+                term = column * power[4 * j + v : 4 * j + v + 1, :]
                 total = term if total is None else total + term
             row = 32 * j + 8 * qb
             out[row : row + 8, :] = total
@@ -590,26 +658,47 @@
     space = pltpu.VMEM((NF, EZ, WX, NY), f32)
     r_far = right_side.reshape(whole)
     side = (((2 * NF + 1) * NZL * SIDE, NY), VM)
-    loaded = [(whole, VM), ((NZL, CX, NY), VM)]
-    to_a, to_b, r, k = call(pack_x, [HBM] * 2, [side] * 2 + loaded, [dma((2,))])(r_far, conductance)
+    scen = spectra.shape[0]
+    rims = [
+        pltpu.VMEM((2 * NF, NZL, 16, NY), f32),
+        pltpu.VMEM((NZL, 16, NY), f32),
+        pltpu.VMEM((4, scen), f32),
+        pltpu.VMEM((1, scen), jnp.int32),
+        dma((6,)),
+    ]
+    to_a, to_b, power = call(
+        pack_x, [HBM] * 4, [side] * 2 + [((16, scen), VM)], rims, limit=FIRST_LIMIT
+    )(r_far, conductance, spectra.T, scenario_tile.reshape(1, scen))
+    r, k = r_far, conductance
     near = exchange(to_a, to_b, "gx")
-    deep = [((n * REACH * (CX + 2 * SIDE), NY), VM) for n in (NF + 1, NF)]
-    packed = call(pack_z, [VM] * 4, [deep[0]] * 2 + [deep[1]] * 2, moved=1 << 22)(r, k, *near)
+    deep = [((rows_of(REACH, with_k), NY), VM) for with_k in (True, False)]
+    *packed, cells = call(
+        pack_z,
+        [VM] * 5,
+        [deep[0]] * 2 + [deep[1]] * 2 + [((1, NY), VM)],
+        [
+            pltpu.VMEM((2 * NF, NZL, WX, NY), f32),
+            pltpu.VMEM((NZL, WX, NY), f32),
+            pltpu.VMEM((2, 8, WX, NY), f32),
+        ],
+        moved=1 << 22,
+    )(r, k, *near, owned_cells[0])
     halo_0 = exchange(*packed[0:2], "gz")
     halo_1 = exchange(*packed[2:4], "gz")
-    back = ((NF * REACH * BACK, NY), VM)
+    back = ((rows_of(0, False), NY), VM)
+    far = pltpu.VMEM((8, WX, NY), f32)
     firsts = [(block, VM), (block, VM), (wide, VM), back, back, (block, HBM), (block, HBM)]
     cost = {"flops": 1 << 24, "moved": 1 << 23}
     *b_0, to_a, to_b, b1_0, b2_0, m = call(
         first_half_0,
         [VM] * 6,
         firsts + [((2, EZ, WX, NY), VM)],
-        [space] * 5 + [dma((2,)), pltpu.VMEM((EZ, WX, NY), f32)],
+        [pltpu.VMEM((EZ, WX, NY), f32)] + [space] * 5 + [far, dma((2,))],
         **cost,
     )(r, k, *near, *halo_0)
     halo_0 = exchange(to_a, to_b, "gz")
     *b_1, to_a, to_b, b1_1, b2_1 = call(
-        first_half_1, [VM] * 6, firsts, [space] * 5 + [dma((2,))], **cost
+        first_half_1, [VM] * 6, firsts, [space] * 5 + [far, dma((2,))], **cost
     )(r, m, *near, *halo_1)
     halo_1 = exchange(to_a, to_b, "gz")
     table = ((64, NY), VM)
@@ -625,26 +714,23 @@
         seconds + [((128, 2 * NY), VM)],
         [pltpu.VMEM((64, NY), f32)] + spaces,
         **cost,
-    )(r, *b_1, m, *halo_1, part_1, total, owned_cells[0])
+    )(r, *b_1, m, *halo_1, part_1, total, cells)
     held = (send, conductance, r_far, b1_0, b2_0, *high_0, b1_1, b2_1, *high_1)
     send, *fars = lax.optimization_barrier(held)
     got = lax.all_to_all(send, ("gz", "gx"), 0, 0, tiled=True)
     x, send = call(
         finish,
-        [VM] + [HBM] * 12,
+        [VM] * 13,
         [(whole, HBM), ((128, NY), VM)],
         [
-            pltpu.VMEM((6, *whole), f32),
             pltpu.VMEM(whole, f32),
-            pltpu.VMEM((NZL, CX, NY), f32),
             pltpu.VMEM((4 * CX, NY), f32),
             pltpu.VMEM((4 * CX, NY), f32),
-            dma((30,)),
+            dma((6,)),
         ],
     )(got, *fars)
     got = lax.all_to_all(send, ("gz", "gx"), 0, 0, tiled=True)
-    scen = spectra.shape[0]
-    (hazard,) = call(hazard_rows, [VM] * 3, [((128, scen), VM)])(got, spectra.T, scenario_tile.reshape(1, scen))
+    (hazard,) = call(hazard_rows, [VM] * 2, [((128, scen), VM)])(got, power)
     return x.reshape(right_side.shape), hazard
 
 

time: 95 us -> 87.3 us (0.919)
  local copies, waits for them, and re-layouts: 3.49 us -> 0.16 us
  waiting for transfers between devices: 8.93 us -> 5.89 us
  blocking collectives: 39.8 us -> 38.7 us
    unnamed x15 -> x9, local copies, waits for them, and re-layouts: 3.35 us -> 0.03 us
    ppermute x10, waiting for transfers between devices: 8.93 us -> 5.89 us  [exchange(): return (lax.ppermute(to_a, axis, first), lax.ppermute(to_b, axis, second))]
    all_to_all x2, blocking collectives: 39.8 us -> 38.7 us  [per_device(): got = lax.all_to_all(send, ('gz', 'gx'), 0, 0, tiled=True)]
  transfers between devices with their start and end apart: 10 -> 10, of which waited for: 3 -> 2; matrix products, arithmetic and copies ran while one was open for 0% -> 0% of each run, Pallas kernels for 10% -> 11%
where the time goes in v4:
time: 87.3 us; the launch traced here: 87 us
  blocking collectives  38.7 us (44%)
  starting transfers between devices  23.3 us (27%)
  Pallas kernels  18.1 us (21%)
  waiting for transfers between devices  5.89 us (7%)
    all_to_all x2, blocking collectives, per_device(): got = lax.all_to_all(send, ('gz', 'gx'), 0, 0, tiled=True)  38.7 us
    ppermute x10, starting transfers between devices, exchange(): return (lax.ppermute(to_a, axis, first), lax.ppermute(to_b, axis, second))  23.3 us
    ppermute x10, waiting for transfers between devices, exchange(): return (lax.ppermute(to_a, axis, first), lax.ppermute(to_b, axis, second))  5.89 us
    pallas_call x1, Pallas kernels, per_device(): call(second_half_1, [VM] * 10, seconds + [((128, 2 * NY), VM)], [pltpu.VM...  3.29 us
    pallas_call x1, Pallas kernels, per_device(): call(second_half_0, [VM] * 8, seconds + [table], spaces, **cost)  3.17 us
    pallas_call x1, Pallas kernels, per_device(): call(first_half_0, [VM] * 6, firsts + [((2, EZ, WX, NY), VM)], [pltpu.VME...  2.67 us
    pallas_call x1, Pallas kernels, per_device(): call(first_half_1, [VM] * 6, firsts, [space] * 5 + [far, dma((2,))], **cost)  2.54 us
    pallas_call x1, Pallas kernels, per_device(): call(finish, [VM] * 13, [(whole, HBM), ((128, NY), VM)], [pltpu.VMEM(whol...  1.97 us
  transfers between devices with their start and end apart: 10, of which 2 were waited for; matrix products, arithmetic and copies ran while one was open for 0% of the time, Pallas kernels for 11%

profile of v4, /device:TPU:1, one launch (start us, length us, event | category | flops | bytes accessed | tf_op | source)
XLA Modules:
  0.0 87.0 jit_solution(6186345409057292420)
XLA Ops:
  0.7 1.9 %shard_map.68 = (f32[312,128]{1,0:T(8,128)}, f32[312,128]{1,0:T(8,128)}, f32[16,512]{1,0:T(8,128)}) custom-call(f32[12,4,32,128]{3,2,1,0:T(8,128)} %bitcast.13, f32[4,32,128]{2,1,0:T(8,128)} %k.6, f32[4,512]{1,0:T(4,128)} %bitcast.26, s32[1,512]{1,0:T(1,128)} %bitcast.27), custom_call_target="tpu_custom_call" | custom-call | tf_op jit(solution)/shard_map/pallas_call | solution.py:669
  2.6 0.0 copy-start.3
  2.6 1.5 %collective-permute-start = (f32[312,128]{1,0:T(8,128)}, f32[312,128]{1,0:T(8,128)S(1)}, u32[]{:S(2)}, u32[]{:S(2)}) collective-permute-start(f32[312,128]{1,0:T(8,128)} %get-tuple-element.50), channel_id=1, source_target_pairs={{0,1},{1,0},{2,3},{3,2},{4,5},{5,4},{6,7},{7,6},{8,9},{9,8},{10,11... | collective-permute-start | bytes 479240 | tf_op jit(solution)/shard_map/ppermute | solution.py:650
  4.1 4.6 %collective-permute-start.1 = (f32[312,128]{1,0:T(8,128)}, f32[312,128]{1,0:T(8,128)S(1)}, u32[]{:S(2)}, u32[]{:S(2)}) collective-permute-start(f32[312,128]{1,0:T(8,128)} %get-tuple-element.51), channel_id=1, source_target_pairs={{1,2},{2,1},{5,6},{6,5},{9,10},{10,9},{13,14},{14,13},{17,18},{18,... | collective-permute-start | bytes 479240 | tf_op jit(solution)/shard_map/ppermute | solution.py:650
  8.7 0.0 collective-permute-done.xa
  8.8 3.6 %collective-permute-done.1.xb = f32[312,128]{1,0:T(8,128)S(1)} collective-permute-done((f32[312,128]{1,0:T(8,128)}, f32[312,128]{1,0:T(8,128)S(1)}, u32[]{:S(2)}, u32[]{:S(2)}) %collective-permute-start.1) | collective-permute-done | bytes 159776 | tf_op jit(solution)/shard_map/ppermute | solution.py:650
  12.4 0.4 shard_map.69
  12.8 1.4 %collective-permute-start.2 = (f32[759,128]{1,0:T(8,128)S(1)}, f32[759,128]{1,0:T(8,128)S(1)}, u32[]{:S(2)}, u32[]{:S(2)}) collective-permute-start(f32[759,128]{1,0:T(8,128)S(1)} %get-tuple-element.52), channel_id=1, source_target_pairs={{0,4},{4,0},{8,12},{12,8},{16,20},{20,16},{24,28},{28,24},{32,36},... | collective-permute-start | bytes 1165832 | tf_op jit(solution)/shard_map/ppermute | solution.py:650
  14.2 0.7 collective-permute-start.3
  14.9 3.6 %collective-permute-start.4 = (f32[674,128]{1,0:T(8,128)S(1)}, f32[674,128]{1,0:T(8,128)S(1)}, u32[]{:S(2)}, u32[]{:S(2)}) collective-permute-start(f32[674,128]{1,0:T(8,128)S(1)} %get-tuple-element.55), channel_id=1, source_target_pairs={{0,4},{4,0},{8,12},{12,8},{16,20},{20,16},{24,28},{28,24},{32,36},... | collective-permute-start | bytes 1035272 | tf_op jit(solution)/shard_map/ppermute | solution.py:650
  18.5 0.7 collective-permute-start.5
  19.2 2.2 %collective-permute-done.2.za = f32[759,128]{1,0:T(8,128)S(1)} collective-permute-done((f32[759,128]{1,0:T(8,128)S(1)}, f32[759,128]{1,0:T(8,128)S(1)}, u32[]{:S(2)}, u32[]{:S(2)}) %collective-permute-start.2) | collective-permute-done | bytes 388640 | tf_op jit(solution)/shard_map/ppermute | solution.py:650
  21.4 0.0 collective-permute-done.3.zb
  21.4 2.7 %shard_map.70 = (f32[6,4,32,128]{3,2,1,0:T(8,128)S(1)}, f32[6,4,32,128]{3,2,1,0:T(8,128)S(1)}, f32[6,4,48,128]{3,2,1,0:T(8,128)S(1)}, f32[578,128]{1,0:T(8,128)S...) custom-call(f32[12,4,32,128]{3,2,1,0:T(8,128)S(1)} %bitcast.15, ...), custom_call_target="tpu_custom_call" | custom-call | flops 16777216 | bytes 8388608 | tf_op jit(solution)/shard_map/pallas_call | solution.py:692
  24.1 4.7 %collective-permute-start.8 = (f32[578,128]{1,0:T(8,128)S(1)}, f32[578,128]{1,0:T(8,128)S(1)}, u32[]{:S(2)}, u32[]{:S(2)}) collective-permute-start(f32[578,128]{1,0:T(8,128)S(1)} %get-tuple-element.66), channel_id=1, source_target_pairs={{0,4},{4,0},{8,12},{12,8},{16,20},{20,16},{24,28},{28,24},{32,36},... | collective-permute-start | bytes 887816 | tf_op jit(solution)/shard_map/ppermute | solution.py:650
  28.8 0.7 collective-permute-start.9
  29.5 0.0 collective-permute-done.4.za
  29.5 0.0 collective-permute-done.5.zb
  29.5 2.5 %shard_map.71 = (f32[6,4,32,128]{3,2,1,0:T(8,128)S(1)}, f32[6,4,32,128]{3,2,1,0:T(8,128)S(1)}, f32[6,4,48,128]{3,2,1,0:T(8,128)S(1)}, f32[578,128]{1,0:T(8,128)S...) custom-call(f32[12,4,32,128]{3,2,1,0:T(8,128)S(1)} %bitcast.16, ...), custom_call_target="tpu_custom_call" | custom-call | flops 16777216 | bytes 8388608 | tf_op jit(solution)/shard_map/pallas_call | solution.py:700
  32.0 4.8 %collective-permute-start.6 = (f32[578,128]{1,0:T(8,128)S(1)}, f32[578,128]{1,0:T(8,128)S(1)}, u32[]{:S(2)}, u32[]{:S(2)}) collective-permute-start(f32[578,128]{1,0:T(8,128)S(1)} %get-tuple-element.60), channel_id=1, source_target_pairs={{0,4},{4,0},{8,12},{12,8},{16,20},{20,16},{24,28},{28,24},{32,36},... | collective-permute-start | bytes 887816 | tf_op jit(solution)/shard_map/ppermute | solution.py:650
  36.8 0.7 collective-permute-start.7
  37.5 1.2 %shard_map.72 = (f32[64,128]{1,0:T(8,128)S(1)}, f32[64,128]{1,0:T(8,128)S(1)}) custom-call(f32[12,4,32,128]{3,2,1,0:T(8,128)S(1)} %bitcast.17, f32[6,4,32,128]{3,2,1,0:T(8,128)S(1)} %get-tuple-element.62.b1_0.b1, f32[6,4,32,128]{3,2,1,0:T(8,128)S(1)} %get-tuple-element.63.b2_0.b2, f32[6,4,48,128]{3,2,1,0:T(8,128)S(1)} %get-tuple-element.64.b3w_0.b3w, ...), custom_call_target="tpu_custom_call" | custom-call | flops 16777216 | bytes 8388608 | tf_op jit(solution)/shard_map/pallas_call | solution.py:705
  38.7 0.0 collective-permute-done.8.za
  38.7 3.2 %shard_map.73 = (f32[6,4,32,128]{3,2,1,0:T(8,128)S(1)}, f32[6,4,32,128]{3,2,1,0:T(8,128)S(1)}, f32[6,4,32,128]{3,2,1,0:T(8,128)S(1)}, f32[64,128]{1,0:T(8,128)S(1)}) custom-call(f32[12,4,32,128]{3,2,1,0:T(8,128)S(1)} %bitcast.18, f32[6,4,32,128]{3,2,1,0:T(8,128)S(1)} %get-tuple-element.62.b1_0.b1, f32[6,4,32,128]{3,2,1,0:T(8,128)S(1)} %get-tuple-element.63.b2_0.b2, ...), custom_call_target="tpu_custom_call" | custom-call | flops 16777216 | bytes 8388608 | tf_op jit(solution)/shard_map/pallas_call | solution.py:708
  41.9 0.0 collective-permute-done.6.za
  41.9 0.0 collective-permute-done.7.zb
  41.9 3.3 %shard_map.74 = (f32[6,4,32,128]{3,2,1,0:T(8,128)S(1)}, f32[6,4,32,128]{3,2,1,0:T(8,128)S(1)}, f32[6,4,32,128]{3,2,1,0:T(8,128)S(1)}, f32[128,256]{1,0:T(8,128)S(1)}) custom-call(f32[12,4,32,128]{3,2,1,0:T(8,128)S(1)} %bitcast.19, f32[6,4,32,128]{3,2,1,0:T(8,128)S(1)} %get-tuple-element.57.b1_1.b1, f32[6,4,32,128]{3,2,1,0:T(8,128)S(1)} %get-tuple-element.58.b2_1.b2, ...), custom_call_target="tpu_custom_call" | custom-call | flops 16777216 | bytes 8388608 | tf_op jit(solution)/shard_map/pallas_call | solution.py:711
  45.2 0.1 copy.7
  45.3 25.3 %all_to_all.22 = f32[128,1,256]{2,1,0:T(1,128)S(1)} all-to-all(f32[128,1,256]{2,1,0:T(1,128)S(1)} %copy.7), channel_id=1, replica_groups=mesh['gz'=32,'gx'=4] {'gz','gx'}, dimensions={0} | all-to-all | bytes 262144 | tf_op jit(solution)/shard_map/all_to_all | solution.py:720
  70.6 2.0 %shard_map.75 = (f32[12,4,32,128]{3,2,1,0:T(8,128)}, f32[128,128]{1,0:T(8,128)S(1)}) custom-call(f32[128,256]{1,0:T(8,128)S(1)} %bitcast.21, f32[4,32,128]{2,1,0:T(8,128)S(1)} %copy-done.1, f32[12,4,32,128]{3,2,1,0:T(8,128)S(1)} %bitcast.20, f32[6,4,32,128]{3,2,1,0:T(8,128)S(1)} %get-tuple-element.85.rest_1_, ...), custom_call_target="tpu_custom_call" | custom-call | tf_op jit(solution)/shard_map/pallas_call | solution.py:721
  72.6 13.5 %all_to_all.23 = f32[128,1,128]{2,1,0:T(1,128)S(1)} all-to-all(f32[128,1,128]{2,1,0:T(1,128)S(1)} %bitcast.24), channel_id=1, replica_groups=mesh['gz'=32,'gx'=4] {'gz','gx'}, dimensions={0} | all-to-all | bytes 131072 | tf_op jit(solution)/shard_map/all_to_all | solution.py:732
  86.0 1.0 %shard_map.76 = f32[128,512]{1,0:T(8,128)} custom-call(f32[128,128]{1,0:T(8,128)S(1)} %bitcast.22, f32[16,512]{1,0:T(8,128)S(1)} %copy-done.2), custom_call_target="tpu_custom_call" | custom-call | tf_op jit(solution)/shard_map/pallas_call | solution.py:733
  (9 shorter events, 0.0 us)
Async XLA Ops:
  0.6 11.8 %copy-start = (f32[2,3,2,4,32,128]{5,4,3,2,1,0:T(8,128)S(1)}, f32[2,3,2,4,32,128]{5,4,3,2,1,0:T(8,128)}, u32[]{:S(2)}) copy-start(f32[2,3,2,4,32,128]{5,4,3,2,1,0:T(8,128)} %param.5) | copy-start | bytes 2359300
  0.6 11.8 %copy-start.1 = (f32[4,32,128]{2,1,0:T(8,128)S(1)}, f32[4,32,128]{2,1,0:T(8,128)}, u32[]{:S(2)}) copy-start(f32[4,32,128]{2,1,0:T(8,128)} %k.6) | copy-start | bytes 196612
  2.6 9.8 %copy-start.3 = (s32[1,4,32]{2,1,0:T(4,128)S(1)}, s32[1,4,32]{2,1,0:T(4,128)}, u32[]{:S(2)}) copy-start(s32[1,4,32]{2,1,0:T(4,128)} %param.7) | copy-start | bytes 1540
  2.6 6.1 %collective-permute-start = (f32[312,128]{1,0:T(8,128)}, f32[312,128]{1,0:T(8,128)S(1)}, u32[]{:S(2)}, u32[]{:S(2)}) collective-permute-start(f32[312,128]{1,0:T(8,128)} %get-tuple-element.50), channel_id=1, source_target_pairs={{0,1},{1,0},{2,3},{3,2},{4,5},{5,4},{6,7},{7,6},{8,9},{9,8},{10,11... | collective-permute-start | bytes 479240 | tf_op jit(solution)/shard_map/ppermute | solution.py:650
  4.1 8.3 %collective-permute-start.1 = (f32[312,128]{1,0:T(8,128)}, f32[312,128]{1,0:T(8,128)S(1)}, u32[]{:S(2)}, u32[]{:S(2)}) collective-permute-start(f32[312,128]{1,0:T(8,128)} %get-tuple-element.51), channel_id=1, source_target_pairs={{1,2},{2,1},{5,6},{6,5},{9,10},{10,9},{13,14},{14,13},{17,18},{18,... | collective-permute-start | bytes 479240 | tf_op jit(solution)/shard_map/ppermute | solution.py:650
  12.8 8.6 %collective-permute-start.2 = (f32[759,128]{1,0:T(8,128)S(1)}, f32[759,128]{1,0:T(8,128)S(1)}, u32[]{:S(2)}, u32[]{:S(2)}) collective-permute-start(f32[759,128]{1,0:T(8,128)S(1)} %get-tuple-element.52), channel_id=1, source_target_pairs={{0,4},{4,0},{8,12},{12,8},{16,20},{20,16},{24,28},{28,24},{32,36},... | collective-permute-start | bytes 1165832 | tf_op jit(solution)/shard_map/ppermute | solution.py:650
  14.2 7.2 %collective-permute-start.3 = (f32[759,128]{1,0:T(8,128)S(1)}, f32[759,128]{1,0:T(8,128)S(1)}, u32[]{:S(2)}, u32[]{:S(2)}) collective-permute-start(f32[759,128]{1,0:T(8,128)S(1)} %get-tuple-element.53), channel_id=1, source_target_pairs={{4,8},{8,4},{12,16},{16,12},{20,24},{24,20},{28,32},{32,28},{36,40... | collective-permute-start | bytes 1165832 | tf_op jit(solution)/shard_map/ppermute | solution.py:650
  14.9 14.6 %collective-permute-start.4 = (f32[674,128]{1,0:T(8,128)S(1)}, f32[674,128]{1,0:T(8,128)S(1)}, u32[]{:S(2)}, u32[]{:S(2)}) collective-permute-start(f32[674,128]{1,0:T(8,128)S(1)} %get-tuple-element.55), channel_id=1, source_target_pairs={{0,4},{4,0},{8,12},{12,8},{16,20},{20,16},{24,28},{28,24},{32,36},... | collective-permute-start | bytes 1035272 | tf_op jit(solution)/shard_map/ppermute | solution.py:650
  18.5 11.0 %collective-permute-start.5 = (f32[674,128]{1,0:T(8,128)S(1)}, f32[674,128]{1,0:T(8,128)S(1)}, u32[]{:S(2)}, u32[]{:S(2)}) collective-permute-start(f32[674,128]{1,0:T(8,128)S(1)} %get-tuple-element.56), channel_id=1, source_target_pairs={{4,8},{8,4},{12,16},{16,12},{20,24},{24,20},{28,32},{32,28},{36,40... | collective-permute-start | bytes 1035272 | tf_op jit(solution)/shard_map/ppermute | solution.py:650
  24.1 14.6 %collective-permute-start.8 = (f32[578,128]{1,0:T(8,128)S(1)}, f32[578,128]{1,0:T(8,128)S(1)}, u32[]{:S(2)}, u32[]{:S(2)}) collective-permute-start(f32[578,128]{1,0:T(8,128)S(1)} %get-tuple-element.66), channel_id=1, source_target_pairs={{0,4},{4,0},{8,12},{12,8},{16,20},{20,16},{24,28},{28,24},{32,36},... | collective-permute-start | bytes 887816 | tf_op jit(solution)/shard_map/ppermute | solution.py:650
  28.8 9.9 %collective-permute-start.9 = (f32[578,128]{1,0:T(8,128)S(1)}, f32[578,128]{1,0:T(8,128)S(1)}, u32[]{:S(2)}, u32[]{:S(2)}) collective-permute-start(f32[578,128]{1,0:T(8,128)S(1)} %get-tuple-element.67), channel_id=1, source_target_pairs={{4,8},{8,4},{12,16},{16,12},{20,24},{24,20},{28,32},{32,28},{36,40... | collective-permute-start | bytes 887816 | tf_op jit(solution)/shard_map/ppermute | solution.py:650
  32.0 9.8 %collective-permute-start.6 = (f32[578,128]{1,0:T(8,128)S(1)}, f32[578,128]{1,0:T(8,128)S(1)}, u32[]{:S(2)}, u32[]{:S(2)}) collective-permute-start(f32[578,128]{1,0:T(8,128)S(1)} %get-tuple-element.60), channel_id=1, source_target_pairs={{0,4},{4,0},{8,12},{12,8},{16,20},{20,16},{24,28},{28,24},{32,36},... | collective-permute-start | bytes 887816 | tf_op jit(solution)/shard_map/ppermute | solution.py:650
  36.8 5.1 %collective-permute-start.7 = (f32[578,128]{1,0:T(8,128)S(1)}, f32[578,128]{1,0:T(8,128)S(1)}, u32[]{:S(2)}, u32[]{:S(2)}) collective-permute-start(f32[578,128]{1,0:T(8,128)S(1)} %get-tuple-element.61), channel_id=1, source_target_pairs={{4,8},{8,4},{12,16},{16,12},{20,24},{24,20},{28,32},{32,28},{36,40... | collective-permute-start | bytes 887816 | tf_op jit(solution)/shard_map/ppermute | solution.py:650
  72.5 13.5 %copy-start.2 = (f32[16,512]{1,0:T(8,128)S(1)}, f32[16,512]{1,0:T(8,128)}, u32[]{:S(2)}) copy-start(f32[16,512]{1,0:T(8,128)} %get-tuple-element.97.power) | copy-start | bytes 98308

commit v5 on v4

--- a/solution.py
+++ b/solution.py
@@ -17,7 +17,7 @@
 f32 = jnp.float32
 VM = pl.BlockSpec(memory_space=pltpu.VMEM)
 LIMIT = 14 * 1024 * 1024
-FIRST_LIMIT = 60 * 1024 * 1024
+FIRST_LIMIT = 14 * 1024 * 1024
 
 
 HBM = pl.BlockSpec(memory_space=pltpu.HBM)
@@ -668,7 +668,7 @@
     ]
     to_a, to_b, power = call(
         pack_x, [HBM] * 4, [side] * 2 + [((16, scen), VM)], rims, limit=FIRST_LIMIT
-    )(r_far, conductance, spectra.T, scenario_tile.reshape(1, scen))
+    )(*[pltpu.with_memory_space_constraint(v, pltpu.HBM) for v in (r_far, conductance, spectra.T, scenario_tile.reshape(1, scen))])
     r, k = r_far, conductance
     near = exchange(to_a, to_b, "gx")
     deep = [((rows_of(REACH, with_k), NY), VM) for with_k in (True, False)]

time: 87.3 us -> 86.4 us (0.990)
  no operation moved by 1% of the time
where the time goes in v5:
time: 86.4 us; the launch traced here: 86.1 us
  blocking collectives  38.7 us (45%)
  starting transfers between devices  23.3 us (27%)
  Pallas kernels  17.4 us (20%)
  waiting for transfers between devices  5.68 us (7%)
    all_to_all x2, blocking collectives, per_device(): got = lax.all_to_all(send, ('gz', 'gx'), 0, 0, tiled=True)  38.7 us
    ppermute x10, starting transfers between devices, exchange(): return (lax.ppermute(to_a, axis, first), lax.ppermute(to_b, axis, second))  23.3 us
    ppermute x10, waiting for transfers between devices, exchange(): return (lax.ppermute(to_a, axis, first), lax.ppermute(to_b, axis, second))  5.68 us
    pallas_call x1, Pallas kernels, per_device(): call(second_half_1, [VM] * 10, seconds + [((128, 2 * NY), VM)], [pltpu.VM...  3.29 us
    pallas_call x1, Pallas kernels, per_device(): call(second_half_0, [VM] * 8, seconds + [table], spaces, **cost)  3.17 us
    pallas_call x1, Pallas kernels, per_device(): call(first_half_0, [VM] * 6, firsts + [((2, EZ, WX, NY), VM)], [pltpu.VME...  2.67 us
    pallas_call x1, Pallas kernels, per_device(): call(first_half_1, [VM] * 6, firsts, [space] * 5 + [far, dma((2,))], **cost)  2.55 us
    pallas_call x1, Pallas kernels, per_device(): call(finish, [VM] * 13, [(whole, HBM), ((128, NY), VM)], [pltpu.VMEM(whol...  1.97 us
  transfers between devices with their start and end apart: 10, of which 2 were waited for; matrix products, arithmetic and copies ran while one was open for 0% of the time, Pallas kernels for 11%

profile of v5, /device:TPU:1, one launch (start us, length us, event | category | flops | bytes accessed | tf_op | source)
XLA Modules:
  0.0 86.1 jit_solution(12718603247222081724)
XLA Ops:
  0.7 1.2 %shard_map.68 = (f32[312,128]{1,0:T(8,128)S(1)}, f32[312,128]{1,0:T(8,128)S(1)}, f32[16,512]{1,0:T(8,128)S(1)}) custom-call(f32[12,4,32,128]{3,2,1,0:T(8,128)} %bitcast.13, f32[4,32,128]{2,1,0:T(8,128)} %k.6, f32[4,512]{1,0:T(4,128)} %bitcast.26, s32[1,512]{1,0:T(1,128)} %bitcast.27), custom_call_target="tpu_custom_call" | custom-call | tf_op jit(solution)/shard_map/pallas_call | solution.py:669
  1.9 0.0 copy-start.2
  1.9 1.5 %collective-permute-start = (f32[312,128]{1,0:T(8,128)S(1)}, f32[312,128]{1,0:T(8,128)S(1)}, u32[]{:S(2)}, u32[]{:S(2)}) collective-permute-start(f32[312,128]{1,0:T(8,128)S(1)} %get-tuple-element.50), channel_id=1, source_target_pairs={{0,1},{1,0},{2,3},{3,2},{4,5},{5,4},{6,7},{7,6},{8,9},{9,8},{10,11... | collective-permute-start | bytes 479240 | tf_op jit(solution)/shard_map/ppermute | solution.py:650
  3.4 4.6 %collective-permute-start.1 = (f32[312,128]{1,0:T(8,128)S(1)}, f32[312,128]{1,0:T(8,128)S(1)}, u32[]{:S(2)}, u32[]{:S(2)}) collective-permute-start(f32[312,128]{1,0:T(8,128)S(1)} %get-tuple-element.51), channel_id=1, source_target_pairs={{1,2},{2,1},{5,6},{6,5},{9,10},{10,9},{13,14},{14,13},{17,18},{18,... | collective-permute-start | bytes 479240 | tf_op jit(solution)/shard_map/ppermute | solution.py:650
  8.0 0.0 collective-permute-done.xa
  8.0 3.4 %collective-permute-done.1.xb = f32[312,128]{1,0:T(8,128)S(1)} collective-permute-done((f32[312,128]{1,0:T(8,128)S(1)}, f32[312,128]{1,0:T(8,128)S(1)}, u32[]{:S(2)}, u32[]{:S(2)}) %collective-permute-start.1) | collective-permute-done | bytes 159776 | tf_op jit(solution)/shard_map/ppermute | solution.py:650
  11.5 0.4 shard_map.69
  11.9 1.4 %collective-permute-start.2 = (f32[759,128]{1,0:T(8,128)S(1)}, f32[759,128]{1,0:T(8,128)S(1)}, u32[]{:S(2)}, u32[]{:S(2)}) collective-permute-start(f32[759,128]{1,0:T(8,128)S(1)} %get-tuple-element.52), channel_id=1, source_target_pairs={{0,4},{4,0},{8,12},{12,8},{16,20},{20,16},{24,28},{28,24},{32,36},... | collective-permute-start | bytes 1165832 | tf_op jit(solution)/shard_map/ppermute | solution.py:650
  13.3 0.7 collective-permute-start.3
  14.0 3.6 %collective-permute-start.4 = (f32[674,128]{1,0:T(8,128)S(1)}, f32[674,128]{1,0:T(8,128)S(1)}, u32[]{:S(2)}, u32[]{:S(2)}) collective-permute-start(f32[674,128]{1,0:T(8,128)S(1)} %get-tuple-element.55), channel_id=1, source_target_pairs={{0,4},{4,0},{8,12},{12,8},{16,20},{20,16},{24,28},{28,24},{32,36},... | collective-permute-start | bytes 1035272 | tf_op jit(solution)/shard_map/ppermute | solution.py:650
  17.6 0.7 collective-permute-start.5
  18.2 2.2 %collective-permute-done.2.za = f32[759,128]{1,0:T(8,128)S(1)} collective-permute-done((f32[759,128]{1,0:T(8,128)S(1)}, f32[759,128]{1,0:T(8,128)S(1)}, u32[]{:S(2)}, u32[]{:S(2)}) %collective-permute-start.2) | collective-permute-done | bytes 388640 | tf_op jit(solution)/shard_map/ppermute | solution.py:650
  20.5 0.0 collective-permute-done.3.zb
  20.5 2.7 %shard_map.70 = (f32[6,4,32,128]{3,2,1,0:T(8,128)S(1)}, f32[6,4,32,128]{3,2,1,0:T(8,128)S(1)}, f32[6,4,48,128]{3,2,1,0:T(8,128)S(1)}, f32[578,128]{1,0:T(8,128)S...) custom-call(f32[12,4,32,128]{3,2,1,0:T(8,128)S(1)} %bitcast.15, ...), custom_call_target="tpu_custom_call" | custom-call | flops 16777216 | bytes 8388608 | tf_op jit(solution)/shard_map/pallas_call | solution.py:692
  23.2 4.7 %collective-permute-start.8 = (f32[578,128]{1,0:T(8,128)S(1)}, f32[578,128]{1,0:T(8,128)S(1)}, u32[]{:S(2)}, u32[]{:S(2)}) collective-permute-start(f32[578,128]{1,0:T(8,128)S(1)} %get-tuple-element.66), channel_id=1, source_target_pairs={{0,4},{4,0},{8,12},{12,8},{16,20},{20,16},{24,28},{28,24},{32,36},... | collective-permute-start | bytes 887816 | tf_op jit(solution)/shard_map/ppermute | solution.py:650
  27.9 0.7 collective-permute-start.9
  28.6 0.0 collective-permute-done.4.za
  28.6 0.0 collective-permute-done.5.zb
  28.6 2.5 %shard_map.71 = (f32[6,4,32,128]{3,2,1,0:T(8,128)S(1)}, f32[6,4,32,128]{3,2,1,0:T(8,128)S(1)}, f32[6,4,48,128]{3,2,1,0:T(8,128)S(1)}, f32[578,128]{1,0:T(8,128)S...) custom-call(f32[12,4,32,128]{3,2,1,0:T(8,128)S(1)} %bitcast.16, ...), custom_call_target="tpu_custom_call" | custom-call | flops 16777216 | bytes 8388608 | tf_op jit(solution)/shard_map/pallas_call | solution.py:700
  31.1 4.8 %collective-permute-start.6 = (f32[578,128]{1,0:T(8,128)S(1)}, f32[578,128]{1,0:T(8,128)S(1)}, u32[]{:S(2)}, u32[]{:S(2)}) collective-permute-start(f32[578,128]{1,0:T(8,128)S(1)} %get-tuple-element.60), channel_id=1, source_target_pairs={{0,4},{4,0},{8,12},{12,8},{16,20},{20,16},{24,28},{28,24},{32,36},... | collective-permute-start | bytes 887816 | tf_op jit(solution)/shard_map/ppermute | solution.py:650
  35.9 0.7 collective-permute-start.7
  36.6 1.2 %shard_map.72 = (f32[64,128]{1,0:T(8,128)S(1)}, f32[64,128]{1,0:T(8,128)S(1)}) custom-call(f32[12,4,32,128]{3,2,1,0:T(8,128)S(1)} %bitcast.17, f32[6,4,32,128]{3,2,1,0:T(8,128)S(1)} %get-tuple-element.62.b1_0.b1, f32[6,4,32,128]{3,2,1,0:T(8,128)S(1)} %get-tuple-element.63.b2_0.b2, f32[6,4,48,128]{3,2,1,0:T(8,128)S(1)} %get-tuple-element.64.b3w_0.b3w, ...), custom_call_target="tpu_custom_call" | custom-call | flops 16777216 | bytes 8388608 | tf_op jit(solution)/shard_map/pallas_call | solution.py:705
  37.8 0.0 collective-permute-done.8.za
  37.8 3.2 %shard_map.73 = (f32[6,4,32,128]{3,2,1,0:T(8,128)S(1)}, f32[6,4,32,128]{3,2,1,0:T(8,128)S(1)}, f32[6,4,32,128]{3,2,1,0:T(8,128)S(1)}, f32[64,128]{1,0:T(8,128)S(1)}) custom-call(f32[12,4,32,128]{3,2,1,0:T(8,128)S(1)} %bitcast.18, f32[6,4,32,128]{3,2,1,0:T(8,128)S(1)} %get-tuple-element.62.b1_0.b1, f32[6,4,32,128]{3,2,1,0:T(8,128)S(1)} %get-tuple-element.63.b2_0.b2, ...), custom_call_target="tpu_custom_call" | custom-call | flops 16777216 | bytes 8388608 | tf_op jit(solution)/shard_map/pallas_call | solution.py:708
  41.0 0.0 collective-permute-done.6.za
  41.0 0.0 collective-permute-done.7.zb
  41.0 3.3 %shard_map.74 = (f32[6,4,32,128]{3,2,1,0:T(8,128)S(1)}, f32[6,4,32,128]{3,2,1,0:T(8,128)S(1)}, f32[6,4,32,128]{3,2,1,0:T(8,128)S(1)}, f32[128,256]{1,0:T(8,128)S(1)}) custom-call(f32[12,4,32,128]{3,2,1,0:T(8,128)S(1)} %bitcast.19, f32[6,4,32,128]{3,2,1,0:T(8,128)S(1)} %get-tuple-element.57.b1_1.b1, f32[6,4,32,128]{3,2,1,0:T(8,128)S(1)} %get-tuple-element.58.b2_1.b2, ...), custom_call_target="tpu_custom_call" | custom-call | flops 16777216 | bytes 8388608 | tf_op jit(solution)/shard_map/pallas_call | solution.py:711
  44.3 0.1 copy.7
  44.4 25.2 %all_to_all.22 = f32[128,1,256]{2,1,0:T(1,128)S(1)} all-to-all(f32[128,1,256]{2,1,0:T(1,128)S(1)} %copy.7), channel_id=1, replica_groups=mesh['gz'=32,'gx'=4] {'gz','gx'}, dimensions={0} | all-to-all | bytes 262144 | tf_op jit(solution)/shard_map/all_to_all | solution.py:720
  69.7 2.0 %shard_map.75 = (f32[12,4,32,128]{3,2,1,0:T(8,128)}, f32[128,128]{1,0:T(8,128)S(1)}) custom-call(f32[128,256]{1,0:T(8,128)S(1)} %bitcast.21, f32[4,32,128]{2,1,0:T(8,128)S(1)} %copy-done.1, f32[12,4,32,128]{3,2,1,0:T(8,128)S(1)} %bitcast.20, f32[6,4,32,128]{3,2,1,0:T(8,128)S(1)} %get-tuple-element.85.rest_1_, ...), custom_call_target="tpu_custom_call" | custom-call | tf_op jit(solution)/shard_map/pallas_call | solution.py:721
  71.6 13.5 %all_to_all.23 = f32[128,1,128]{2,1,0:T(1,128)S(1)} all-to-all(f32[128,1,128]{2,1,0:T(1,128)S(1)} %bitcast.24), channel_id=1, replica_groups=mesh['gz'=32,'gx'=4] {'gz','gx'}, dimensions={0} | all-to-all | bytes 131072 | tf_op jit(solution)/shard_map/all_to_all | solution.py:732
  85.1 1.0 %shard_map.76 = f32[128,512]{1,0:T(8,128)} custom-call(f32[128,128]{1,0:T(8,128)S(1)} %bitcast.22, f32[16,512]{1,0:T(8,128)S(1)} %get-tuple-element.97.power), custom_call_target="tpu_custom_call" | custom-call | tf_op jit(solution)/shard_map/pallas_call | solution.py:733
  (7 shorter events, 0.0 us)
Async XLA Ops:
  0.6 10.8 %copy-start = (f32[2,3,2,4,32,128]{5,4,3,2,1,0:T(8,128)S(1)}, f32[2,3,2,4,32,128]{5,4,3,2,1,0:T(8,128)}, u32[]{:S(2)}) copy-start(f32[2,3,2,4,32,128]{5,4,3,2,1,0:T(8,128)} %param.5) | copy-start | bytes 2359300
  0.6 10.8 %copy-start.1 = (f32[4,32,128]{2,1,0:T(8,128)S(1)}, f32[4,32,128]{2,1,0:T(8,128)}, u32[]{:S(2)}) copy-start(f32[4,32,128]{2,1,0:T(8,128)} %k.6) | copy-start | bytes 196612
  1.9 9.6 %copy-start.2 = (s32[1,4,32]{2,1,0:T(4,128)S(1)}, s32[1,4,32]{2,1,0:T(4,128)}, u32[]{:S(2)}) copy-start(s32[1,4,32]{2,1,0:T(4,128)} %param.7) | copy-start | bytes 1540
  1.9 6.1 %collective-permute-start = (f32[312,128]{1,0:T(8,128)S(1)}, f32[312,128]{1,0:T(8,128)S(1)}, u32[]{:S(2)}, u32[]{:S(2)}) collective-permute-start(f32[312,128]{1,0:T(8,128)S(1)} %get-tuple-element.50), channel_id=1, source_target_pairs={{0,1},{1,0},{2,3},{3,2},{4,5},{5,4},{6,7},{7,6},{8,9},{9,8},{10,11... | collective-permute-start | bytes 479240 | tf_op jit(solution)/shard_map/ppermute | solution.py:650
  3.4 8.1 %collective-permute-start.1 = (f32[312,128]{1,0:T(8,128)S(1)}, f32[312,128]{1,0:T(8,128)S(1)}, u32[]{:S(2)}, u32[]{:S(2)}) collective-permute-start(f32[312,128]{1,0:T(8,128)S(1)} %get-tuple-element.51), channel_id=1, source_target_pairs={{1,2},{2,1},{5,6},{6,5},{9,10},{10,9},{13,14},{14,13},{17,18},{18,... | collective-permute-start | bytes 479240 | tf_op jit(solution)/shard_map/ppermute | solution.py:650
  11.9 8.6 %collective-permute-start.2 = (f32[759,128]{1,0:T(8,128)S(1)}, f32[759,128]{1,0:T(8,128)S(1)}, u32[]{:S(2)}, u32[]{:S(2)}) collective-permute-start(f32[759,128]{1,0:T(8,128)S(1)} %get-tuple-element.52), channel_id=1, source_target_pairs={{0,4},{4,0},{8,12},{12,8},{16,20},{20,16},{24,28},{28,24},{32,36},... | collective-permute-start | bytes 1165832 | tf_op jit(solution)/shard_map/ppermute | solution.py:650
  13.3 7.2 %collective-permute-start.3 = (f32[759,128]{1,0:T(8,128)S(1)}, f32[759,128]{1,0:T(8,128)S(1)}, u32[]{:S(2)}, u32[]{:S(2)}) collective-permute-start(f32[759,128]{1,0:T(8,128)S(1)} %get-tuple-element.53), channel_id=1, source_target_pairs={{4,8},{8,4},{12,16},{16,12},{20,24},{24,20},{28,32},{32,28},{36,40... | collective-permute-start | bytes 1165832 | tf_op jit(solution)/shard_map/ppermute | solution.py:650
  14.0 14.6 %collective-permute-start.4 = (f32[674,128]{1,0:T(8,128)S(1)}, f32[674,128]{1,0:T(8,128)S(1)}, u32[]{:S(2)}, u32[]{:S(2)}) collective-permute-start(f32[674,128]{1,0:T(8,128)S(1)} %get-tuple-element.55), channel_id=1, source_target_pairs={{0,4},{4,0},{8,12},{12,8},{16,20},{20,16},{24,28},{28,24},{32,36},... | collective-permute-start | bytes 1035272 | tf_op jit(solution)/shard_map/ppermute | solution.py:650
  17.6 11.0 %collective-permute-start.5 = (f32[674,128]{1,0:T(8,128)S(1)}, f32[674,128]{1,0:T(8,128)S(1)}, u32[]{:S(2)}, u32[]{:S(2)}) collective-permute-start(f32[674,128]{1,0:T(8,128)S(1)} %get-tuple-element.56), channel_id=1, source_target_pairs={{4,8},{8,4},{12,16},{16,12},{20,24},{24,20},{28,32},{32,28},{36,40... | collective-permute-start | bytes 1035272 | tf_op jit(solution)/shard_map/ppermute | solution.py:650
  23.2 14.6 %collective-permute-start.8 = (f32[578,128]{1,0:T(8,128)S(1)}, f32[578,128]{1,0:T(8,128)S(1)}, u32[]{:S(2)}, u32[]{:S(2)}) collective-permute-start(f32[578,128]{1,0:T(8,128)S(1)} %get-tuple-element.66), channel_id=1, source_target_pairs={{0,4},{4,0},{8,12},{12,8},{16,20},{20,16},{24,28},{28,24},{32,36},... | collective-permute-start | bytes 887816 | tf_op jit(solution)/shard_map/ppermute | solution.py:650
  27.9 9.9 %collective-permute-start.9 = (f32[578,128]{1,0:T(8,128)S(1)}, f32[578,128]{1,0:T(8,128)S(1)}, u32[]{:S(2)}, u32[]{:S(2)}) collective-permute-start(f32[578,128]{1,0:T(8,128)S(1)} %get-tuple-element.67), channel_id=1, source_target_pairs={{4,8},{8,4},{12,16},{16,12},{20,24},{24,20},{28,32},{32,28},{36,40... | collective-permute-start | bytes 887816 | tf_op jit(solution)/shard_map/ppermute | solution.py:650
  31.1 9.8 %collective-permute-start.6 = (f32[578,128]{1,0:T(8,128)S(1)}, f32[578,128]{1,0:T(8,128)S(1)}, u32[]{:S(2)}, u32[]{:S(2)}) collective-permute-start(f32[578,128]{1,0:T(8,128)S(1)} %get-tuple-element.60), channel_id=1, source_target_pairs={{0,4},{4,0},{8,12},{12,8},{16,20},{20,16},{24,28},{28,24},{32,36},... | collective-permute-start | bytes 887816 | tf_op jit(solution)/shard_map/ppermute | solution.py:650
  35.9 5.1 %collective-permute-start.7 = (f32[578,128]{1,0:T(8,128)S(1)}, f32[578,128]{1,0:T(8,128)S(1)}, u32[]{:S(2)}, u32[]{:S(2)}) collective-permute-start(f32[578,128]{1,0:T(8,128)S(1)} %get-tuple-element.61), channel_id=1, source_target_pairs={{4,8},{8,4},{12,16},{16,12},{20,24},{24,20},{28,32},{32,28},{36,40... | collective-permute-start | bytes 887816 | tf_op jit(solution)/shard_map/ppermute | solution.py:650

commit v6 on v5

--- a/solution.py
+++ b/solution.py
@@ -293,7 +293,7 @@
     lax.fori_loop(0, NF, field, 0)
 
 
-def first_steps(p, r, k, kx, xa, xb, za, zb, b1, b2, b3w, to_a, to_b, b1_far, b2_far, m, ba, bb, ya, yb, hs, far, sem):
+def first_steps(p, r, k, kx, xa, xb, za, zb, b1, b2, b3w, to_a, to_b, m, ba, bb, ya, yb, hs, far):
     for f in range(NF):
         clear_sides(ba.at[f])
         own_layers(ba.at[f], REACH, r.at[p * NF + f], xa, xb, p * NF + f)
@@ -316,24 +316,21 @@
     all_smooth(ba, ya, m)
     apply_k(ba, ya, bb, yb, hs, m, 1, EZ - 1, SHIFTS[0], True)
     keep(bb, b1)
-    copies = start_all([(b1, b1_far)], sem)
     apply_k(bb, yb, ba, ya, hs, m, 2, EZ - 2, SHIFTS[1], True)
     keep(ba, b2)
-    copies += start_all([(b2, b2_far)], sem, 1)
     apply_k(ba, ya, bb, yb, hs, m, 3, EZ - 3, SHIFTS[2], False)
     for f in range(NF):
         b3w[f] = bb[f, REACH : REACH + NZL]
     far_fields(bb, REACH, lambda z: (m[0, REACH + z], m[1, REACH + z]), far)
     either(odd("gz"), lambda up, down: fill_messages(bb, REACH, far, None, 0, up, down), to_a, to_b)
-    wait_all(copies)
-
-
-def first_half_0(r, k, xa, xb, za, zb, b1, b2, b3w, to_a, to_b, b1_far, b2_far, m, kx, *space):
-    first_steps(0, r, k, kx, xa, xb, za, zb, b1, b2, b3w, to_a, to_b, b1_far, b2_far, m, *space)
-
-
-def first_half_1(r, m, xa, xb, za, zb, b1, b2, b3w, to_a, to_b, b1_far, b2_far, *space):
-    first_steps(1, r, None, None, xa, xb, za, zb, b1, b2, b3w, to_a, to_b, b1_far, b2_far, m, *space)
+
+
+def first_half_0(r, k, xa, xb, za, zb, b1, b2, b3w, to_a, to_b, m, kx, *space):
+    first_steps(0, r, k, kx, xa, xb, za, zb, b1, b2, b3w, to_a, to_b, m, *space)
+
+
+def first_half_1(r, m, xa, xb, za, zb, b1, b2, b3w, to_a, to_b, *space):
+    first_steps(1, r, None, None, xa, xb, za, zb, b1, b2, b3w, to_a, to_b, m, *space)
 
 
 PAIRS = [(i, j) for i in range(7) for j in range(i, 7)]
@@ -344,7 +341,7 @@
     SLOT[_pair] = sum(1 if a == b else 2 for a, b in SLOT)
 
 
-def gram(read, pairs, out):
+def gram(read, pairs, out, unroll=False):
     used = sorted({i for pair in pairs for i in pair})
     count = sum(1 if i == j else 2 for i, j in pairs)
 
@@ -363,7 +360,7 @@
                     at += 1
         return tuple(acc)
 
-    acc = lax.fori_loop(0, 3 * NZL, block, (jnp.zeros((8, NY), f32),) * count)
+    acc = lax.fori_loop(0, 3 * NZL, block, (jnp.zeros((8, NY), f32),) * count, unroll=unroll)
     at = 0
     for i, j in pairs:
         for part in range(1 if i == j else 2):
@@ -405,9 +402,11 @@
     copies += start_all([(bb.at[:, own, mid, :], b4_far)], sem, 1)
     apply_k(bb, yb, bc, ya, hs, m, 2, EZ - 2, SHIFTS[4], True)
     copies += start_all([(bc.at[:, own, mid, :], b5_far)], sem, 2)
+    total[...] = part[...]
+    read = reader(p, b0, b1, b2, b3w, bb, bc, bd)
     apply_k(bc, ya, bd, yb, hs, m, 3, EZ - 3, SHIFTS[5], False)
-    total[...] = part[...]
-    gram(reader(p, b0, b1, b2, b3w, bb, bc, bd), HIGH, total)
+    gram(read, [pair for pair in HIGH if pair[1] < 6], total, True)
+    gram(read, [pair for pair in HIGH if pair[1] == 6], total, True)
     wait_all(copies)
 
 
@@ -687,18 +686,18 @@
     halo_1 = exchange(*packed[2:4], "gz")
     back = ((rows_of(0, False), NY), VM)
     far = pltpu.VMEM((8, WX, NY), f32)
-    firsts = [(block, VM), (block, VM), (wide, VM), back, back, (block, HBM), (block, HBM)]
+    firsts = [(block, VM), (block, VM), (wide, VM), back, back]
     cost = {"flops": 1 << 24, "moved": 1 << 23}
-    *b_0, to_a, to_b, b1_0, b2_0, m = call(
+    *b_0, to_a, to_b, m = call(
         first_half_0,
         [VM] * 6,
         firsts + [((2, EZ, WX, NY), VM)],
-        [pltpu.VMEM((EZ, WX, NY), f32)] + [space] * 5 + [far, dma((2,))],
+        [pltpu.VMEM((EZ, WX, NY), f32)] + [space] * 5 + [far],
         **cost,
     )(r, k, *near, *halo_0)
     halo_0 = exchange(to_a, to_b, "gz")
-    *b_1, to_a, to_b, b1_1, b2_1 = call(
-        first_half_1, [VM] * 6, firsts, [space] * 5 + [far, dma((2,))], **cost
+    *b_1, to_a, to_b = call(
+        first_half_1, [VM] * 6, firsts, [space] * 5 + [far], **cost
     )(r, m, *near, *halo_1)
     halo_1 = exchange(to_a, to_b, "gz")
     table = ((64, NY), VM)
@@ -715,7 +714,7 @@
         [pltpu.VMEM((64, NY), f32)] + spaces,
         **cost,
     )(r, *b_1, m, *halo_1, part_1, total, cells)
-    held = (send, conductance, r_far, b1_0, b2_0, *high_0, b1_1, b2_1, *high_1)
+    held = (send, conductance, r_far, *b_0[:2], *high_0, *b_1[:2], *high_1)
     send, *fars = lax.optimization_barrier(held)
     got = lax.all_to_all(send, ("gz", "gx"), 0, 0, tiled=True)
     x, send = call(

time: 86.4 us -> 85.5 us (0.990)
  Pallas kernels: 17.4 us -> 16.3 us
  transfers between devices with their start and end apart: 10 -> 10, of which waited for: 2 -> 2; matrix products, arithmetic and copies ran while one was open for 0% -> 0% of each run, Pallas kernels for 11% -> 10%
where the time goes in v6:
time: 85.5 us; the launch traced here: 85.2 us
  blocking collectives  39 us (46%)
  starting transfers between devices  23.3 us (27%)
  Pallas kernels  16.3 us (19%)
  waiting for transfers between devices  5.68 us (7%)
    all_to_all x2, blocking collectives, per_device(): got = lax.all_to_all(send, ('gz', 'gx'), 0, 0, tiled=True)  39 us
    ppermute x10, starting transfers between devices, exchange(): return (lax.ppermute(to_a, axis, first), lax.ppermute(to_b, axis, second))  23.3 us
    ppermute x10, waiting for transfers between devices, exchange(): return (lax.ppermute(to_a, axis, first), lax.ppermute(to_b, axis, second))  5.68 us
    pallas_call x1, Pallas kernels, per_device(): call(second_half_1, [VM] * 10, seconds + [((128, 2 * NY), VM)], [pltpu.VM...  3.26 us
    pallas_call x1, Pallas kernels, per_device(): call(second_half_0, [VM] * 8, seconds + [table], spaces, **cost)  2.95 us
    pallas_call x1, Pallas kernels, per_device(): call(first_half_0, [VM] * 6, firsts + [((2, EZ, WX, NY), VM)], [pltpu.VME...  2.27 us
    pallas_call x1, Pallas kernels, per_device(): call(first_half_1, [VM] * 6, firsts, [space] * 5 + [far], **cost)  2.14 us
    pallas_call x1, Pallas kernels, per_device(): call(finish, [VM] * 13, [(whole, HBM), ((128, NY), VM)], [pltpu.VMEM(whol...  1.97 us
  transfers between devices with their start and end apart: 10, of which 2 were waited for; matrix products, arithmetic and copies ran while one was open for 0% of the time, Pallas kernels for 10%

profile of v6, /device:TPU:1, one launch (start us, length us, event | category | flops | bytes accessed | tf_op | source)
XLA Modules:
  0.0 85.2 jit_solution(8906736615597759723)
XLA Ops:
  0.7 1.2 %shard_map.68 = (f32[312,128]{1,0:T(8,128)S(1)}, f32[312,128]{1,0:T(8,128)S(1)}, f32[16,512]{1,0:T(8,128)S(1)}) custom-call(f32[12,4,32,128]{3,2,1,0:T(8,128)} %bitcast.13, f32[4,32,128]{2,1,0:T(8,128)} %k.6, f32[4,512]{1,0:T(4,128)} %bitcast.26, s32[1,512]{1,0:T(1,128)} %bitcast.27), custom_call_target="tpu_custom_call" | custom-call | tf_op jit(solution)/shard_map/pallas_call | solution.py:668
  1.9 0.0 copy-start.2
  1.9 1.5 %collective-permute-start = (f32[312,128]{1,0:T(8,128)S(1)}, f32[312,128]{1,0:T(8,128)S(1)}, u32[]{:S(2)}, u32[]{:S(2)}) collective-permute-start(f32[312,128]{1,0:T(8,128)S(1)} %get-tuple-element.46), channel_id=1, source_target_pairs={{0,1},{1,0},{2,3},{3,2},{4,5},{5,4},{6,7},{7,6},{8,9},{9,8},{10,11... | collective-permute-start | bytes 479240 | tf_op jit(solution)/shard_map/ppermute | solution.py:649
  3.4 4.6 %collective-permute-start.1 = (f32[312,128]{1,0:T(8,128)S(1)}, f32[312,128]{1,0:T(8,128)S(1)}, u32[]{:S(2)}, u32[]{:S(2)}) collective-permute-start(f32[312,128]{1,0:T(8,128)S(1)} %get-tuple-element.47), channel_id=1, source_target_pairs={{1,2},{2,1},{5,6},{6,5},{9,10},{10,9},{13,14},{14,13},{17,18},{18,... | collective-permute-start | bytes 479240 | tf_op jit(solution)/shard_map/ppermute | solution.py:649
  8.0 0.0 collective-permute-done.xa
  8.0 3.4 %collective-permute-done.1.xb = f32[312,128]{1,0:T(8,128)S(1)} collective-permute-done((f32[312,128]{1,0:T(8,128)S(1)}, f32[312,128]{1,0:T(8,128)S(1)}, u32[]{:S(2)}, u32[]{:S(2)}) %collective-permute-start.1) | collective-permute-done | bytes 159776 | tf_op jit(solution)/shard_map/ppermute | solution.py:649
  11.5 0.4 shard_map.69
  11.9 1.4 %collective-permute-start.2 = (f32[759,128]{1,0:T(8,128)S(1)}, f32[759,128]{1,0:T(8,128)S(1)}, u32[]{:S(2)}, u32[]{:S(2)}) collective-permute-start(f32[759,128]{1,0:T(8,128)S(1)} %get-tuple-element.48), channel_id=1, source_target_pairs={{0,4},{4,0},{8,12},{12,8},{16,20},{20,16},{24,28},{28,24},{32,36},... | collective-permute-start | bytes 1165832 | tf_op jit(solution)/shard_map/ppermute | solution.py:649
  13.3 0.7 collective-permute-start.3
  13.9 3.6 %collective-permute-start.4 = (f32[674,128]{1,0:T(8,128)S(1)}, f32[674,128]{1,0:T(8,128)S(1)}, u32[]{:S(2)}, u32[]{:S(2)}) collective-permute-start(f32[674,128]{1,0:T(8,128)S(1)} %get-tuple-element.51), channel_id=1, source_target_pairs={{0,4},{4,0},{8,12},{12,8},{16,20},{20,16},{24,28},{28,24},{32,36},... | collective-permute-start | bytes 1035272 | tf_op jit(solution)/shard_map/ppermute | solution.py:649
  17.6 0.7 collective-permute-start.5
  18.2 2.2 %collective-permute-done.2.za = f32[759,128]{1,0:T(8,128)S(1)} collective-permute-done((f32[759,128]{1,0:T(8,128)S(1)}, f32[759,128]{1,0:T(8,128)S(1)}, u32[]{:S(2)}, u32[]{:S(2)}) %collective-permute-start.2) | collective-permute-done | bytes 388640 | tf_op jit(solution)/shard_map/ppermute | solution.py:649
  20.5 0.0 collective-permute-done.3.zb
  20.5 2.3 %shard_map.70 = (f32[6,4,32,128]{3,2,1,0:T(8,128)S(1)}, f32[6,4,32,128]{3,2,1,0:T(8,128)S(1)}, f32[6,4,48,128]{3,2,1,0:T(8,128)S(1)}, f32[578,128]{1,0:T(8,128)S...) custom-call(f32[12,4,32,128]{3,2,1,0:T(8,128)S(1)} %bitcast.15, f32[4,32,128]{2,1,0:T(8,128)S(1)} %copy-done.1, ...), custom_call_target="tpu_custom_call" | custom-call | flops 16777216 | bytes 8388608 | tf_op jit(solution)/shard_map/pallas_call | solution.py:691
  22.7 4.7 %collective-permute-start.8 = (f32[578,128]{1,0:T(8,128)S(1)}, f32[578,128]{1,0:T(8,128)S(1)}, u32[]{:S(2)}, u32[]{:S(2)}) collective-permute-start(f32[578,128]{1,0:T(8,128)S(1)} %get-tuple-element.62), channel_id=1, source_target_pairs={{0,4},{4,0},{8,12},{12,8},{16,20},{20,16},{24,28},{28,24},{32,36},... | collective-permute-start | bytes 887816 | tf_op jit(solution)/shard_map/ppermute | solution.py:649
  27.4 0.7 collective-permute-start.9
  28.1 0.0 collective-permute-done.4.za
  28.1 0.0 collective-permute-done.5.zb
  28.1 2.1 %shard_map.71 = (f32[6,4,32,128]{3,2,1,0:T(8,128)S(1)}, f32[6,4,32,128]{3,2,1,0:T(8,128)S(1)}, f32[6,4,48,128]{3,2,1,0:T(8,128)S(1)}, f32[578,128]{1,0:T(8,128)S(1)}, f32[578,128]{1,0:T(8,128)S(1)}) custom-call(f32[12,4,32,128]{3,2,1,0:T(8,128)S(1)} %bitcast.16, f32[2,10,48,128]{3,2,1,0:T(8,128)S(1)} %get-tuple-element.50.m, ...), custom_call_target="tpu_custom_call" | custom-call | flops 16777216 | bytes 8388608 | tf_op jit(solution)/shard_map/pallas_call | solution.py:699
  30.3 4.8 %collective-permute-start.6 = (f32[578,128]{1,0:T(8,128)S(1)}, f32[578,128]{1,0:T(8,128)S(1)}, u32[]{:S(2)}, u32[]{:S(2)}) collective-permute-start(f32[578,128]{1,0:T(8,128)S(1)} %get-tuple-element.56), channel_id=1, source_target_pairs={{0,4},{4,0},{8,12},{12,8},{16,20},{20,16},{24,28},{28,24},{32,36},... | collective-permute-start | bytes 887816 | tf_op jit(solution)/shard_map/ppermute | solution.py:649
  35.1 0.7 collective-permute-start.7
  35.8 1.2 %shard_map.72 = (f32[64,128]{1,0:T(8,128)S(1)}, f32[64,128]{1,0:T(8,128)S(1)}) custom-call(f32[12,4,32,128]{3,2,1,0:T(8,128)S(1)} %bitcast.17, f32[6,4,32,128]{3,2,1,0:T(8,128)S(1)} %get-tuple-element.77.b1_0.b1.rest_1_, f32[6,4,32,128]{3,2,1,0:T(8,128)S(1)} %get-tuple-element.78.b2_0.b2.rest_2_, f32[6,4,48,128]{3,2,1,0:T(8,128)S(1)} %get-tuple-element.60.b3w_0.b3w, ...), custom_call_target="tpu_custom_call" | custom-call | flops 16777216 | bytes 8388608 | tf_op jit(solution)/shard_map/pallas_call | solution.py:704
  36.9 0.0 collective-permute-done.8.za
  36.9 0.0 collective-permute-done.9.zb
  36.9 3.0 %shard_map.73 = (f32[6,4,32,128]{3,2,1,0:T(8,128)S(1)}, f32[6,4,32,128]{3,2,1,0:T(8,128)S(1)}, f32[6,4,32,128]{3,2,1,0:T(8,128)S(1)}, f32[64,128]{1,0:T(8,128)S(1)}) custom-call(f32[12,4,32,128]{3,2,1,0:T(8,128)S(1)} %bitcast.18, f32[6,4,32,128]{3,2,1,0:T(8,128)S(1)} %get-tuple-element.77.b1_0.b1.rest_1_, ...), custom_call_target="tpu_custom_call" | custom-call | flops 16777216 | bytes 8388608 | tf_op jit(solution)/shard_map/pallas_call | solution.py:707
  39.9 0.0 collective-permute-done.7.zb
  39.9 3.3 %shard_map.74 = (f32[6,4,32,128]{3,2,1,0:T(8,128)S(1)}, f32[6,4,32,128]{3,2,1,0:T(8,128)S(1)}, f32[6,4,32,128]{3,2,1,0:T(8,128)S(1)}, f32[128,256]{1,0:T(8,128)S(1)}) custom-call(f32[12,4,32,128]{3,2,1,0:T(8,128)S(1)} %bitcast.19, f32[6,4,32,128]{3,2,1,0:T(8,128)S(1)} %get-tuple-element.82.b1_1.b1.rest_6_, ...), custom_call_target="tpu_custom_call" | custom-call | flops 16777216 | bytes 8388608 | tf_op jit(solution)/shard_map/pallas_call | solution.py:710
  43.2 0.1 copy.7
  43.3 25.5 %all_to_all.22 = f32[128,1,256]{2,1,0:T(1,128)S(1)} all-to-all(f32[128,1,256]{2,1,0:T(1,128)S(1)} %copy.7), channel_id=1, replica_groups=mesh['gz'=32,'gx'=4] {'gz','gx'}, dimensions={0} | all-to-all | bytes 262144 | tf_op jit(solution)/shard_map/all_to_all | solution.py:719
  68.8 2.0 %shard_map.75 = (f32[12,4,32,128]{3,2,1,0:T(8,128)}, f32[128,128]{1,0:T(8,128)S(1)}) custom-call(f32[128,256]{1,0:T(8,128)S(1)} %bitcast.21, f32[4,32,128]{2,1,0:T(8,128)S(1)} %copy-done.1, f32[12,4,32,128]{3,2,1,0:T(8,128)S(1)} %bitcast.20, f32[6,4,32,128]{3,2,1,0:T(8,128)S(1)} %get-tuple-element.77.b1_0.b1.rest_1_, ...), custom_call_target="tpu_custom_call" | custom-call | tf_op jit(solution)/shard_map/pallas_call | solution.py:720
  70.8 13.5 %all_to_all.23 = f32[128,1,128]{2,1,0:T(1,128)S(1)} all-to-all(f32[128,1,128]{2,1,0:T(1,128)S(1)} %bitcast.24), channel_id=1, replica_groups=mesh['gz'=32,'gx'=4] {'gz','gx'}, dimensions={0} | all-to-all | bytes 131072 | tf_op jit(solution)/shard_map/all_to_all | solution.py:731
  84.3 1.0 %shard_map.76 = f32[128,512]{1,0:T(8,128)} custom-call(f32[128,128]{1,0:T(8,128)S(1)} %bitcast.22, f32[16,512]{1,0:T(8,128)S(1)} %get-tuple-element.89.power), custom_call_target="tpu_custom_call" | custom-call | tf_op jit(solution)/shard_map/pallas_call | solution.py:732
  (7 shorter events, 0.0 us)
Async XLA Ops:
  0.6 10.8 %copy-start = (f32[2,3,2,4,32,128]{5,4,3,2,1,0:T(8,128)S(1)}, f32[2,3,2,4,32,128]{5,4,3,2,1,0:T(8,128)}, u32[]{:S(2)}) copy-start(f32[2,3,2,4,32,128]{5,4,3,2,1,0:T(8,128)} %param.5) | copy-start | bytes 2359300
  0.6 10.8 %copy-start.1 = (f32[4,32,128]{2,1,0:T(8,128)S(1)}, f32[4,32,128]{2,1,0:T(8,128)}, u32[]{:S(2)}) copy-start(f32[4,32,128]{2,1,0:T(8,128)} %k.6) | copy-start | bytes 196612
  1.9 9.6 %copy-start.2 = (s32[1,4,32]{2,1,0:T(4,128)S(1)}, s32[1,4,32]{2,1,0:T(4,128)}, u32[]{:S(2)}) copy-start(s32[1,4,32]{2,1,0:T(4,128)} %param.7) | copy-start | bytes 1540
  1.9 6.1 %collective-permute-start = (f32[312,128]{1,0:T(8,128)S(1)}, f32[312,128]{1,0:T(8,128)S(1)}, u32[]{:S(2)}, u32[]{:S(2)}) collective-permute-start(f32[312,128]{1,0:T(8,128)S(1)} %get-tuple-element.46), channel_id=1, source_target_pairs={{0,1},{1,0},{2,3},{3,2},{4,5},{5,4},{6,7},{7,6},{8,9},{9,8},{10,11... | collective-permute-start | bytes 479240 | tf_op jit(solution)/shard_map/ppermute | solution.py:649
  3.4 8.1 %collective-permute-start.1 = (f32[312,128]{1,0:T(8,128)S(1)}, f32[312,128]{1,0:T(8,128)S(1)}, u32[]{:S(2)}, u32[]{:S(2)}) collective-permute-start(f32[312,128]{1,0:T(8,128)S(1)} %get-tuple-element.47), channel_id=1, source_target_pairs={{1,2},{2,1},{5,6},{6,5},{9,10},{10,9},{13,14},{14,13},{17,18},{18,... | collective-permute-start | bytes 479240 | tf_op jit(solution)/shard_map/ppermute | solution.py:649
  11.9 8.6 %collective-permute-start.2 = (f32[759,128]{1,0:T(8,128)S(1)}, f32[759,128]{1,0:T(8,128)S(1)}, u32[]{:S(2)}, u32[]{:S(2)}) collective-permute-start(f32[759,128]{1,0:T(8,128)S(1)} %get-tuple-element.48), channel_id=1, source_target_pairs={{0,4},{4,0},{8,12},{12,8},{16,20},{20,16},{24,28},{28,24},{32,36},... | collective-permute-start | bytes 1165832 | tf_op jit(solution)/shard_map/ppermute | solution.py:649
  13.3 7.2 %collective-permute-start.3 = (f32[759,128]{1,0:T(8,128)S(1)}, f32[759,128]{1,0:T(8,128)S(1)}, u32[]{:S(2)}, u32[]{:S(2)}) collective-permute-start(f32[759,128]{1,0:T(8,128)S(1)} %get-tuple-element.49), channel_id=1, source_target_pairs={{4,8},{8,4},{12,16},{16,12},{20,24},{24,20},{28,32},{32,28},{36,40... | collective-permute-start | bytes 1165832 | tf_op jit(solution)/shard_map/ppermute | solution.py:649
  13.9 14.2 %collective-permute-start.4 = (f32[674,128]{1,0:T(8,128)S(1)}, f32[674,128]{1,0:T(8,128)S(1)}, u32[]{:S(2)}, u32[]{:S(2)}) collective-permute-start(f32[674,128]{1,0:T(8,128)S(1)} %get-tuple-element.51), channel_id=1, source_target_pairs={{0,4},{4,0},{8,12},{12,8},{16,20},{20,16},{24,28},{28,24},{32,36},... | collective-permute-start | bytes 1035272 | tf_op jit(solution)/shard_map/ppermute | solution.py:649
  17.6 10.6 %collective-permute-start.5 = (f32[674,128]{1,0:T(8,128)S(1)}, f32[674,128]{1,0:T(8,128)S(1)}, u32[]{:S(2)}, u32[]{:S(2)}) collective-permute-start(f32[674,128]{1,0:T(8,128)S(1)} %get-tuple-element.52), channel_id=1, source_target_pairs={{4,8},{8,4},{12,16},{16,12},{20,24},{24,20},{28,32},{32,28},{36,40... | collective-permute-start | bytes 1035272 | tf_op jit(solution)/shard_map/ppermute | solution.py:649
  22.7 14.2 %collective-permute-start.8 = (f32[578,128]{1,0:T(8,128)S(1)}, f32[578,128]{1,0:T(8,128)S(1)}, u32[]{:S(2)}, u32[]{:S(2)}) collective-permute-start(f32[578,128]{1,0:T(8,128)S(1)} %get-tuple-element.62), channel_id=1, source_target_pairs={{0,4},{4,0},{8,12},{12,8},{16,20},{20,16},{24,28},{28,24},{32,36},... | collective-permute-start | bytes 887816 | tf_op jit(solution)/shard_map/ppermute | solution.py:649
  27.4 9.5 %collective-permute-start.9 = (f32[578,128]{1,0:T(8,128)S(1)}, f32[578,128]{1,0:T(8,128)S(1)}, u32[]{:S(2)}, u32[]{:S(2)}) collective-permute-start(f32[578,128]{1,0:T(8,128)S(1)} %get-tuple-element.63), channel_id=1, source_target_pairs={{4,8},{8,4},{12,16},{16,12},{20,24},{24,20},{28,32},{32,28},{36,40... | collective-permute-start | bytes 887816 | tf_op jit(solution)/shard_map/ppermute | solution.py:649
  30.3 9.6 %collective-permute-start.6 = (f32[578,128]{1,0:T(8,128)S(1)}, f32[578,128]{1,0:T(8,128)S(1)}, u32[]{:S(2)}, u32[]{:S(2)}) collective-permute-start(f32[578,128]{1,0:T(8,128)S(1)} %get-tuple-element.56), channel_id=1, source_target_pairs={{0,4},{4,0},{8,12},{12,8},{16,20},{20,16},{24,28},{28,24},{32,36},... | collective-permute-start | bytes 887816 | tf_op jit(solution)/shard_map/ppermute | solution.py:649
  35.1 4.8 %collective-permute-start.7 = (f32[578,128]{1,0:T(8,128)S(1)}, f32[578,128]{1,0:T(8,128)S(1)}, u32[]{:S(2)}, u32[]{:S(2)}) collective-permute-start(f32[578,128]{1,0:T(8,128)S(1)} %get-tuple-element.57), channel_id=1, source_target_pairs={{4,8},{8,4},{12,16},{16,12},{20,24},{24,20},{28,32},{32,28},{36,40... | collective-permute-start | bytes 887816 | tf_op jit(solution)/shard_map/ppermute | solution.py:649

commit v7 on v6

--- a/solution.py
+++ b/solution.py
@@ -5,7 +5,7 @@
 from jax.experimental.pallas import tpu as pltpu
 from jax.sharding import PartitionSpec as P
 
-SHIFTS = (1.8, 0.6, 1.8, 0.6, 1.8, 0.6)
+SHIFTS = (0.3, 1.9, 0.3, 1.9, 0.3, 1.9)
 SCALE = 1.0
 ITERS = 3
 REACH = 3

time: 85.5 us -> 85.5 us (level)
  no operation moved by 1% of the time
where the time goes in v7:
time: 85.5 us; the launch traced here: 85.2 us
  blocking collectives  39 us (46%)
  starting transfers between devices  23.3 us (27%)
  Pallas kernels  16.3 us (19%)
  waiting for transfers between devices  5.68 us (7%)
    all_to_all x2, blocking collectives, per_device(): got = lax.all_to_all(send, ('gz', 'gx'), 0, 0, tiled=True)  39 us
    ppermute x10, starting transfers between devices, exchange(): return (lax.ppermute(to_a, axis, first), lax.ppermute(to_b, axis, second))  23.3 us
    ppermute x10, waiting for transfers between devices, exchange(): return (lax.ppermute(to_a, axis, first), lax.ppermute(to_b, axis, second))  5.68 us
    pallas_call x1, Pallas kernels, per_device(): call(second_half_1, [VM] * 10, seconds + [((128, 2 * NY), VM)], [pltpu.VM...  3.26 us
    pallas_call x1, Pallas kernels, per_device(): call(second_half_0, [VM] * 8, seconds + [table], spaces, **cost)  2.95 us
    pallas_call x1, Pallas kernels, per_device(): call(first_half_0, [VM] * 6, firsts + [((2, EZ, WX, NY), VM)], [pltpu.VME...  2.27 us
    pallas_call x1, Pallas kernels, per_device(): call(first_half_1, [VM] * 6, firsts, [space] * 5 + [far], **cost)  2.14 us
    pallas_call x1, Pallas kernels, per_device(): call(finish, [VM] * 13, [(whole, HBM), ((128, NY), VM)], [pltpu.VMEM(whol...  1.97 us
  transfers between devices with their start and end apart: 10, of which 2 were waited for; matrix products, arithmetic and copies ran while one was open for 0% of the time, Pallas kernels for 10%

profile of v7, /device:TPU:1, one launch (start us, length us, event | category | flops | bytes accessed | tf_op | source)
XLA Modules:
  0.0 85.2 jit_solution(639212867542862681)
XLA Ops:
  0.7 1.2 %shard_map.68 = (f32[312,128]{1,0:T(8,128)S(1)}, f32[312,128]{1,0:T(8,128)S(1)}, f32[16,512]{1,0:T(8,128)S(1)}) custom-call(f32[12,4,32,128]{3,2,1,0:T(8,128)} %bitcast.13, f32[4,32,128]{2,1,0:T(8,128)} %k.6, f32[4,512]{1,0:T(4,128)} %bitcast.26, s32[1,512]{1,0:T(1,128)} %bitcast.27), custom_call_target="tpu_custom_call" | custom-call | tf_op jit(solution)/shard_map/pallas_call | solution.py:668
  1.9 0.0 copy-start.2
  1.9 1.5 %collective-permute-start = (f32[312,128]{1,0:T(8,128)S(1)}, f32[312,128]{1,0:T(8,128)S(1)}, u32[]{:S(2)}, u32[]{:S(2)}) collective-permute-start(f32[312,128]{1,0:T(8,128)S(1)} %get-tuple-element.46), channel_id=1, source_target_pairs={{0,1},{1,0},{2,3},{3,2},{4,5},{5,4},{6,7},{7,6},{8,9},{9,8},{10,11... | collective-permute-start | bytes 479240 | tf_op jit(solution)/shard_map/ppermute | solution.py:649
  3.4 4.6 %collective-permute-start.1 = (f32[312,128]{1,0:T(8,128)S(1)}, f32[312,128]{1,0:T(8,128)S(1)}, u32[]{:S(2)}, u32[]{:S(2)}) collective-permute-start(f32[312,128]{1,0:T(8,128)S(1)} %get-tuple-element.47), channel_id=1, source_target_pairs={{1,2},{2,1},{5,6},{6,5},{9,10},{10,9},{13,14},{14,13},{17,18},{18,... | collective-permute-start | bytes 479240 | tf_op jit(solution)/shard_map/ppermute | solution.py:649
  8.0 0.0 collective-permute-done.xa
  8.0 3.4 %collective-permute-done.1.xb = f32[312,128]{1,0:T(8,128)S(1)} collective-permute-done((f32[312,128]{1,0:T(8,128)S(1)}, f32[312,128]{1,0:T(8,128)S(1)}, u32[]{:S(2)}, u32[]{:S(2)}) %collective-permute-start.1) | collective-permute-done | bytes 159776 | tf_op jit(solution)/shard_map/ppermute | solution.py:649
  11.5 0.4 shard_map.69
  11.9 1.4 %collective-permute-start.2 = (f32[759,128]{1,0:T(8,128)S(1)}, f32[759,128]{1,0:T(8,128)S(1)}, u32[]{:S(2)}, u32[]{:S(2)}) collective-permute-start(f32[759,128]{1,0:T(8,128)S(1)} %get-tuple-element.48), channel_id=1, source_target_pairs={{0,4},{4,0},{8,12},{12,8},{16,20},{20,16},{24,28},{28,24},{32,36},... | collective-permute-start | bytes 1165832 | tf_op jit(solution)/shard_map/ppermute | solution.py:649
  13.3 0.7 collective-permute-start.3
  13.9 3.6 %collective-permute-start.4 = (f32[674,128]{1,0:T(8,128)S(1)}, f32[674,128]{1,0:T(8,128)S(1)}, u32[]{:S(2)}, u32[]{:S(2)}) collective-permute-start(f32[674,128]{1,0:T(8,128)S(1)} %get-tuple-element.51), channel_id=1, source_target_pairs={{0,4},{4,0},{8,12},{12,8},{16,20},{20,16},{24,28},{28,24},{32,36},... | collective-permute-start | bytes 1035272 | tf_op jit(solution)/shard_map/ppermute | solution.py:649
  17.6 0.7 collective-permute-start.5
  18.2 2.2 %collective-permute-done.2.za = f32[759,128]{1,0:T(8,128)S(1)} collective-permute-done((f32[759,128]{1,0:T(8,128)S(1)}, f32[759,128]{1,0:T(8,128)S(1)}, u32[]{:S(2)}, u32[]{:S(2)}) %collective-permute-start.2) | collective-permute-done | bytes 388640 | tf_op jit(solution)/shard_map/ppermute | solution.py:649
  20.5 0.0 collective-permute-done.3.zb
  20.5 2.3 %shard_map.70 = (f32[6,4,32,128]{3,2,1,0:T(8,128)S(1)}, f32[6,4,32,128]{3,2,1,0:T(8,128)S(1)}, f32[6,4,48,128]{3,2,1,0:T(8,128)S(1)}, f32[578,128]{1,0:T(8,128)S...) custom-call(f32[12,4,32,128]{3,2,1,0:T(8,128)S(1)} %bitcast.15, f32[4,32,128]{2,1,0:T(8,128)S(1)} %copy-done.1, ...), custom_call_target="tpu_custom_call" | custom-call | flops 16777216 | bytes 8388608 | tf_op jit(solution)/shard_map/pallas_call | solution.py:691
  22.7 4.7 %collective-permute-start.8 = (f32[578,128]{1,0:T(8,128)S(1)}, f32[578,128]{1,0:T(8,128)S(1)}, u32[]{:S(2)}, u32[]{:S(2)}) collective-permute-start(f32[578,128]{1,0:T(8,128)S(1)} %get-tuple-element.62), channel_id=1, source_target_pairs={{0,4},{4,0},{8,12},{12,8},{16,20},{20,16},{24,28},{28,24},{32,36},... | collective-permute-start | bytes 887816 | tf_op jit(solution)/shard_map/ppermute | solution.py:649
  27.4 0.7 collective-permute-start.9
  28.1 0.0 collective-permute-done.4.za
  28.1 0.0 collective-permute-done.5.zb
  28.1 2.1 %shard_map.71 = (f32[6,4,32,128]{3,2,1,0:T(8,128)S(1)}, f32[6,4,32,128]{3,2,1,0:T(8,128)S(1)}, f32[6,4,48,128]{3,2,1,0:T(8,128)S(1)}, f32[578,128]{1,0:T(8,128)S(1)}, f32[578,128]{1,0:T(8,128)S(1)}) custom-call(f32[12,4,32,128]{3,2,1,0:T(8,128)S(1)} %bitcast.16, f32[2,10,48,128]{3,2,1,0:T(8,128)S(1)} %get-tuple-element.50.m, ...), custom_call_target="tpu_custom_call" | custom-call | flops 16777216 | bytes 8388608 | tf_op jit(solution)/shard_map/pallas_call | solution.py:699
  30.3 4.8 %collective-permute-start.6 = (f32[578,128]{1,0:T(8,128)S(1)}, f32[578,128]{1,0:T(8,128)S(1)}, u32[]{:S(2)}, u32[]{:S(2)}) collective-permute-start(f32[578,128]{1,0:T(8,128)S(1)} %get-tuple-element.56), channel_id=1, source_target_pairs={{0,4},{4,0},{8,12},{12,8},{16,20},{20,16},{24,28},{28,24},{32,36},... | collective-permute-start | bytes 887816 | tf_op jit(solution)/shard_map/ppermute | solution.py:649
  35.1 0.7 collective-permute-start.7
  35.8 1.2 %shard_map.72 = (f32[64,128]{1,0:T(8,128)S(1)}, f32[64,128]{1,0:T(8,128)S(1)}) custom-call(f32[12,4,32,128]{3,2,1,0:T(8,128)S(1)} %bitcast.17, f32[6,4,32,128]{3,2,1,0:T(8,128)S(1)} %get-tuple-element.77.b1_0.b1.rest_1_, f32[6,4,32,128]{3,2,1,0:T(8,128)S(1)} %get-tuple-element.78.b2_0.b2.rest_2_, f32[6,4,48,128]{3,2,1,0:T(8,128)S(1)} %get-tuple-element.60.b3w_0.b3w, ...), custom_call_target="tpu_custom_call" | custom-call | flops 16777216 | bytes 8388608 | tf_op jit(solution)/shard_map/pallas_call | solution.py:704
  36.9 0.0 collective-permute-done.8.za
  36.9 0.0 collective-permute-done.9.zb
  36.9 3.0 %shard_map.73 = (f32[6,4,32,128]{3,2,1,0:T(8,128)S(1)}, f32[6,4,32,128]{3,2,1,0:T(8,128)S(1)}, f32[6,4,32,128]{3,2,1,0:T(8,128)S(1)}, f32[64,128]{1,0:T(8,128)S(1)}) custom-call(f32[12,4,32,128]{3,2,1,0:T(8,128)S(1)} %bitcast.18, f32[6,4,32,128]{3,2,1,0:T(8,128)S(1)} %get-tuple-element.77.b1_0.b1.rest_1_, ...), custom_call_target="tpu_custom_call" | custom-call | flops 16777216 | bytes 8388608 | tf_op jit(solution)/shard_map/pallas_call | solution.py:707
  39.9 0.0 collective-permute-done.7.zb
  39.9 3.3 %shard_map.74 = (f32[6,4,32,128]{3,2,1,0:T(8,128)S(1)}, f32[6,4,32,128]{3,2,1,0:T(8,128)S(1)}, f32[6,4,32,128]{3,2,1,0:T(8,128)S(1)}, f32[128,256]{1,0:T(8,128)S(1)}) custom-call(f32[12,4,32,128]{3,2,1,0:T(8,128)S(1)} %bitcast.19, f32[6,4,32,128]{3,2,1,0:T(8,128)S(1)} %get-tuple-element.82.b1_1.b1.rest_6_, ...), custom_call_target="tpu_custom_call" | custom-call | flops 16777216 | bytes 8388608 | tf_op jit(solution)/shard_map/pallas_call | solution.py:710
  43.2 0.1 copy.7
  43.3 25.5 %all_to_all.22 = f32[128,1,256]{2,1,0:T(1,128)S(1)} all-to-all(f32[128,1,256]{2,1,0:T(1,128)S(1)} %copy.7), channel_id=1, replica_groups=mesh['gz'=32,'gx'=4] {'gz','gx'}, dimensions={0} | all-to-all | bytes 262144 | tf_op jit(solution)/shard_map/all_to_all | solution.py:719
  68.8 2.0 %shard_map.75 = (f32[12,4,32,128]{3,2,1,0:T(8,128)}, f32[128,128]{1,0:T(8,128)S(1)}) custom-call(f32[128,256]{1,0:T(8,128)S(1)} %bitcast.21, f32[4,32,128]{2,1,0:T(8,128)S(1)} %copy-done.1, f32[12,4,32,128]{3,2,1,0:T(8,128)S(1)} %bitcast.20, f32[6,4,32,128]{3,2,1,0:T(8,128)S(1)} %get-tuple-element.77.b1_0.b1.rest_1_, ...), custom_call_target="tpu_custom_call" | custom-call | tf_op jit(solution)/shard_map/pallas_call | solution.py:720
  70.8 13.5 %all_to_all.23 = f32[128,1,128]{2,1,0:T(1,128)S(1)} all-to-all(f32[128,1,128]{2,1,0:T(1,128)S(1)} %bitcast.24), channel_id=1, replica_groups=mesh['gz'=32,'gx'=4] {'gz','gx'}, dimensions={0} | all-to-all | bytes 131072 | tf_op jit(solution)/shard_map/all_to_all | solution.py:731
  84.3 1.0 %shard_map.76 = f32[128,512]{1,0:T(8,128)} custom-call(f32[128,128]{1,0:T(8,128)S(1)} %bitcast.22, f32[16,512]{1,0:T(8,128)S(1)} %get-tuple-element.89.power), custom_call_target="tpu_custom_call" | custom-call | tf_op jit(solution)/shard_map/pallas_call | solution.py:732
  (7 shorter events, 0.0 us)
Async XLA Ops:
  0.6 10.8 %copy-start = (f32[2,3,2,4,32,128]{5,4,3,2,1,0:T(8,128)S(1)}, f32[2,3,2,4,32,128]{5,4,3,2,1,0:T(8,128)}, u32[]{:S(2)}) copy-start(f32[2,3,2,4,32,128]{5,4,3,2,1,0:T(8,128)} %param.5) | copy-start | bytes 2359300
  0.6 10.8 %copy-start.1 = (f32[4,32,128]{2,1,0:T(8,128)S(1)}, f32[4,32,128]{2,1,0:T(8,128)}, u32[]{:S(2)}) copy-start(f32[4,32,128]{2,1,0:T(8,128)} %k.6) | copy-start | bytes 196612
  1.9 9.6 %copy-start.2 = (s32[1,4,32]{2,1,0:T(4,128)S(1)}, s32[1,4,32]{2,1,0:T(4,128)}, u32[]{:S(2)}) copy-start(s32[1,4,32]{2,1,0:T(4,128)} %param.7) | copy-start | bytes 1540
  1.9 6.1 %collective-permute-start = (f32[312,128]{1,0:T(8,128)S(1)}, f32[312,128]{1,0:T(8,128)S(1)}, u32[]{:S(2)}, u32[]{:S(2)}) collective-permute-start(f32[312,128]{1,0:T(8,128)S(1)} %get-tuple-element.46), channel_id=1, source_target_pairs={{0,1},{1,0},{2,3},{3,2},{4,5},{5,4},{6,7},{7,6},{8,9},{9,8},{10,11... | collective-permute-start | bytes 479240 | tf_op jit(solution)/shard_map/ppermute | solution.py:649
  3.4 8.1 %collective-permute-start.1 = (f32[312,128]{1,0:T(8,128)S(1)}, f32[312,128]{1,0:T(8,128)S(1)}, u32[]{:S(2)}, u32[]{:S(2)}) collective-permute-start(f32[312,128]{1,0:T(8,128)S(1)} %get-tuple-element.47), channel_id=1, source_target_pairs={{1,2},{2,1},{5,6},{6,5},{9,10},{10,9},{13,14},{14,13},{17,18},{18,... | collective-permute-start | bytes 479240 | tf_op jit(solution)/shard_map/ppermute | solution.py:649
  11.9 8.6 %collective-permute-start.2 = (f32[759,128]{1,0:T(8,128)S(1)}, f32[759,128]{1,0:T(8,128)S(1)}, u32[]{:S(2)}, u32[]{:S(2)}) collective-permute-start(f32[759,128]{1,0:T(8,128)S(1)} %get-tuple-element.48), channel_id=1, source_target_pairs={{0,4},{4,0},{8,12},{12,8},{16,20},{20,16},{24,28},{28,24},{32,36},... | collective-permute-start | bytes 1165832 | tf_op jit(solution)/shard_map/ppermute | solution.py:649
  13.3 7.2 %collective-permute-start.3 = (f32[759,128]{1,0:T(8,128)S(1)}, f32[759,128]{1,0:T(8,128)S(1)}, u32[]{:S(2)}, u32[]{:S(2)}) collective-permute-start(f32[759,128]{1,0:T(8,128)S(1)} %get-tuple-element.49), channel_id=1, source_target_pairs={{4,8},{8,4},{12,16},{16,12},{20,24},{24,20},{28,32},{32,28},{36,40... | collective-permute-start | bytes 1165832 | tf_op jit(solution)/shard_map/ppermute | solution.py:649
  13.9 14.2 %collective-permute-start.4 = (f32[674,128]{1,0:T(8,128)S(1)}, f32[674,128]{1,0:T(8,128)S(1)}, u32[]{:S(2)}, u32[]{:S(2)}) collective-permute-start(f32[674,128]{1,0:T(8,128)S(1)} %get-tuple-element.51), channel_id=1, source_target_pairs={{0,4},{4,0},{8,12},{12,8},{16,20},{20,16},{24,28},{28,24},{32,36},... | collective-permute-start | bytes 1035272 | tf_op jit(solution)/shard_map/ppermute | solution.py:649
  17.6 10.6 %collective-permute-start.5 = (f32[674,128]{1,0:T(8,128)S(1)}, f32[674,128]{1,0:T(8,128)S(1)}, u32[]{:S(2)}, u32[]{:S(2)}) collective-permute-start(f32[674,128]{1,0:T(8,128)S(1)} %get-tuple-element.52), channel_id=1, source_target_pairs={{4,8},{8,4},{12,16},{16,12},{20,24},{24,20},{28,32},{32,28},{36,40... | collective-permute-start | bytes 1035272 | tf_op jit(solution)/shard_map/ppermute | solution.py:649
  22.7 14.2 %collective-permute-start.8 = (f32[578,128]{1,0:T(8,128)S(1)}, f32[578,128]{1,0:T(8,128)S(1)}, u32[]{:S(2)}, u32[]{:S(2)}) collective-permute-start(f32[578,128]{1,0:T(8,128)S(1)} %get-tuple-element.62), channel_id=1, source_target_pairs={{0,4},{4,0},{8,12},{12,8},{16,20},{20,16},{24,28},{28,24},{32,36},... | collective-permute-start | bytes 887816 | tf_op jit(solution)/shard_map/ppermute | solution.py:649
  27.4 9.5 %collective-permute-start.9 = (f32[578,128]{1,0:T(8,128)S(1)}, f32[578,128]{1,0:T(8,128)S(1)}, u32[]{:S(2)}, u32[]{:S(2)}) collective-permute-start(f32[578,128]{1,0:T(8,128)S(1)} %get-tuple-element.63), channel_id=1, source_target_pairs={{4,8},{8,4},{12,16},{16,12},{20,24},{24,20},{28,32},{32,28},{36,40... | collective-permute-start | bytes 887816 | tf_op jit(solution)/shard_map/ppermute | solution.py:649
  30.3 9.6 %collective-permute-start.6 = (f32[578,128]{1,0:T(8,128)S(1)}, f32[578,128]{1,0:T(8,128)S(1)}, u32[]{:S(2)}, u32[]{:S(2)}) collective-permute-start(f32[578,128]{1,0:T(8,128)S(1)} %get-tuple-element.56), channel_id=1, source_target_pairs={{0,4},{4,0},{8,12},{12,8},{16,20},{20,16},{24,28},{28,24},{32,36},... | collective-permute-start | bytes 887816 | tf_op jit(solution)/shard_map/ppermute | solution.py:649
  35.1 4.8 %collective-permute-start.7 = (f32[578,128]{1,0:T(8,128)S(1)}, f32[578,128]{1,0:T(8,128)S(1)}, u32[]{:S(2)}, u32[]{:S(2)}) collective-permute-start(f32[578,128]{1,0:T(8,128)S(1)} %get-tuple-element.57), channel_id=1, source_target_pairs={{4,8},{8,4},{12,16},{16,12},{20,24},{24,20},{28,32},{32,28},{36,40... | collective-permute-start | bytes 887816 | tf_op jit(solution)/shard_map/ppermute | solution.py:649
